TPU v7x, 128 devices: a whole 4x4x4 slice. The times are simulated.
128 devices in a mesh: sp: 16 (over z, y), hd: 8 (over x, core).
Axes of the slice: x: 4, y: 4, z: 4, core: 2. Of those that a mesh axis runs over, the one named last changes fastest.
Arguments:
- latent: bfloat16 [8, 64, 64, 320], P(None, 'sp', 'hd'), may hold values from -6 to 6
- condition: bfloat16 [8, 64, 64, 192], P(None, 'sp', 'hd'), may hold values from -6 to 6
- text_states: bfloat16 [8, 77, 768], replicated, may hold values from -6 to 6
- valid_rows: int32 [8], replicated, may hold values from 16 to 64, as said below
- text_lengths: int32 [8], replicated, may hold values from 8 to 77, as said below
- w_in: bfloat16 [192, 320], replicated, may hold values from -0.4375 to 0.4375
- b_in: float32 [320], replicated, may hold values from -3 to 3
- w_conv: bfloat16 [3, 3, 320, 320], replicated, may hold values from -0.109375 to 0.109375
- b_conv: float32 [320], replicated, may hold values from -3 to 3
- w_out: bfloat16 [320, 320], replicated, may hold values from -0.3125 to 0.3125
- b_out: float32 [320], replicated, may hold values from -3 to 3
- w_query: bfloat16 [320, 320], replicated, may hold values from -0.3125 to 0.3125
- w_key: bfloat16 [320, 320], replicated, may hold values from -0.3125 to 0.3125
- w_value: bfloat16 [320, 320], replicated, may hold values from -0.3125 to 0.3125
- w_attn_out: bfloat16 [320, 320], replicated, may hold values from -6 to 6
- b_attn_out: float32 [320], replicated, may hold values from -3 to 3
- w_cross_query: bfloat16 [320, 320], replicated, may hold values from -0.3125 to 0.3125
- w_cross_key: bfloat16 [768, 320], replicated, may hold values from -0.21875 to 0.21875
- w_cross_value: bfloat16 [768, 320], replicated, may hold values from -0.21875 to 0.21875
- w_cross_out: bfloat16 [320, 320], replicated, may hold values from -2 to 2
- b_cross_out: float32 [320], replicated, may hold values from -3 to 3
- w_ff_in: bfloat16 [320, 2560], replicated, may hold values from -0.3125 to 0.3125
- b_ff_in: float32 [2560], replicated, may hold values from -3 to 3
- w_ff_out: bfloat16 [1280, 320], replicated, may hold values from -0.15625 to 0.15625
- b_ff_out: float32 [320], replicated, may hold values from -3 to 3
- cotangent: bfloat16 [8, 64, 64, 320], P(None, 'sp', 'hd'), may hold values from -6 to 6
Outputs:
- mixed_out: bfloat16 [8, 64, 64, 320], P(None, 'sp', 'hd')
- latent_grad: float32 [8, 64, 64, 320], P(None, 'sp', 'hd')
- grad_w_in: float32 [192, 320], replicated
- grad_b_in: float32 [320], replicated
- grad_w_conv: float32 [3, 3, 320, 320], replicated
- grad_b_conv: float32 [320], replicated
- grad_w_out: float32 [320, 320], replicated
- grad_b_out: float32 [320], replicated
Inputs may be any that keep to these rules, and one draw needn't show every extreme that they name: `valid_rows`: some item has all 64 rows valid. The first text_lengths[item] tokens are valid; some item has all 77.
All inputs are finite; a program needn't handle non-finite values.
Results may differ from a plain program's by a relative error of at most 0.012.
Values may be sent and summed in bfloat16 or wider, within the bound.
No kernel may reach another device: no remote copies, remote signals or barrier semaphores. Data moves between devices by JAX's collectives and lax.ppermute only.
A program may use at most 128 MiB of HBM per device.

v0:
```python
import jax
import jax.numpy as jnp
from jax import lax
from jax.experimental import pallas as pl
from jax.experimental.pallas import tpu as pltpu
from jax.sharding import Mesh
from jax.sharding import PartitionSpec as P

ITEMS, ROWS, COLS, C, CIN, HEADS, HEAD, FF = 8, 4, 8, 320, 192, 8, 40, 1280
CELLS = ITEMS * ROWS * COLS
PART = ROWS * COLS
CHIPS = 64
HALF = CHIPS * PART
TEXT = 80
LANES = 128
WIDE = 256
SCALE = HEAD**-0.5
LOG2E = 1.4426950408889634
EPS = 1e-5
MASKED = -1e30
KEY, VALUE, MASK = HEAD, 2 * HEAD, 3 * HEAD
ACROSS = ("sp", "x")
SUM_ROWS = 3072

bf16, f32 = jnp.bfloat16, jnp.float32
NT = (((1,), (1,)), ((), ()))


def dot(left, right):
    return jnp.dot(left, right, preferred_element_type=f32)


def dot_nt(left, right):
    return lax.dot_general(left, right, NT, preferred_element_type=f32)


def lane_of(shape):
    return lax.broadcasted_iota(jnp.int32, shape, len(shape) - 1)


def moments(values):
    center = values - jnp.mean(values, -1, keepdims=True)
    rate = lax.rsqrt(jnp.mean(center * center, -1, keepdims=True) + EPS)
    return center * rate, rate


def norm_back(unit, rate, grads):
    return rate * (
        grads
        - jnp.mean(grads, -1, keepdims=True)
        - unit * jnp.mean(grads * unit, -1, keepdims=True)
    )


class Fetched:
    def __init__(self, source, buffer, semaphore):
        self.copy = pltpu.make_async_copy(source, buffer, semaphore)
        self.buffer, self.shape, self.here = buffer, buffer.shape, False
        self.copy.start()

    def __getitem__(self, index):
        if not self.here:
            self.copy.wait()
            self.here = True
        return self.buffer[index]


class Stored:
    def __init__(self, target, buffer, semaphore):
        self.copy = pltpu.make_async_copy(buffer, target, semaphore)
        self.buffer, self.started = buffer, False

    def __setitem__(self, index, values):
        self.buffer[index] = values
        if index is Ellipsis:
            self.start()

    def start(self):
        if not self.started:
            self.copy.start()
            self.started = True


def call(kernel, outs, ins, name, scalars=0, scratch=(), vmem=16, fetch=(), store=(), far=(),
    near=(), held=(),
):
    fetch, store = list(fetch), list(store)
    far_in = [i for i in far if i < len(ins)]
    far_out = [i - len(ins) for i in far if i >= len(ins)]

    def body(*refs):
        refs = list(refs)
        given, refs = refs[: len(ins)], refs[len(ins) :]
        made, refs = refs[: len(outs)], refs[len(outs) :]
        own, refs = refs[: len(scratch)], refs[len(scratch) :]
        buffers, semaphores = refs[:-1], refs[-1] if refs else None
        for n, i in enumerate(fetch):
            given[i] = Fetched(given[i], buffers[n], semaphores.at[n])
        kept = []
        for n, i in enumerate(store, len(fetch)):
            made[i] = Stored(made[i], buffers[n], semaphores.at[n])
            kept.append(made[i])
        kernel(*given, *made, *own)
        for part in given:
            if isinstance(part, Fetched) and not part.here:
                part.copy.wait()
        for part in kept:
            part.start()
        for part in kept:
            part.copy.wait()

    def made_as(i, made):
        if i in store or i in far_out:
            return pltpu.HBM(made.shape, made.dtype)
        return pltpu.VMEM(made.shape, made.dtype) if i in near else made

    def in_spec(i):
        if i < scalars:
            return pl.BlockSpec(memory_space=pltpu.SMEM)
        space = pltpu.HBM if i in fetch or i in far_in else pltpu.VMEM
        return pl.BlockSpec(memory_space=space)

    def out_spec(i):
        space = pltpu.HBM if i in store or i in far_out else pltpu.VMEM
        return pl.BlockSpec(memory_space=space)

    extra = [pltpu.VMEM(ins[i].shape, ins[i].dtype) for i in fetch]
    extra += [pltpu.VMEM(outs[i].shape, outs[i].dtype) for i in store]
    if extra:
        extra.append(pltpu.SemaphoreType.DMA((len(extra),)))
    return pl.pallas_call(
        body,
        out_shape=tuple(made_as(i, made) for i, made in enumerate(outs)),
        in_specs=[in_spec(i) for i in range(len(ins))],
        out_specs=tuple(out_spec(i) for i in range(len(outs))),
        scratch_shapes=list(scratch) + extra,
        compiler_params=pltpu.CompilerParams(vmem_limit_bytes=vmem << 20),
        name=name,
    )(
        *(
            pltpu.with_memory_space_constraint(x, pltpu.HBM)
            if i in fetch or i in far_in
            else (pltpu.with_memory_space_constraint(x, pltpu.VMEM) if i in held else x)
            for i, x in enumerate(ins)
        )
    )


def bring(arrays, name, kernel=None, made=(), near=()):
    count, given = len(arrays), len(near)

    def body(*refs):
        sources, inputs = refs[:count], refs[count : count + given]
        targets = refs[count + given : -1]
        copies = [
            pltpu.make_async_copy(sources[n], targets[n], refs[-1].at[n]) for n in range(count)
        ]
        for copy in copies:
            copy.start()
        if kernel is not None:
            kernel(*inputs, *targets[count:])
        for copy in copies:
            copy.wait()

    shapes = [jax.ShapeDtypeStruct(x.shape, x.dtype) for x in arrays] + list(made)
    return pl.pallas_call(
        body,
        out_shape=tuple(pltpu.VMEM(x.shape, x.dtype) for x in shapes),
        in_specs=[pl.BlockSpec(memory_space=pltpu.HBM)] * count
        + [pl.BlockSpec(memory_space=pltpu.VMEM)] * given,
        out_specs=(pl.BlockSpec(memory_space=pltpu.VMEM),) * len(shapes),
        scratch_shapes=[pltpu.SemaphoreType.DMA((max(count, 1),))],
        compiler_params=pltpu.CompilerParams(vmem_limit_bytes=8 << 20),
        name=name,
    )(*(pltpu.with_memory_space_constraint(x, pltpu.HBM) for x in arrays), *near)


def after(value, *arrays):
    return lax.optimization_barrier((value,) + arrays)


def out(*shape, dtype=bf16):
    return jax.ShapeDtypeStruct(shape, dtype)


def bias_rows(bias):
    row = lax.broadcasted_iota(jnp.int32, (WIDE - CIN, C), 0)
    rest = jnp.broadcast_to(bias, (WIDE - CIN, C))
    rows = jnp.zeros((WIDE - CIN, C), f32)
    for n in range(3):
        piece = rest.astype(bf16).astype(f32)
        rows = jnp.where(row == n, piece, rows)
        rest = rest - piece
    return rows.astype(bf16)


def adapter_kernel(
    place, valid, center, top, bottom, left, right, latent, w_in, b_in, w_conv, b_conv, w_out,
    b_out, w_query, w_key, w_value, rows_out, mixed_out, smooth_out, slope_out, cond_out,
    w_wide,
):
    span = ITEMS * (ROWS + 2)
    w_wide[:CIN, :] = w_in[...]
    w_wide[CIN:, :] = bias_rows(b_in[...])

    def widen(values):
        blank = jnp.zeros(values.shape[:-1] + (WIDE - CIN,), f32)
        return jnp.concatenate([values.astype(f32), blank], axis=-1)

    block = jnp.concatenate([top[...], center[...], bottom[...]], axis=1)
    block = widen(block.reshape(span, COLS, CIN))
    shape = (ITEMS, ROWS + 2, COLS, WIDE)
    row = lax.broadcasted_iota(jnp.int32, shape, 1) + ROWS * place[0] - 1
    inside = (row >= 0) & (row < ROWS * 16)
    inside = jnp.where(inside, 1.0, 0.0).reshape(span, COLS, WIDE)
    lane = lane_of((span, COLS, WIDE))
    col = lax.broadcasted_iota(jnp.int32, (span, COLS, WIDE), 1)
    at = COLS * place[2]
    edges = []
    for n, side in enumerate((left, right)):
        there = (at > 0) if n == 0 else (at < COLS * 7)
        edges.append((widen(side[...]).reshape(span, 1, WIDE), jnp.where(there, inside, 0.0)))
    near = jnp.where(col == 0, edges[0][0], pltpu.roll(block, 1, 1))
    near_inside = jnp.where(col == 0, edges[0][1], inside)
    far = jnp.where(col == COLS - 1, edges[1][0], pltpu.roll(block, COLS - 1, 1))
    far_inside = jnp.where(col == COLS - 1, edges[1][1], inside)
    inner = jnp.zeros((CELLS, C), f32)
    start_here = None
    one = (lane >= CIN) & (lane < CIN + 3)
    moves = ((near, near_inside), (block, inside), (far, far_inside))
    for j, (moved, present) in enumerate(moves):
        moved = jnp.where(one, present, moved)
        start = dot(moved.reshape(span * COLS, WIDE).astype(bf16), w_wide[...])
        start = start.reshape(ITEMS, ROWS + 2, COLS, C)
        moved = moved.reshape(ITEMS, ROWS + 2, COLS, WIDE)
        for i in range(3):
            patch = start[:, i : i + ROWS].reshape(CELLS, C).astype(bf16)
            if i == 1 and j == 1:
                start_here = patch.astype(f32)
            inner += dot(patch, w_conv[3 * i + j])
            cond_out[3 * i + j] = moved[:, i : i + ROWS].reshape(CELLS, WIDE).astype(bf16)
    inner += b_conv[...]
    gate = jax.nn.sigmoid(inner)
    smooth = (inner * gate).astype(bf16)
    smooth_out[...] = smooth
    slope_out[...] = gate * (1.0 + inner * (1.0 - gate))
    mixed = latent[...].astype(f32) + (start_here + dot(smooth, w_out[...]) + b_out[...])
    mixed_out[...] = mixed
    normed = moments(mixed)[0].astype(bf16)
    projected = [dot(normed, w[...]) for w in (w_query, w_key, w_value)]
    lane = lane_of((PART, LANES - MASK))
    row = lax.broadcasted_iota(jnp.int32, (PART, LANES - MASK), 0) // COLS + ROWS * place[0]
    extras = []
    for item in range(ITEMS):
        hidden = jnp.where(row >= valid[item], MASKED, 0.0)
        extras.append(jnp.where(lane == 0, hidden, 1.0))
    extras = jnp.concatenate(extras, axis=0)
    for head in range(HEADS):
        at = slice(head * HEAD, (head + 1) * HEAD)
        joined = jnp.concatenate([part[:, at] for part in projected] + [extras], axis=1)
        rows_out[:, head] = joined.astype(bf16).reshape(ITEMS, PART, LANES)


def text_kernel(text, w_key_turned, w_value_turned, keys_out, values_out):
    count = text.shape[0]
    token = lax.broadcasted_iota(jnp.int32, (TEXT, count), 0)
    place = lane_of((TEXT, count))
    text[:1], w_key_turned[:1], w_value_turned[:1]

    def body(item, carry):
        pick = jnp.where(place == token * ITEMS + item, 1.0, 0.0).astype(bf16)
        states = dot(pick, text[...]).astype(bf16)
        keys_out[item] = dot_nt(states, w_key_turned[...]).astype(bf16)
        values_out[item] = dot_nt(states, w_value_turned[...]).astype(bf16)
        return carry

    lax.fori_loop(0, ITEMS, body, 0)


BLOCK = 256
STEP = 512


def attend_kernel(
    own, other, packed_out, full_out, probs_out,
    scores_a, scores_b, probs_a, probs_b, turned_a, turned_b, keys_turned, query, output, sems,
):
    count = HALF // BLOCK
    keys_turned[:, :HALF] = jnp.transpose(own[...])
    keys_turned[:, HALF:] = jnp.transpose(other[...])
    lane = lane_of((HALF, LANES))
    rows = pltpu.roll(own[...].astype(f32), KEY, 1)
    rows = jnp.where((lane >= KEY) & (lane < VALUE), rows, jnp.where(lane == MASK, 1.0, 0.0))
    query[...] = jnp.transpose(rows.astype(bf16))
    chunks = [(ref, at) for ref in (own, other) for at in range(0, HALF, STEP)]

    def columns(b):
        return pl.ds(pl.multiple_of(b * BLOCK, BLOCK), BLOCK)

    def score(queries, n, scores, peak):
        ref, at = chunks[n]
        part = dot(ref[at : at + STEP, :], queries)
        scores[n * STEP : (n + 1) * STEP, :] = part
        part = jnp.max(part.reshape(STEP // 8, 8, BLOCK), axis=0)
        return part if peak is None else jnp.maximum(peak, part)

    def sent(b, turned, n):
        return pltpu.make_async_copy(turned, probs_out.at[columns(b)], sems.at[n])

    def half(b, peak, following, scores, probs, turned):
        shift = jnp.max(peak, axis=0, keepdims=True) * (SCALE * LOG2E)
        queries = query[:, columns(jnp.minimum(b + 1, count - 1))]
        ahead = None
        for n in range(len(chunks)):
            ahead = score(queries, n, following, ahead)
            keys = slice(n * STEP, (n + 1) * STEP)
            part = jnp.exp2(scores[keys, :] * (SCALE * LOG2E) - shift).astype(bf16)
            probs[keys, :] = part
            turned[:, keys] = jnp.transpose(part)
        output[:, columns(b)] = dot(keys_turned[...], probs[...])
        return ahead

    peak = None
    for n in range(len(chunks)):
        peak = score(query[:, :BLOCK], n, scores_a, peak)

    def body(i, peak):
        @pl.when(i > 0)
        def _():
            sent(2 * i - 2, turned_a, 0).wait()

        peak = half(2 * i, peak, scores_b, scores_a, probs_a, turned_a)
        sent(2 * i, turned_a, 0).start()

        @pl.when(i > 0)
        def _():
            sent(2 * i - 1, turned_b, 1).wait()

        peak = half(2 * i + 1, peak, scores_a, scores_b, probs_b, turned_b)
        sent(2 * i + 1, turned_b, 1).start()
        return peak

    lax.fori_loop(0, count // 2, body, peak)
    total = output[...]
    inverse = 1.0 / total[MASK + 1 : MASK + 2, :]
    row = lax.broadcasted_iota(jnp.int32, (LANES, HALF), 0)
    total = jnp.transpose(jnp.where(row == 0, inverse, total * inverse))
    full_out[...] = total
    pairs = total.reshape(CHIPS, 2, PART // 2, LANES)
    lane = lane_of((HALF // 2, LANES))
    low = pltpu.roll(pairs[:, 0].reshape(HALF // 2, LANES), LANES - VALUE, 1)
    high = pltpu.roll(pairs[:, 1].reshape(HALF // 2, LANES), LANES - VALUE + HEAD, 1)
    packed = jnp.where(lane < HEAD, low, jnp.where(lane < 2 * HEAD, high, 0.0))
    packed_out[...] = packed.astype(bf16).reshape(CHIPS, PART // 2, LANES)
    sent(count - 2, turned_a, 0).wait()
    sent(count - 1, turned_b, 1).wait()


def middle_kernel(
    lengths, heads_in, mixed, cotangent, text_keys, text_values, w_attn, b_attn, w_cross_query,
    w_cross_out, b_cross, w_ff_in, b_ff_in, w_ff_turned, b_ff_out, result_out, grad_out, heads_out,
    probs_keep,
):
    half = CELLS // 2
    split = w_attn.shape[1] // 2
    packed = jnp.concatenate(
        [heads_in[:, head].reshape(half, LANES) for head in range(HEADS)], axis=1
    )
    both = dot(packed, w_attn[...])
    shape = (ITEMS, 1, PART // 2, C)
    attended = jnp.concatenate(
        [both[:, :C].reshape(shape), both[:, split : split + C].reshape(shape)], axis=1
    ).reshape(CELLS, C)
    first = mixed[...] + attended + b_attn[...]
    unit_two, rate_two = moments(first)
    cross_query = dot(unit_two.astype(bf16), w_cross_query[...]).astype(bf16)
    lane = lane_of((PART, C))
    in_head = [(lane >= HEAD * h) & (lane < HEAD * (h + 1)) for h in range(HEADS)]

    def spread(values):
        return jnp.concatenate(
            [jnp.where(mask, values, jnp.zeros_like(values)) for mask in in_head], axis=0
        )

    def gather(values):
        total = jnp.zeros((PART, C), f32)
        for h, mask in enumerate(in_head):
            total = jnp.where(mask, values[h * PART : (h + 1) * PART], total)
        return total

    token = lane_of((HEADS * PART, TEXT))
    outs = []
    for item in range(ITEMS):
        cells = slice(item * PART, (item + 1) * PART)
        scores = dot_nt(spread(cross_query[cells]), text_keys[item]) * SCALE
        scores = jnp.where(token < lengths[item], scores, MASKED)
        weights = jnp.exp(scores - jnp.max(scores, -1, keepdims=True))
        probs = weights / jnp.sum(weights, -1, keepdims=True)
        probs_keep[item] = probs
        outs.append(gather(dot(probs.astype(bf16), text_values[item])))
    cross = jnp.concatenate(outs, axis=0).astype(bf16)
    second = first + dot(cross, w_cross_out[...]) + b_cross[...]
    unit_three, rate_three = moments(second)
    normed_three = unit_three.astype(bf16)
    upstream = cotangent[...]
    result = second + b_ff_out[...]
    grad_normed = jnp.zeros((CELLS, C), f32)
    step = 256
    for at in range(0, FF, step):
        values, gates = slice(at, at + step), slice(FF + at, FF + at + step)
        value = dot(normed_three, w_ff_in[:, values]) + b_ff_in[values]
        gate = dot(normed_three, w_ff_in[:, gates]) + b_ff_in[gates]
        normal = 0.5 + 0.5 * lax.erf(gate * (0.5**0.5))
        density = jnp.exp(gate * gate * -0.5) * 0.3989422804014327
        gelu = gate * normal
        result += dot_nt((value * gelu).astype(bf16), w_ff_turned[:, values])
        grad_act = dot(upstream, w_ff_turned[:, values])
        grad_value = (grad_act * gelu).astype(bf16)
        grad_gate = (grad_act * value * (normal + gate * density)).astype(bf16)
        grad_normed += dot_nt(grad_value, w_ff_in[:, values])
        grad_normed += dot_nt(grad_gate, w_ff_in[:, gates])
    result_out[...] = result.astype(bf16)
    grad_second = upstream.astype(f32) + norm_back(unit_three, rate_three, grad_normed)
    grad_cross = dot_nt(grad_second.astype(bf16), w_cross_out[...]).astype(bf16)
    outs = []
    for item in range(ITEMS):
        cells = slice(item * PART, (item + 1) * PART)
        grad_probs = dot_nt(spread(grad_cross[cells]), text_values[item])
        probs = probs_keep[item]
        weighted = jnp.sum(probs * grad_probs, -1, keepdims=True)
        grad_scores = (probs * (grad_probs - weighted)).astype(bf16)
        outs.append(gather(dot(grad_scores, text_keys[item])))
    grad_query = (jnp.concatenate(outs, axis=0) * SCALE).astype(bf16)
    grad_first = grad_second + norm_back(
        unit_two, rate_two, dot_nt(grad_query, w_cross_query[...])
    )
    grad_out[...] = grad_first
    pairs = grad_first.reshape(ITEMS, 2, PART // 2, C)
    gap = jnp.zeros((half, split - C), f32)
    both = jnp.concatenate(
        [pairs[:, 0].reshape(half, C), gap, pairs[:, 1].reshape(half, C), gap], axis=1
    ).astype(bf16)
    packed = dot_nt(both, w_attn[...]).astype(bf16)
    for head in range(HEADS):
        piece = packed[:, head * LANES : (head + 1) * LANES]
        heads_out[:, head] = piece.reshape(ITEMS, PART // 2, LANES)


WIDE_BLOCK = 512
WIDE_STEP = 1024


def turn_kernel(own, other, keys_out, query_out):
    keys_out[:, :HALF] = jnp.transpose(own[...])
    keys_out[:, HALF:] = jnp.transpose(other[...])
    lane = lane_of((HALF, LANES))
    query = pltpu.roll(own[...].astype(f32), KEY, 1)
    query = jnp.where((lane >= KEY) & (lane < VALUE), query, 0.0).astype(bf16)
    query_out[...] = jnp.transpose(query)


def attend_back_kernel(
    keys_turned, query_turned, full, packed, probs_in, own_out, other_out,
    grads, left, sums, scores, probs_a, probs_b, sems,
):
    half, count = HALF // 2, HALF // WIDE_BLOCK

    def block(b):
        return pl.ds(pl.multiple_of(b * WIDE_BLOCK, WIDE_BLOCK), WIDE_BLOCK)

    def fetched(b, probs, n):
        return pltpu.make_async_copy(probs_in.at[block(b)], probs, sems.at[n])

    fetched(0, probs_a, 0).start()
    fetched(1, probs_b, 1).start()
    lane = lane_of((half, LANES))
    value_lane = (lane >= VALUE) & (lane < MASK)
    pairs = packed[...].reshape(half, LANES).astype(f32)
    low = jnp.where(value_lane, pltpu.roll(pairs, VALUE, 1), 0.0)
    high = jnp.where(value_lane, pltpu.roll(pairs, VALUE - HEAD, 1), 0.0)
    shape = (CHIPS, 1, PART // 2, LANES)
    upstream = jnp.concatenate([low.reshape(shape), high.reshape(shape)], axis=1)
    upstream = upstream.reshape(HALF, LANES)
    lane = lane_of((HALF, LANES))
    outputs = full[...]
    upstream *= jnp.sum(jnp.where(lane == 0, outputs, 0.0), axis=1, keepdims=True)
    weighted = jnp.sum(upstream * outputs, axis=1, keepdims=True)
    first = weighted.astype(bf16).astype(f32)
    upstream = jnp.where(lane == MASK + 4, -first, upstream)
    upstream = jnp.where(lane == MASK + 5, first - weighted, upstream).astype(bf16)
    grads[...] = upstream
    for b in range(count):
        rows, at = slice(b * WIDE_BLOCK, (b + 1) * WIDE_BLOCK), 2 * b * WIDE_BLOCK
        left[:, at : at + WIDE_BLOCK] = query_turned[:, rows]
        left[:, at + WIDE_BLOCK : at + 2 * WIDE_BLOCK] = jnp.transpose(upstream[rows])
    sums[...] = jnp.zeros_like(sums)

    def work(b, probs):
        rows = block(b)
        upstream = grads[rows, :]
        both = left[:, pl.ds(pl.multiple_of(2 * b * WIDE_BLOCK, 2 * WIDE_BLOCK), 2 * WIDE_BLOCK)]
        for at in range(0, 2 * HALF, WIDE_STEP):
            keys = slice(at, at + WIDE_STEP)
            part = probs[:, keys]
            grad = dot(upstream, keys_turned[:, keys])
            grad = (part.astype(f32) * grad).astype(bf16)
            sums[:, keys] += dot(both, jnp.concatenate([grad, part], axis=0))
            scores[keys, :] = jnp.transpose(grad)
        grad_query = jnp.transpose(dot(keys_turned[...], scores[...])) * SCALE
        own_out[rows, :] = pltpu.roll(grad_query, LANES - KEY, 1)

    def body(i, carry):
        fetched(2 * i, probs_a, 0).wait()
        work(2 * i, probs_a)

        @pl.when(2 * i + 2 < count)
        def _():
            fetched(2 * i + 2, probs_a, 0).start()

        fetched(2 * i + 1, probs_b, 1).wait()
        work(2 * i + 1, probs_b)

        @pl.when(2 * i + 3 < count)
        def _():
            fetched(2 * i + 3, probs_b, 1).start()

        return carry

    lax.fori_loop(0, count // 2, body, 0)
    scale = jnp.where(lane < VALUE, SCALE, 1.0)
    rest = jnp.where(lane < MASK, jnp.transpose(sums[:, :HALF]) * scale, 0.0)
    own_out[...] = jnp.where(lane < KEY, own_out[...], rest)
    rest = jnp.where(
        (lane >= KEY) & (lane < MASK), jnp.transpose(sums[:, HALF:]) * scale, 0.0
    )
    other_out[...] = rest.astype(bf16)


def join_kernel(w_query, w_key, w_value, joined_out):
    blank = jnp.zeros((C, LANES - MASK), f32)
    parts = [w[...].astype(f32) for w in (w_query, w_key, w_value)]
    for head in range(HEADS):
        at = slice(head * HEAD, (head + 1) * HEAD)
        joined = jnp.concatenate([part[:, at] for part in parts] + [blank], axis=1)
        joined_out[:, head * LANES : (head + 1) * LANES] = joined.astype(bf16)


def spread_kernel(w_attn, spread_out):
    rows = w_attn[...].astype(f32)
    gap = jnp.zeros((HEAD, 384 - C), f32)
    for head in range(HEADS):
        part = jnp.concatenate([rows[head * HEAD : (head + 1) * HEAD], gap], axis=1)
        blank = jnp.zeros_like(part)
        block = jnp.concatenate(
            [
                jnp.concatenate([part, blank], axis=1),
                jnp.concatenate([blank, part], axis=1),
                jnp.zeros((LANES - 2 * HEAD, 768), f32),
            ],
            axis=0,
        )
        spread_out[head * LANES : (head + 1) * LANES, :] = block.astype(bf16)


def widen_kernel(w_in, b_in, turned_out):
    wide = jnp.concatenate([w_in[...], bias_rows(b_in[...])], axis=0)
    turned_out[...] = jnp.transpose(wide)


def finish_kernel(
    place, rows, w_qkv, mixed, grad_first, slope, smooth, cond, w_out, latent_out, parts_out
):
    joined = jnp.concatenate(
        [rows[:, head].reshape(CELLS, LANES) for head in range(HEADS)], axis=1
    )
    unit, rate = moments(mixed[...])
    latent = grad_first[...] + norm_back(unit, rate, dot_nt(joined, w_qkv[...]))
    latent_out[...] = latent
    branch = latent.astype(bf16)
    inner = (dot_nt(branch, w_out[...]) * slope[...]).astype(bf16)
    inner_turned = jnp.transpose(inner)
    branch_turned = jnp.transpose(branch)
    here, there = place[1], 1 - place[1]

    def put(side, at, values):
        values = values.astype(bf16)
        for t in range(0, 3 * LANES, LANES):
            parts_out[side, at : at + C, :] = values[:, t : t + LANES]
            at += C

    lane = lane_of((C, LANES))
    ones = jnp.zeros((C, LANES), f32)
    kept = None
    for n in range(10):
        moment = dot(inner_turned, cond[n]) if n < 9 else dot(branch_turned, cond[4])
        one = pltpu.roll(moment[:, LANES:], n, 1)
        ones = jnp.where(lane == 64 + n, one, ones)
        if n % 2 == 0:
            kept = moment[:, :CIN]
            continue
        both = jnp.concatenate([kept, moment[:, :CIN]], axis=1)
        pair = n // 2
        put(here if pair < 3 else there, 3 * C * (pair % 3), both)
    values = dot(branch_turned, smooth[...])
    last = jnp.concatenate([values[:, 2 * LANES :], ones[:, 64:]], axis=1)
    put(there, 6 * C, jnp.concatenate([values[:, : 2 * LANES], last], axis=1))
    for side in range(2):
        parts_out[side, 9 * C :, :] = jnp.zeros((SUM_ROWS - 9 * C, LANES), bf16)


def weights_kernel(
    place, mine, theirs, w_turned, w_conv, win_out, bin_out, wconv_out, bconv_out, wout_out,
    bout_out, total, taps, sems,
):
    here = place[1]
    total[here] = mine[...]
    total[1 - here] = theirs[...]

    def take(half, at):
        return jnp.concatenate(
            [total[half, at + C * t : at + C * (t + 1), :] for t in range(3)], axis=1
        )

    last = take(1, 6 * C).astype(f32)
    ones = last[:, 2 * LANES :]
    lane = lane_of((C, LANES))

    def moment_of(n):
        pair = n // 2
        both = take(pair // 3, 3 * C * (pair % 3)).astype(f32)
        both = both[:, CIN * (n % 2) : CIN * (n % 2 + 1)]
        one = jnp.sum(jnp.where(lane == 64 + n, ones, 0.0), axis=1, keepdims=True)
        spare = lane_of((C, WIDE - CIN))
        return jnp.concatenate([both, jnp.where(spare < 3, one, 0.0)], axis=1).astype(bf16)

    grad_in = jnp.zeros((C, WIDE), f32)
    copies = []
    for n in range(9):
        moment = moment_of(n)
        taps[n] = dot_nt(w_turned[...], moment)
        copy = pltpu.make_async_copy(taps.at[n], wconv_out.at[n], sems.at[n])
        copy.start()
        copies.append(copy)
        grad_in += dot(w_conv[n], moment)
        if n == 4:
            bconv_out[...] = jnp.transpose(moment.astype(f32))[CIN]
    moment = jnp.transpose(moment_of(9).astype(f32))
    grad_in = jnp.transpose(grad_in) + moment
    win_out[...] = grad_in[:CIN]
    bin_out[...] = grad_in[CIN]
    bout_out[...] = moment[CIN]
    wout_out[...] = jnp.transpose(last)[:C]
    for copy in copies:
        copy.wait()


def swap(array):
    return lax.ppermute(array, "c", [(0, 1), (1, 0)])


def across(blocks):
    return lax.all_to_all(blocks, ACROSS, 0, 0, tiled=True)


def per_device(
    latent, condition, text_states, valid_rows, text_lengths, w_in, b_in, w_conv, b_conv, w_out,
    b_out, w_query, w_key, w_value, w_attn_out, b_attn_out, w_cross_query, w_cross_key,
    w_cross_value, w_cross_out, b_cross_out, w_ff_in, b_ff_in, w_ff_out, b_ff_out, cotangent,
):
    core = lax.axis_index("c")
    place = jnp.stack([lax.axis_index("sp"), core, 2 * lax.axis_index("x") + core])
    place = place.astype(jnp.int32)

    down = [(i, i + 1) for i in range(15)]
    top = lax.ppermute(condition[:, ROWS - 1 :], "sp", down)
    bottom = lax.ppermute(condition[:, :1], "sp", [(b, a) for a, b in down])
    right_way = [(i, i + 1) for i in range(7)]

    def edge(col):
        tall = jnp.concatenate([top[:, :, col], condition[:, :, col], bottom[:, :, col]], axis=1)
        return tall.reshape(ITEMS * (ROWS + 2), CIN)

    left = lax.ppermute(edge(COLS - 1), ("x", "c"), right_way)
    right = lax.ppermute(edge(0), ("x", "c"), [(b, a) for a, b in right_way])
    top, first_bias = after(top, b_in)
    adapter_arrays = bring(
        [
            w_in, first_bias, w_conv.reshape(9, C, C), condition, latent.reshape(CELLS, C),
            b_conv, w_out, b_out, w_query, w_key, w_value,
        ],
        "load_adapter",
    )
    (w_in_here, b_in_here, taps_here, condition_here, latent_here, b_conv_here) = adapter_arrays[:6]
    (w_out_here, b_out_here, w_query_here, w_key_here, w_value_here) = adapter_arrays[6:]

    rows, mixed, smooth, slope, cond = call(
        adapter_kernel,
        (
            out(ITEMS, HEADS, PART, LANES),
            out(CELLS, C, dtype=f32),
            out(CELLS, C),
            out(CELLS, C, dtype=f32),
            out(9, CELLS, WIDE),
        ),
        (
            place, valid_rows, condition_here, top, bottom, left, right, latent_here, w_in_here,
            b_in_here, taps_here, b_conv_here, w_out_here, b_out_here, w_query_here, w_key_here,
            w_value_here,
        ),
        "adapter",
        scalars=2,
        scratch=[pltpu.VMEM((WIDE, C), bf16)],
        vmem=24,
        store=(1, 2, 3, 4),
        near=(0,),
        held=(2,) + tuple(range(7, 17)),
    )

    own = across(rows.reshape(CHIPS, PART, LANES)).reshape(HALF, LANES)
    other = swap(own)
    packed, full, probs = call(
        attend_kernel,
        (
            out(CHIPS, PART // 2, LANES),
            out(HALF, LANES, dtype=f32),
            out(HALF, 2 * HALF),
        ),
        (own, other),
        "attend",
        scratch=[
            pltpu.VMEM((2 * HALF, BLOCK), f32),
            pltpu.VMEM((2 * HALF, BLOCK), f32),
            pltpu.VMEM((2 * HALF, BLOCK), bf16),
            pltpu.VMEM((2 * HALF, BLOCK), bf16),
            pltpu.VMEM((BLOCK, 2 * HALF), bf16),
            pltpu.VMEM((BLOCK, 2 * HALF), bf16),
            pltpu.VMEM((LANES, 2 * HALF), bf16),
            pltpu.VMEM((LANES, HALF), bf16),
            pltpu.VMEM((LANES, HALF), f32),
            pltpu.SemaphoreType.DMA((2,)),
        ],
        vmem=32,
        store=(0, 1),
        far=(4,),
    )

    packed, text, attn_weight = after(packed, text_states, w_attn_out)
    text_keys, text_values = call(
        text_kernel,
        (out(ITEMS, TEXT, C), out(ITEMS, TEXT, C)),
        (text.transpose(1, 0, 2).reshape(-1, text.shape[2]), w_cross_key.T, w_cross_value.T),
        "text",
        fetch=(0, 1, 2),
        store=(0, 1),
    )
    (w_attn_spread,) = bring(
        [], "spread", spread_kernel, (out(HEADS * LANES, 768),), (attn_weight,)
    )
    heads_in = across(packed).reshape(ITEMS, HEADS, PART // 2, LANES)
    result, grad_first, heads_out = call(
        middle_kernel,
        (out(CELLS, C), out(CELLS, C, dtype=f32), out(ITEMS, HEADS, PART // 2, LANES)),
        (
            text_lengths, heads_in, mixed, cotangent.reshape(CELLS, C), text_keys, text_values,
            w_attn_spread, b_attn_out, w_cross_query, w_cross_out, b_cross_out, w_ff_in, b_ff_in,
            w_ff_out.T, b_ff_out,
        ),
        "middle",
        scalars=1,
        scratch=[pltpu.VMEM((ITEMS, HEADS * PART, TEXT), f32)],
        vmem=32,
        fetch=(2, 7, 8, 4, 5, 9, 10, 3, 11, 12, 13, 14),
        store=(0, 1, 2),
        held=(6,),
    )

    heads_out, own_again = after(heads_out, own)
    keys_turned, query_turned = bring(
        [],
        "turn",
        turn_kernel,
        (out(LANES, 2 * HALF), out(LANES, HALF)),
        (own_again, other),
    )
    grads_in = across(heads_out.reshape(CHIPS, PART // 2, LANES))
    own_grads, other_grads = call(
        attend_back_kernel,
        (out(HALF, LANES, dtype=f32), out(HALF, LANES)),
        (keys_turned, query_turned, full, grads_in, probs),
        "attend_back",
        scratch=[
            pltpu.VMEM((HALF, LANES), bf16),
            pltpu.VMEM((LANES, 2 * HALF), bf16),
            pltpu.VMEM((LANES, 2 * HALF), f32),
            pltpu.VMEM((2 * HALF, WIDE_BLOCK), bf16),
            pltpu.VMEM((WIDE_BLOCK, 2 * HALF), bf16),
            pltpu.VMEM((WIDE_BLOCK, 2 * HALF), bf16),
            pltpu.SemaphoreType.DMA((2,)),
        ],
        vmem=36,
        near=(0, 1),
        held=(0, 1),
        fetch=(2,),
        far=(4,),
    )
    row_grads = (own_grads + swap(other_grads).astype(f32)).astype(bf16)

    row_grads, query_weight = after(row_grads, w_query)
    mixed_here, grad_here, w_out_here, slope_here, smooth_here, w_joined = bring(
        [mixed, grad_first, w_out, slope, smooth],
        "load_finish",
        join_kernel,
        (out(C, HEADS * LANES),),
        (query_weight, w_key, w_value),
    )
    row_grads = across(row_grads.reshape(CHIPS, PART, LANES))
    latent_grad, parts = call(
        finish_kernel,
        (out(CELLS, C, dtype=f32), out(2, SUM_ROWS, LANES)),
        (
            place, row_grads.reshape(ITEMS, HEADS, PART, LANES), w_joined, mixed_here, grad_here,
            slope_here, smooth_here, cond, w_out_here,
        ),
        "finish",
        scalars=1,
        store=(0,),
        fetch=(7,),
        held=(2, 3, 4, 5, 6, 8),
    )

    shares = (parts[0].astype(f32) + swap(parts[1]).astype(f32)).astype(bf16)
    shares, last_bias = after(shares, b_in)
    taps_last, w_turned = bring(
        [w_conv.reshape(9, C, C)],
        "load_weights",
        widen_kernel,
        (out(C, WIDE),),
        (w_in, last_bias),
    )
    shares = across(shares.reshape(CHIPS, SUM_ROWS // CHIPS, LANES))
    share = jnp.sum(shares.astype(f32), axis=0).astype(bf16)
    mine = across(jnp.broadcast_to(share[None], shares.shape)).reshape(SUM_ROWS, LANES)
    theirs = swap(mine)
    grad_w_in, grad_b_in, grad_w_conv, grad_b_conv, grad_w_out, grad_b_out = call(
        weights_kernel,
        (
            out(CIN, C, dtype=f32),
            out(C, dtype=f32),
            out(9, C, C, dtype=f32),
            out(C, dtype=f32),
            out(C, C, dtype=f32),
            out(C, dtype=f32),
        ),
        (place, mine, theirs, w_turned, taps_last),
        "weights",
        scalars=1,
        scratch=[
            pltpu.VMEM((2, SUM_ROWS, LANES), bf16),
            pltpu.VMEM((9, C, C), f32),
            pltpu.SemaphoreType.DMA((9,)),
        ],
        vmem=24,
        store=(0, 4),
        far=(7,),
        held=(3, 4),
    )
    grid = (ITEMS, ROWS, COLS, C)
    return (
        result.reshape(grid),
        latent_grad.reshape(grid),
        grad_w_in,
        grad_b_in,
        grad_w_conv.reshape(3, 3, C, C),
        grad_b_conv,
        grad_w_out,
        grad_b_out,
    )


def solution(mesh):
    split = Mesh(mesh.devices.reshape(16, 4, 2), ("sp", "x", "c"))
    cells = P(None, "sp", ("x", "c"), None)
    in_specs = (cells, cells) + (P(),) * 23 + (cells,)
    out_specs = (cells, cells) + (P(),) * 6
    return jax.shard_map(
        per_device, mesh=split, in_specs=in_specs, out_specs=out_specs, check_vma=False
    )
```

profile of v0, /device:TPU:1, one launch (start us, length us, event | category | flops | bytes accessed | tf_op | source)
XLA Modules:
  0.0 204.2 jit_solution(6283126753749249759)
XLA Ops:
  2.7 4.7 %collective-permute-start = (bf16[8,1,8,192]{3,2,1,0:T(8,128)(2,1)S(1)}, bf16[8,1,8,192]{3,2,1,0:T(8,128)(2,1)S(1)}, u32[]{:S(2)}, u32[]{:S(2)}) collective-permute-start(bf16[8,1,8,192]{3,2,1,0:T(8,128)(2,1)S(1)} %get-tuple-element.121), channel_id=1, source_target_pairs={{0,8},{8,16},{16,24},{24,32},{32,40},{40,48},{48,56},{56,64},{64,7... | collective-permute-start | bytes 73736 | tf_op jit(solution)/shard_map/ppermute | solution.py:675
  8.7 4.8 %collective-permute-start.2 = (bf16[48,192]{1,0:T(8,128)(2,1)S(1)}, bf16[48,192]{1,0:T(8,128)(2,1)S(1)}, u32[]{:S(2)}, u32[]{:S(2)}) collective-permute-start(bf16[48,192]{1,0:T(8,128)(2,1)S(1)} %reshape.73), channel_id=1, source_target_pairs={{0,1},{1,2},{2,3},{3,4},{4,5},{5,6},{6,7},{8,9},{9,10},{10,11},{11... | collective-permute-start | bytes 55304 | tf_op jit(solution)/shard_map/ppermute | solution.py:683
  13.5 1.9 collective-permute-start.3
  15.5 2.1 %load_adapter.1 = (bf16[192,320]{1,0:T(8,128)(2,1)S(1)}, f32[320]{0:T(512)S(1)}, bf16[9,320,320]{2,1,0:T(8,128)(2,1)S(1)}, bf16[8,4,8,192]{3,2,1,0:T(8,128)(2,1)...) custom-call(bf16[192,320]{1,0:T(8,128)(2,1)} %refs_1_.4, ...), custom_call_target="tpu_custom_call" | custom-call | tf_op jit(solution)/shard_map/load_adapter/pallas_call | solution.py:166
  18.7 4.6 %adapter.1 = (bf16[8,8,32,128]{3,2,1,0:T(8,128)(2,1)S(1)}, f32[256,320]{1,0:T(8,128)}, bf16[256,320]{1,0:T(8,128)(2,1)}, f32[256,320]{1,0:T(8,128)}, bf16[9,256,256]{2,1,0:T(8,128)(2,1)}) custom-call(s32[3]{0:T(128)S(1)} %pad_add_fusion.refs_0_, s32[8]{0:T(128)S(1)} %copy-done.6, bf16[8,4,8,192]{3,2,1,0:T(8,128)(2,1)S(1)} %get-tuple-element.64.refs_2_, ...), custom_call_target="tpu_custom_call" | custom-call | tf_op jit(solution)/shard_map/adapter/pallas_call | solution.py:131
  23.3 26.2 %all_to_all.30 = bf16[64,32,128]{2,1,0:T(8,128)(2,1)S(1)} all-to-all(bf16[64,32,128]{2,1,0:T(8,128)(2,1)S(1)} %bitcast.47), channel_id=1, replica_groups=mesh['sp'=16,'x'=4,'c'=2] {'sp','x'}, dimensions={0} | all-to-all | bytes 1048576 | tf_op jit(solution)/shard_map/all_to_all | solution.py:662
  52.6 12.5 %attend.1 = (bf16[64,16,128]{2,1,0:T(8,128)(2,1)}, f32[2048,128]{1,0:T(8,128)}, bf16[2048,4096]{1,0:T(8,128)(2,1)}) custom-call(bf16[2048,128]{1,0:T(8,128)(2,1)S(1)} %bitcast.41, bf16[2048,128]{1,0:T(8,128)(2,1)S(1)} %collective-permute-done.4.refs_1_), custom_call_target="tpu_custom_call" | custom-call | tf_op jit(solution)/shard_map/attend/pallas_call | solution.py:131
  65.1 4.8 %all-to-all-start.1 = ((bf16[64,16,128]{2,1,0:T(8,128)(2,1)}), bf16[64,16,128]{2,1,0:T(8,128)(2,1)S(1)}, u32[]{:S(2)}, u32[]{:S(2)}) async-start(bf16[64,16,128]{2,1,0:T(8,128)(2,1)} %get-tuple-element.78), calls=%async_computation.1 | async-start | bytes 524288 | tf_op jit(solution)/shard_map/all_to_all | solution.py:662
  70.0 7.4 %text.1 = (bf16[8,80,320]{2,1,0:T(8,128)(2,1)}, bf16[8,80,320]{2,1,0:T(8,128)(2,1)}) custom-call(bf16[616,768]{1,0:T(8,128)(2,1)} %bitcast.51, bf16[320,768]{1,0:T(8,128)(2,1)} %bitcast.53, bf16[320,768]{1,0:T(8,128)(2,1)} %bitcast.54), custom_call_target="tpu_custom_call" | custom-call | tf_op jit(solution)/shard_map/text/pallas_call | solution.py:131
  77.4 2.5 %all-to-all-done.1 = bf16[64,16,128]{2,1,0:T(8,128)(2,1)S(1)} async-done(((bf16[64,16,128]{2,1,0:T(8,128)(2,1)}), bf16[64,16,128]{2,1,0:T(8,128)(2,1)S(1)}, u32[]{:S(2)}, u32[]{:S(2)}) %all-to-all-start.1) | async-done | bytes 262176 | tf_op jit(solution)/shard_map/all_to_all | solution.py:662
  79.9 13.8 %middle.1 = (bf16[256,320]{1,0:T(8,128)(2,1)}, f32[256,320]{1,0:T(8,128)}, bf16[8,8,16,128]{3,2,1,0:T(8,128)(2,1)}) custom-call(s32[8]{0:T(128)S(1)} %copy-done.7, bf16[8,8,16,128]{3,2,1,0:T(8,128)(2,1)S(1)} %bitcast.46, f32[256,320]{1,0:T(8,128)} %get-tuple-element.79.refs_2_.refs_0_, bf16[256,320]{1,0:T(8,128)(2,1)} %bitcast.56, ...), custom_call_target="tpu_custom_call" | custom-call | tf_op jit(solution)/shard_map/middle/pallas_call | solution.py:131
  93.7 7.4 %all-to-all-start.2 = ((bf16[64,16,128]{2,1,0:T(8,128)(2,1)}), bf16[64,16,128]{2,1,0:T(8,128)(2,1)S(1)}, u32[]{:S(2)}, u32[]{:S(2)}) async-start(bf16[64,16,128]{2,1,0:T(8,128)(2,1)} %bitcast.55), calls=%async_computation.2 | async-start | bytes 524288 | tf_op jit(solution)/shard_map/all_to_all | solution.py:662
  101.7 8.6 %all-to-all-done.2.refs_3_ = bf16[64,16,128]{2,1,0:T(8,128)(2,1)S(1)} async-done(((bf16[64,16,128]{2,1,0:T(8,128)(2,1)}), bf16[64,16,128]{2,1,0:T(8,128)(2,1)S(1)}, u32[]{:S(2)}, u32[]{:S(2)}) %all-to-all-start.2) | async-done | bytes 262176 | tf_op jit(solution)/shard_map/all_to_all | solution.py:662
  110.4 15.8 %attend_back.1 = (f32[2048,128]{1,0:T(8,128)S(1)}, bf16[2048,128]{1,0:T(8,128)(2,1)S(1)}) custom-call(bf16[128,4096]{1,0:T(8,128)(2,1)S(1)} %get-tuple-element.87.refs_0_, bf16[128,2048]{1,0:T(8,128)(2,1)S(1)} %get-tuple-element.88.refs_1_, f32[2048,128]{1,0:T(8,128)} %get-tuple-element.89.refs_2_, bf16[64,16,128]{2,1,0:T(8,128)(2,1)S(1)} %all-to-all-done.2.refs_3_, ...), custom_call_target="tpu_custom_call" | custom-call | tf_op jit(solution)/shard_map/attend_back/pallas_call | solution.py:131
  126.2 2.2 %collective-permute-start.5 = (bf16[2048,128]{1,0:T(8,128)(2,1)S(1)}, bf16[2048,128]{1,0:T(8,128)(2,1)S(1)}, u32[]{:S(2)}, u32[]{:S(2)}) collective-permute-start(bf16[2048,128]{1,0:T(8,128)(2,1)S(1)} %get-tuple-element.93), channel_id=1, source_target_pairs={{0,1},{1,0},{2,3},{3,2},{4,5},{5,4},{6,7},{7,6},{8,9},{9,8},{10,11... | collective-permute-start | bytes 1572872 | tf_op jit(solution)/shard_map/ppermute | solution.py:658
  130.8 4.6 %all-to-all-start.3 = ((bf16[64,32,128]{2,1,0:T(8,128)(2,1)}), bf16[64,32,128]{2,1,0:T(8,128)(2,1)S(1)}, u32[]{:S(2)}, u32[]{:S(2)}) async-start(bf16[64,32,128]{2,1,0:T(8,128)(2,1)} %bitcast.18), calls=%async_computation.3 | async-start | bytes 1048576 | tf_op jit(solution)/shard_map/all_to_all | solution.py:662
  135.5 2.0 load_finish.1
  137.4 10.5 %all-to-all-done.3 = bf16[64,32,128]{2,1,0:T(8,128)(2,1)S(1)} async-done(((bf16[64,32,128]{2,1,0:T(8,128)(2,1)}), bf16[64,32,128]{2,1,0:T(8,128)(2,1)S(1)}, u32[]{:S(2)}, u32[]{:S(2)}) %all-to-all-start.3) | async-done | bytes 524320 | tf_op jit(solution)/shard_map/all_to_all | solution.py:662
  148.0 2.5 %finish.1 = (f32[256,320]{1,0:T(8,128)}, bf16[2,3072,128]{2,1,0:T(8,128)(2,1)S(1)}) custom-call(s32[3]{0:T(128)S(1)} %pad_add_fusion.refs_0_, bf16[8,8,32,128]{3,2,1,0:T(8,128)(2,1)S(1)} %bitcast.45, bf16[320,1024]{1,0:T(8,128)(2,1)S(1)} %get-tuple-element.99.refs_2_, f32[256,320]{1,0:T(8,128)S(1)} %get-tuple-element.100.refs_3_, ...), custom_call_target="tpu_custom_call" | custom-call | tf_op jit(solution)/shard_map/finish/pallas_call | solution.py:131
  152.5 1.9 collective-permute-done.6
  154.6 19.7 %all_to_all.31 = bf16[64,48,128]{2,1,0:T(8,128)(2,1)S(1)} all-to-all(bf16[64,48,128]{2,1,0:T(8,128)(2,1)S(1)} %bitcast.50), channel_id=1, replica_groups=mesh['sp'=16,'x'=4,'c'=2] {'sp','x'}, dimensions={0} | all-to-all | bytes 1572864 | tf_op jit(solution)/shard_map/all_to_all | solution.py:662
  174.5 18.3 %all_to_all.32 = bf16[64,48,128]{2,1,0:T(8,128)(2,1)S(1)} all-to-all(bf16[64,48,128]{2,1,0:T(8,128)(2,1)S(1)} %broadcast_in_dim.2), channel_id=1, replica_groups=mesh['sp'=16,'x'=4,'c'=2] {'sp','x'}, dimensions={0} | all-to-all | bytes 1572864 | tf_op jit(solution)/shard_map/all_to_all | solution.py:662
  192.8 3.1 %collective-permute-start.7 = (bf16[3072,128]{1,0:T(8,128)(2,1)S(1)}, bf16[3072,128]{1,0:T(8,128)(2,1)S(1)}, u32[]{:S(2)}, u32[]{:S(2)}) collective-permute-start(bf16[3072,128]{1,0:T(8,128)(2,1)S(1)} %bitcast.43), channel_id=1, source_target_pairs={{0,1},{1,0},{2,3},{3,2},{4,5},{5,4},{6,7},{7,6},{8,9},{9,8},{10,11... | collective-permute-start | bytes 2359304 | tf_op jit(solution)/shard_map/ppermute | solution.py:658
  197.9 6.1 %weights.1 = (f32[192,320]{1,0:T(8,128)}, f32[320]{0:T(512)}, f32[9,320,320]{2,1,0:T(8,128)}, f32[320]{0:T(512)}, f32[320,320]{1,0:T(8,128)}, /*index=5*/f32[320]{0:T(512)}) custom-call(s32[3]{0:T(128)S(1)} %pad_add_fusion.refs_0_, bf16[3072,128]{1,0:T(8,128)(2,1)S(1)} %bitcast.44, bf16[3072,128]{1,0:T(8,128)(2,1)S(1)} %collective-permute-done.7.refs_2_, ...), custom_call_target="tpu_custom_call" | custom-call | tf_op jit(solution)/shard_map/weights/pallas_call | solution.py:131
  (48 shorter events, 14.8 us)
Async XLA Ops:
  1.4 7.0 %collective-permute-start.1 = (bf16[8,1,8,192]{3,2,1,0:T(8,128)(2,1)S(1)}, bf16[8,1,8,192]{3,2,1,0:T(8,128)(2,1)S(1)}, u32[]{:S(2)}, u32[]{:S(2)}) collective-permute-start(bf16[8,1,8,192]{3,2,1,0:T(8,128)(2,1)S(1)} %get-tuple-element.120), channel_id=1, source_target_pairs={{8,0},{16,8},{24,16},{32,24},{40,32},{48,40},{56,48},{64,56},{72,6... | collective-permute-start | bytes 73736 | tf_op jit(solution)/shard_map/ppermute | solution.py:676
  2.7 5.8 %collective-permute-start = (bf16[8,1,8,192]{3,2,1,0:T(8,128)(2,1)S(1)}, bf16[8,1,8,192]{3,2,1,0:T(8,128)(2,1)S(1)}, u32[]{:S(2)}, u32[]{:S(2)}) collective-permute-start(bf16[8,1,8,192]{3,2,1,0:T(8,128)(2,1)S(1)} %get-tuple-element.121), channel_id=1, source_target_pairs={{0,8},{8,16},{16,24},{24,32},{32,40},{40,48},{48,56},{56,64},{64,7... | collective-permute-start | bytes 73736 | tf_op jit(solution)/shard_map/ppermute | solution.py:675
  8.7 9.0 %collective-permute-start.2 = (bf16[48,192]{1,0:T(8,128)(2,1)S(1)}, bf16[48,192]{1,0:T(8,128)(2,1)S(1)}, u32[]{:S(2)}, u32[]{:S(2)}) collective-permute-start(bf16[48,192]{1,0:T(8,128)(2,1)S(1)} %reshape.73), channel_id=1, source_target_pairs={{0,1},{1,2},{2,3},{3,4},{4,5},{5,6},{6,7},{8,9},{9,10},{10,11},{11... | collective-permute-start | bytes 55304 | tf_op jit(solution)/shard_map/ppermute | solution.py:683
  13.5 5.1 %collective-permute-start.3 = (bf16[48,192]{1,0:T(8,128)(2,1)S(1)}, bf16[48,192]{1,0:T(8,128)(2,1)S(1)}, u32[]{:S(2)}, u32[]{:S(2)}) collective-permute-start(bf16[48,192]{1,0:T(8,128)(2,1)S(1)} %reshape.74), channel_id=1, source_target_pairs={{1,0},{2,1},{3,2},{4,3},{5,4},{6,5},{7,6},{9,8},{10,9},{11,10},{12... | collective-permute-start | bytes 55304 | tf_op jit(solution)/shard_map/ppermute | solution.py:684
  15.5 3.1 %copy-start.6 = (s32[8]{0:T(128)S(1)}, s32[8]{0:T(128)}, u32[]{:S(2)}) copy-start(s32[8]{0:T(128)} %refs_1_.3) | copy-start | bytes 100
  23.3 46.6 %copy-start.4 = (bf16[320,320]{1,0:T(8,128)(2,1)S(1)}, bf16[320,320]{1,0:T(8,128)(2,1)}, u32[]{:S(2)}) copy-start(bf16[320,320]{1,0:T(8,128)(2,1)} %refs_0_.3) | copy-start | bytes 614404
  49.5 3.0 %collective-permute-start.4 = (bf16[2048,128]{1,0:T(8,128)(2,1)S(1)}, bf16[2048,128]{1,0:T(8,128)(2,1)S(1)}, u32[]{:S(2)}, u32[]{:S(2)}) collective-permute-start(bf16[2048,128]{1,0:T(8,128)(2,1)S(1)} %bitcast.40), channel_id=1, source_target_pairs={{0,1},{1,0},{2,3},{3,2},{4,5},{5,4},{6,7},{7,6},{8,9},{9,8},{10,11... | collective-permute-start | bytes 1572872 | tf_op jit(solution)/shard_map/ppermute | solution.py:658
  65.1 14.8 %all-to-all-start.1 = ((bf16[64,16,128]{2,1,0:T(8,128)(2,1)}), bf16[64,16,128]{2,1,0:T(8,128)(2,1)S(1)}, u32[]{:S(2)}, u32[]{:S(2)}) async-start(bf16[64,16,128]{2,1,0:T(8,128)(2,1)} %get-tuple-element.78), calls=%async_computation.1 | async-start | bytes 524288 | tf_op jit(solution)/shard_map/all_to_all | solution.py:662
  69.9 10.0 %copy-start.7 = (s32[8]{0:T(128)S(1)}, s32[8]{0:T(128)}, u32[]{:S(2)}) copy-start(s32[8]{0:T(128)} %refs_0_.4) | copy-start | bytes 100
  93.7 16.7 %all-to-all-start.2 = ((bf16[64,16,128]{2,1,0:T(8,128)(2,1)}), bf16[64,16,128]{2,1,0:T(8,128)(2,1)S(1)}, u32[]{:S(2)}, u32[]{:S(2)}) async-start(bf16[64,16,128]{2,1,0:T(8,128)(2,1)} %bitcast.55), calls=%async_computation.2 | async-start | bytes 524288 | tf_op jit(solution)/shard_map/all_to_all | solution.py:662
  126.2 3.8 %collective-permute-start.5 = (bf16[2048,128]{1,0:T(8,128)(2,1)S(1)}, bf16[2048,128]{1,0:T(8,128)(2,1)S(1)}, u32[]{:S(2)}, u32[]{:S(2)}) collective-permute-start(bf16[2048,128]{1,0:T(8,128)(2,1)S(1)} %get-tuple-element.93), channel_id=1, source_target_pairs={{0,1},{1,0},{2,3},{3,2},{4,5},{5,4},{6,7},{7,6},{8,9},{9,8},{10,11... | collective-permute-start | bytes 1572872 | tf_op jit(solution)/shard_map/ppermute | solution.py:658
  129.9 5.5 %copy-start = (bf16[320,320]{1,0:T(8,128)(2,1)S(1)}, bf16[320,320]{1,0:T(8,128)(2,1)}, u32[]{:S(2)}) copy-start(bf16[320,320]{1,0:T(8,128)(2,1)} %refs_5_.2) | copy-start | bytes 614404
  129.9 5.6 %copy-start.1 = (bf16[320,320]{1,0:T(8,128)(2,1)S(1)}, bf16[320,320]{1,0:T(8,128)(2,1)}, u32[]{:S(2)}) copy-start(bf16[320,320]{1,0:T(8,128)(2,1)} %refs_6_.3) | copy-start | bytes 614404
  129.9 5.6 %copy-start.2 = (bf16[320,320]{1,0:T(8,128)(2,1)S(1)}, bf16[320,320]{1,0:T(8,128)(2,1)}, u32[]{:S(2)}) copy-start(bf16[320,320]{1,0:T(8,128)(2,1)} %refs_7_.5) | copy-start | bytes 614404
  130.8 17.1 %all-to-all-start.3 = ((bf16[64,32,128]{2,1,0:T(8,128)(2,1)}), bf16[64,32,128]{2,1,0:T(8,128)(2,1)S(1)}, u32[]{:S(2)}, u32[]{:S(2)}) async-start(bf16[64,32,128]{2,1,0:T(8,128)(2,1)} %bitcast.18), calls=%async_computation.3 | async-start | bytes 1048576 | tf_op jit(solution)/shard_map/all_to_all | solution.py:662
  150.6 3.8 %collective-permute-start.6 = (bf16[3072,128]{1,0:T(8,128)(2,1)S(1)}, bf16[3072,128]{1,0:T(8,128)(2,1)S(1)}, u32[]{:S(2)}, u32[]{:S(2)}) collective-permute-start(bf16[3072,128]{1,0:T(8,128)(2,1)S(1)} %slice_bitcast_fusion), channel_id=1, source_target_pairs={{0,1},{1,0},{2,3},{3,2},{4,5},{5,4},{6,7},{7,6},{8,9},{9,8},{10,11... | collective-permute-start | bytes 2359304 | tf_op jit(solution)/shard_map/ppermute | solution.py:658
  174.3 21.7 %copy-start.3 = (bf16[192,320]{1,0:T(8,128)(2,1)S(1)}, bf16[192,320]{1,0:T(8,128)(2,1)}, u32[]{:S(2)}) copy-start(bf16[192,320]{1,0:T(8,128)(2,1)} %refs_1_.4) | copy-start | bytes 368644
  174.3 21.7 %copy-start.5 = (f32[320]{0:T(512)S(1)}, f32[320]{0:T(512)}, u32[]{:S(2)}) copy-start(f32[320]{0:T(512)} %refs_2_.2) | copy-start | bytes 3844
  192.8 5.1 %collective-permute-start.7 = (bf16[3072,128]{1,0:T(8,128)(2,1)S(1)}, bf16[3072,128]{1,0:T(8,128)(2,1)S(1)}, u32[]{:S(2)}, u32[]{:S(2)}) collective-permute-start(bf16[3072,128]{1,0:T(8,128)(2,1)S(1)} %bitcast.43), channel_id=1, source_target_pairs={{0,1},{1,0},{2,3},{3,2},{4,5},{5,4},{6,7},{7,6},{8,9},{9,8},{10,11... | collective-permute-start | bytes 2359304 | tf_op jit(solution)/shard_map/ppermute | solution.py:658
where the time goes:
time: 205 us; the launch traced here: 204 us
  Pallas kernels  69.2 us (34%)
  blocking collectives  64.2 us (31%)
  starting transfers between devices  38.3 us (19%)
  waiting for transfers between devices  27.9 us (14%)
  local copies, waits for them, and re-layouts  2.14 us (1%)
    all_to_all x3, blocking collectives, across(): return lax.all_to_all(blocks, ACROSS, 0, 0, tiled=True)  64.2 us
    pallas_call x7, Pallas kernels, call(): pl.pallas_call(body, out_shape=tuple((made_as(i, made) for i, made in enu...  62.7 us
    all_to_all x3, waiting for transfers between devices, across(): return lax.all_to_all(blocks, ACROSS, 0, 0, tiled=True)  21.6 us
    all_to_all x3, starting transfers between devices, across(): return lax.all_to_all(blocks, ACROSS, 0, 0, tiled=True)  16.8 us
    ppermute x4, starting transfers between devices, swap(): return lax.ppermute(array, 'c', [(0, 1), (1, 0)])  8.73 us
    pallas_call x5, Pallas kernels, bring(): pl.pallas_call(body, out_shape=tuple((pltpu.VMEM(x.shape, x.dtype) for x...  6.49 us
    ppermute x4, waiting for transfers between devices, swap(): return lax.ppermute(array, 'c', [(0, 1), (1, 0)])  5.25 us
    ppermute x1, starting transfers between devices, per_device(): left = lax.ppermute(edge(COLS - 1), ('x', 'c'), right_way)  4.84 us
  transfers between devices with their start and end apart: 11, of which 8 were waited for; matrix products, arithmetic and copies ran while one was open for 1% of the time, Pallas kernels for 7%

commit v1 on v0

--- a/solution.py
+++ b/solution.py
@@ -14,6 +14,7 @@
 TEXT = 80
 LANES = 128
 WIDE = 256
+GROUP = 160
 SCALE = HEAD**-0.5
 LOG2E = 1.4426950408889634
 EPS = 1e-5
@@ -248,6 +249,7 @@
     mixed_out[...] = mixed
     normed = moments(mixed)[0].astype(bf16)
     projected = [dot(normed, w[...]) for w in (w_query, w_key, w_value)]
+    projected[0] *= SCALE * LOG2E
     lane = lane_of((PART, LANES - MASK))
     row = lax.broadcasted_iota(jnp.int32, (PART, LANES - MASK), 0) // COLS + ROWS * place[0]
     extras = []
@@ -261,20 +263,53 @@
         rows_out[:, head] = joined.astype(bf16).reshape(ITEMS, PART, LANES)
 
 
-def text_kernel(text, w_key_turned, w_value_turned, keys_out, values_out):
+def text_kernel(
+    text, w_key_turned, w_value_turned, keys_out, values_out, wide_key, wide_value
+):
     count = text.shape[0]
     token = lax.broadcasted_iota(jnp.int32, (TEXT, count), 0)
     place = lane_of((TEXT, count))
-    text[:1], w_key_turned[:1], w_value_turned[:1]
+    blank = jnp.zeros((WIDE - GROUP, text.shape[1]), bf16)
+    for source, wide in ((w_key_turned, wide_key), (w_value_turned, wide_value)):
+        for g in range(2):
+            wide[g * WIDE : g * WIDE + GROUP, :] = source[g * GROUP : (g + 1) * GROUP, :]
+            wide[g * WIDE + GROUP : (g + 1) * WIDE, :] = blank
+    text[:16]
 
     def body(item, carry):
         pick = jnp.where(place == token * ITEMS + item, 1.0, 0.0).astype(bf16)
         states = dot(pick, text[...]).astype(bf16)
-        keys_out[item] = dot_nt(states, w_key_turned[...]).astype(bf16)
-        values_out[item] = dot_nt(states, w_value_turned[...]).astype(bf16)
+        keys_out.buffer[item] = dot_nt(states, wide_key[...]).astype(bf16)
+        values_out.buffer[item] = dot_nt(states, wide_value[...]).astype(bf16)
         return carry
 
     lax.fori_loop(0, ITEMS, body, 0)
+    keys_out.start()
+    values_out.start()
+
+
+def form_kernel(w_query, w_cross_out, w_attn, query_out, cross_out, spread_out):
+    rows = w_query[...].astype(f32)
+    blank = jnp.zeros((C, WIDE - GROUP), f32)
+    rows = [rows[:, :GROUP], blank, rows[:, GROUP:], blank]
+    query_out[...] = jnp.concatenate(rows, axis=1).astype(bf16)
+    rows = w_cross_out[...]
+    blank = jnp.zeros((WIDE - GROUP, C), bf16)
+    cross_out[...] = jnp.concatenate([rows[:GROUP], blank, rows[GROUP:], blank], axis=0)
+    rows = w_attn[...].astype(f32)
+    gap = jnp.zeros((HEAD, 384 - C), f32)
+    for head in range(HEADS):
+        part = jnp.concatenate([rows[head * HEAD : (head + 1) * HEAD], gap], axis=1)
+        blank = jnp.zeros_like(part)
+        block = jnp.concatenate(
+            [
+                jnp.concatenate([part, blank], axis=1),
+                jnp.concatenate([blank, part], axis=1),
+                jnp.zeros((LANES - 2 * HEAD, 768), f32),
+            ],
+            axis=0,
+        )
+        spread_out[head * LANES : (head + 1) * LANES, :] = block.astype(bf16)
 
 
 BLOCK = 256
@@ -308,13 +343,13 @@
         return pltpu.make_async_copy(turned, probs_out.at[columns(b)], sems.at[n])
 
     def half(b, peak, following, scores, probs, turned):
-        shift = jnp.max(peak, axis=0, keepdims=True) * (SCALE * LOG2E)
+        shift = jnp.max(peak, axis=0, keepdims=True)
         queries = query[:, columns(jnp.minimum(b + 1, count - 1))]
         ahead = None
         for n in range(len(chunks)):
             ahead = score(queries, n, following, ahead)
             keys = slice(n * STEP, (n + 1) * STEP)
-            part = jnp.exp2(scores[keys, :] * (SCALE * LOG2E) - shift).astype(bf16)
+            part = jnp.exp2(scores[keys, :] - shift).astype(bf16)
             probs[keys, :] = part
             turned[:, keys] = jnp.transpose(part)
         output[:, columns(b)] = dot(keys_turned[...], probs[...])
@@ -374,30 +409,39 @@
     first = mixed[...] + attended + b_attn[...]
     unit_two, rate_two = moments(first)
     cross_query = dot(unit_two.astype(bf16), w_cross_query[...]).astype(bf16)
-    lane = lane_of((PART, C))
-    in_head = [(lane >= HEAD * h) & (lane < HEAD * (h + 1)) for h in range(HEADS)]
-
-    def spread(values):
-        return jnp.concatenate(
-            [jnp.where(mask, values, jnp.zeros_like(values)) for mask in in_head], axis=0
-        )
-
-    def gather(values):
-        total = jnp.zeros((PART, C), f32)
-        for h, mask in enumerate(in_head):
-            total = jnp.where(mask, values[h * PART : (h + 1) * PART], total)
-        return total
+    lane = lane_of((PART, WIDE))
+    in_head = [(lane >= HEAD * h) & (lane < HEAD * (h + 1)) for h in range(HEADS // 2)]
+    groups = [slice(0, WIDE), slice(WIDE, 2 * WIDE)]
+    half_rows = HEADS * PART // 2
+
+    def by_head(values, others):
+        parts = []
+        for lanes in groups:
+            here = values[:, lanes]
+            rows = [jnp.where(mask, here, jnp.zeros_like(here)) for mask in in_head]
+            parts.append(dot_nt(jnp.concatenate(rows, axis=0), others[:, lanes]))
+        return jnp.concatenate(parts, axis=0)
+
+    def by_cell(weights, others):
+        parts = []
+        for g, lanes in enumerate(groups):
+            rows = dot(weights[g * half_rows : (g + 1) * half_rows], others[:, lanes])
+            total = jnp.zeros((PART, WIDE), f32)
+            for h, mask in enumerate(in_head):
+                total = jnp.where(mask, rows[h * PART : (h + 1) * PART], total)
+            parts.append(total)
+        return jnp.concatenate(parts, axis=1)
 
     token = lane_of((HEADS * PART, TEXT))
     outs = []
     for item in range(ITEMS):
         cells = slice(item * PART, (item + 1) * PART)
-        scores = dot_nt(spread(cross_query[cells]), text_keys[item]) * SCALE
+        scores = by_head(cross_query[cells], text_keys[item]) * SCALE
         scores = jnp.where(token < lengths[item], scores, MASKED)
         weights = jnp.exp(scores - jnp.max(scores, -1, keepdims=True))
         probs = weights / jnp.sum(weights, -1, keepdims=True)
         probs_keep[item] = probs
-        outs.append(gather(dot(probs.astype(bf16), text_values[item])))
+        outs.append(by_cell(probs.astype(bf16), text_values[item]))
     cross = jnp.concatenate(outs, axis=0).astype(bf16)
     second = first + dot(cross, w_cross_out[...]) + b_cross[...]
     unit_three, rate_three = moments(second)
@@ -425,11 +469,11 @@
     outs = []
     for item in range(ITEMS):
         cells = slice(item * PART, (item + 1) * PART)
-        grad_probs = dot_nt(spread(grad_cross[cells]), text_values[item])
+        grad_probs = by_head(grad_cross[cells], text_values[item])
         probs = probs_keep[item]
         weighted = jnp.sum(probs * grad_probs, -1, keepdims=True)
         grad_scores = (probs * (grad_probs - weighted)).astype(bf16)
-        outs.append(gather(dot(grad_scores, text_keys[item])))
+        outs.append(by_cell(grad_scores, text_keys[item]))
     grad_query = (jnp.concatenate(outs, axis=0) * SCALE).astype(bf16)
     grad_first = grad_second + norm_back(
         unit_two, rate_two, dot_nt(grad_query, w_cross_query[...])
@@ -527,7 +571,7 @@
         return carry
 
     lax.fori_loop(0, count // 2, body, 0)
-    scale = jnp.where(lane < VALUE, SCALE, 1.0)
+    scale = jnp.where(lane < VALUE, 1.0 / LOG2E, 1.0)
     rest = jnp.where(lane < MASK, jnp.transpose(sums[:, :HALF]) * scale, 0.0)
     own_out[...] = jnp.where(lane < KEY, own_out[...], rest)
     rest = jnp.where(
@@ -543,23 +587,6 @@
         at = slice(head * HEAD, (head + 1) * HEAD)
         joined = jnp.concatenate([part[:, at] for part in parts] + [blank], axis=1)
         joined_out[:, head * LANES : (head + 1) * LANES] = joined.astype(bf16)
-
-
-def spread_kernel(w_attn, spread_out):
-    rows = w_attn[...].astype(f32)
-    gap = jnp.zeros((HEAD, 384 - C), f32)
-    for head in range(HEADS):
-        part = jnp.concatenate([rows[head * HEAD : (head + 1) * HEAD], gap], axis=1)
-        blank = jnp.zeros_like(part)
-        block = jnp.concatenate(
-            [
-                jnp.concatenate([part, blank], axis=1),
-                jnp.concatenate([blank, part], axis=1),
-                jnp.zeros((LANES - 2 * HEAD, 768), f32),
-            ],
-            axis=0,
-        )
-        spread_out[head * LANES : (head + 1) * LANES, :] = block.astype(bf16)
 
 
 def widen_kernel(w_in, b_in, turned_out):
@@ -593,8 +620,8 @@
     kept = None
     for n in range(10):
         moment = dot(inner_turned, cond[n]) if n < 9 else dot(branch_turned, cond[4])
-        one = pltpu.roll(moment[:, LANES:], n, 1)
-        ones = jnp.where(lane == 64 + n, one, ones)
+        one = pltpu.roll(moment[:, LANES:], 3 * n, 1)
+        ones = jnp.where((lane >= 64 + 3 * n) & (lane < 67 + 3 * n), one, ones)
         if n % 2 == 0:
             kept = moment[:, :CIN]
             continue
@@ -610,28 +637,26 @@
 
 def weights_kernel(
     place, mine, theirs, w_turned, w_conv, win_out, bin_out, wconv_out, bconv_out, wout_out,
-    bout_out, total, taps, sems,
+    bout_out, taps, sems,
 ):
     here = place[1]
-    total[here] = mine[...]
-    total[1 - here] = theirs[...]
-
-    def take(half, at):
-        return jnp.concatenate(
-            [total[half, at + C * t : at + C * (t + 1), :] for t in range(3)], axis=1
-        )
-
-    last = take(1, 6 * C).astype(f32)
-    ones = last[:, 2 * LANES :]
+
+    def tile(half, n):
+        rows = slice(C * n, C * (n + 1))
+        return jnp.where(here == half, mine[rows, :], theirs[rows, :]).astype(f32)
+
+    ones = tile(1, 8)
     lane = lane_of((C, LANES))
+    low = lane < 64
 
     def moment_of(n):
         pair = n // 2
-        both = take(pair // 3, 3 * C * (pair % 3)).astype(f32)
-        both = both[:, CIN * (n % 2) : CIN * (n % 2 + 1)]
-        one = jnp.sum(jnp.where(lane == 64 + n, ones, 0.0), axis=1, keepdims=True)
-        spare = lane_of((C, WIDE - CIN))
-        return jnp.concatenate([both, jnp.where(spare < 3, one, 0.0)], axis=1).astype(bf16)
+        first, middle, last = [tile(pair // 3, 3 * (pair % 3) + t) for t in range(3)]
+        if n % 2:
+            middle, last = pltpu.roll(middle, 64, 1), pltpu.roll(last, 64, 1)
+            first, middle = jnp.where(low, middle, last), last
+        one = jnp.where(lane < 67, pltpu.roll(ones, LANES - 3 * n, 1) if n else ones, 0.0)
+        return jnp.concatenate([first, jnp.where(low, middle, one)], axis=1).astype(bf16)
 
     grad_in = jnp.zeros((C, WIDE), f32)
     copies = []
@@ -642,14 +667,14 @@
         copy.start()
         copies.append(copy)
         grad_in += dot(w_conv[n], moment)
-        if n == 4:
-            bconv_out[...] = jnp.transpose(moment.astype(f32))[CIN]
-    moment = jnp.transpose(moment_of(9).astype(f32))
-    grad_in = jnp.transpose(grad_in) + moment
+    last = jnp.concatenate([tile(1, 6), tile(1, 7), ones], axis=1)
+    last = jnp.transpose(last)
+    wout_out[...] = last[:C]
+    bconv_out[...] = last[C + 12]
+    bout_out[...] = last[C + 27]
+    grad_in = jnp.transpose(grad_in + moment_of(9).astype(f32))
     win_out[...] = grad_in[:CIN]
     bin_out[...] = grad_in[CIN]
-    bout_out[...] = moment[CIN]
-    wout_out[...] = jnp.transpose(last)[:C]
     for copy in copies:
         copy.wait()
 
@@ -718,6 +743,17 @@
 
     own = across(rows.reshape(CHIPS, PART, LANES)).reshape(HALF, LANES)
     other = swap(own)
+    _, attn_weight = after(own, w_attn_out)
+    w_cross_query_wide, w_cross_out_wide, w_attn_spread = call(
+        form_kernel,
+        (out(C, 2 * WIDE), out(2 * WIDE, C), out(HEADS * LANES, 768)),
+        (w_cross_query, w_cross_out, attn_weight),
+        "form",
+        fetch=(2, 0, 1),
+        store=(0, 1),
+        near=(2,),
+    )
+    own, w_attn_spread = after(own, w_attn_spread)
     packed, full, probs = call(
         attend_kernel,
         (
@@ -744,17 +780,15 @@
         far=(4,),
     )
 
-    packed, text, attn_weight = after(packed, text_states, w_attn_out)
+    packed, text = after(packed, text_states)
     text_keys, text_values = call(
         text_kernel,
-        (out(ITEMS, TEXT, C), out(ITEMS, TEXT, C)),
+        (out(ITEMS, TEXT, 2 * WIDE), out(ITEMS, TEXT, 2 * WIDE)),
         (text.transpose(1, 0, 2).reshape(-1, text.shape[2]), w_cross_key.T, w_cross_value.T),
         "text",
-        fetch=(0, 1, 2),
+        scratch=[pltpu.VMEM((2 * WIDE, text.shape[2]), bf16)] * 2,
+        fetch=(1, 2, 0),
         store=(0, 1),
-    )
-    (w_attn_spread,) = bring(
-        [], "spread", spread_kernel, (out(HEADS * LANES, 768),), (attn_weight,)
     )
     heads_in = across(packed).reshape(ITEMS, HEADS, PART // 2, LANES)
     result, grad_first, heads_out = call(
@@ -762,8 +796,8 @@
         (out(CELLS, C), out(CELLS, C, dtype=f32), out(ITEMS, HEADS, PART // 2, LANES)),
         (
             text_lengths, heads_in, mixed, cotangent.reshape(CELLS, C), text_keys, text_values,
-            w_attn_spread, b_attn_out, w_cross_query, w_cross_out, b_cross_out, w_ff_in, b_ff_in,
-            w_ff_out.T, b_ff_out,
+            w_attn_spread, b_attn_out, w_cross_query_wide, w_cross_out_wide, b_cross_out,
+            w_ff_in, b_ff_in, w_ff_out.T, b_ff_out,
         ),
         "middle",
         scalars=1,
@@ -855,7 +889,6 @@
         "weights",
         scalars=1,
         scratch=[
-            pltpu.VMEM((2, SUM_ROWS, LANES), bf16),
             pltpu.VMEM((9, C, C), f32),
             pltpu.SemaphoreType.DMA((9,)),
         ],

time: 205 us -> 202 us (0.985)
    pallas_call x7 -> x8, Pallas kernels: 62.7 us -> 61.8 us  [call(): pl.pallas_call(body, out_shape=tuple((made_as(i, made) for i, made in enu...]
    pallas_call x5 -> x4, Pallas kernels: 6.49 us -> 6.38 us  [bring(): pl.pallas_call(body, out_shape=tuple((pltpu.VMEM(x.shape, x.dtype) for x...]
  transfers between devices with their start and end apart: 11 -> 11, of which waited for: 8 -> 7; matrix products, arithmetic and copies ran while one was open for 1% -> 1% of each run, Pallas kernels for 7% -> 8%
where the time goes in v1:
time: 202 us; the launch traced here: 201 us
  Pallas kernels  68.1 us (34%)
  blocking collectives  64.1 us (32%)
  starting transfers between devices  38.1 us (19%)
  waiting for transfers between devices  26.5 us (13%)
  local copies, waits for them, and re-layouts  2.13 us (1%)
    all_to_all x3, blocking collectives, across(): return lax.all_to_all(blocks, ACROSS, 0, 0, tiled=True)  64.1 us
    pallas_call x8, Pallas kernels, call(): pl.pallas_call(body, out_shape=tuple((made_as(i, made) for i, made in enu...  61.8 us
    all_to_all x3, waiting for transfers between devices, across(): return lax.all_to_all(blocks, ACROSS, 0, 0, tiled=True)  21.8 us
    all_to_all x3, starting transfers between devices, across(): return lax.all_to_all(blocks, ACROSS, 0, 0, tiled=True)  17.2 us
    ppermute x4, starting transfers between devices, swap(): return lax.ppermute(array, 'c', [(0, 1), (1, 0)])  8.14 us
    pallas_call x4, Pallas kernels, bring(): pl.pallas_call(body, out_shape=tuple((pltpu.VMEM(x.shape, x.dtype) for x...  6.38 us
    ppermute x1, starting transfers between devices, per_device(): left = lax.ppermute(edge(COLS - 1), ('x', 'c'), right_way)  4.84 us
    ppermute x1, starting transfers between devices, per_device(): top = lax.ppermute(condition[:, ROWS - 1:], 'sp', down)  4.66 us
  transfers between devices with their start and end apart: 11, of which 7 were waited for; matrix products, arithmetic and copies ran while one was open for 1% of the time, Pallas kernels for 8%

profile of v1, /device:TPU:1, one launch (start us, length us, event | category | flops | bytes accessed | tf_op | source)
XLA Modules:
  0.0 201.4 jit_solution(17143115308850601608)
XLA Ops:
  2.7 4.7 %collective-permute-start = (bf16[8,1,8,192]{3,2,1,0:T(8,128)(2,1)S(1)}, bf16[8,1,8,192]{3,2,1,0:T(8,128)(2,1)S(1)}, u32[]{:S(2)}, u32[]{:S(2)}) collective-permute-start(bf16[8,1,8,192]{3,2,1,0:T(8,128)(2,1)S(1)} %get-tuple-element.131), channel_id=1, source_target_pairs={{0,8},{8,16},{16,24},{24,32},{32,40},{40,48},{48,56},{56,64},{64,7... | collective-permute-start | bytes 73736 | tf_op jit(solution)/shard_map/ppermute | solution.py:700
  8.7 4.8 %collective-permute-start.2 = (bf16[48,192]{1,0:T(8,128)(2,1)S(1)}, bf16[48,192]{1,0:T(8,128)(2,1)S(1)}, u32[]{:S(2)}, u32[]{:S(2)}) collective-permute-start(bf16[48,192]{1,0:T(8,128)(2,1)S(1)} %reshape.73), channel_id=1, source_target_pairs={{0,1},{1,2},{2,3},{3,4},{4,5},{5,6},{6,7},{8,9},{9,10},{10,11},{11... | collective-permute-start | bytes 55304 | tf_op jit(solution)/shard_map/ppermute | solution.py:708
  13.5 1.9 collective-permute-start.3
  15.5 2.1 %load_adapter.1 = (bf16[192,320]{1,0:T(8,128)(2,1)S(1)}, f32[320]{0:T(512)S(1)}, bf16[9,320,320]{2,1,0:T(8,128)(2,1)S(1)}, bf16[8,4,8,192]{3,2,1,0:T(8,128)(2,1)...) custom-call(bf16[192,320]{1,0:T(8,128)(2,1)} %refs_1_.6, ...), custom_call_target="tpu_custom_call" | custom-call | tf_op jit(solution)/shard_map/load_adapter/pallas_call | solution.py:167
  18.7 4.6 %adapter.1 = (bf16[8,8,32,128]{3,2,1,0:T(8,128)(2,1)S(1)}, f32[256,320]{1,0:T(8,128)}, bf16[256,320]{1,0:T(8,128)(2,1)}, f32[256,320]{1,0:T(8,128)}, bf16[9,256,256]{2,1,0:T(8,128)(2,1)}) custom-call(s32[3]{0:T(128)S(1)} %pad_add_fusion.refs_0_, s32[8]{0:T(128)S(1)} %copy-done.5, bf16[8,4,8,192]{3,2,1,0:T(8,128)(2,1)S(1)} %get-tuple-element.69.refs_2_, ...), custom_call_target="tpu_custom_call" | custom-call | tf_op jit(solution)/shard_map/adapter/pallas_call | solution.py:132
  23.3 26.1 %all_to_all.30 = bf16[64,32,128]{2,1,0:T(8,128)(2,1)S(1)} all-to-all(bf16[64,32,128]{2,1,0:T(8,128)(2,1)S(1)} %bitcast.47), channel_id=1, replica_groups=mesh['sp'=16,'x'=4,'c'=2] {'sp','x'}, dimensions={0} | all-to-all | bytes 1048576 | tf_op jit(solution)/shard_map/all_to_all | solution.py:687
  50.9 2.1 %form.1 = (bf16[320,512]{1,0:T(8,128)(2,1)}, bf16[512,320]{1,0:T(8,128)(2,1)}, bf16[1024,768]{1,0:T(8,128)(2,1)S(1)}) custom-call(bf16[320,320]{1,0:T(8,128)(2,1)} %refs_0_.4, bf16[320,320]{1,0:T(8,128)(2,1)} %refs_1_.5, bf16[320,320]{1,0:T(8,128)(2,1)} %refs_2_.1), custom_call_target="tpu_custom_call" | custom-call | tf_op jit(solution)/shard_map/form/pallas_call | solution.py:132
  53.0 11.9 %attend.1 = (bf16[64,16,128]{2,1,0:T(8,128)(2,1)}, f32[2048,128]{1,0:T(8,128)}, bf16[2048,4096]{1,0:T(8,128)(2,1)}) custom-call(bf16[2048,128]{1,0:T(8,128)(2,1)S(1)} %bitcast.41, bf16[2048,128]{1,0:T(8,128)(2,1)S(1)} %collective-permute-done.4.refs_1_), custom_call_target="tpu_custom_call" | custom-call | tf_op jit(solution)/shard_map/attend/pallas_call | solution.py:132
  64.9 4.8 %all-to-all-start.1 = ((bf16[64,16,128]{2,1,0:T(8,128)(2,1)}), bf16[64,16,128]{2,1,0:T(8,128)(2,1)S(1)}, u32[]{:S(2)}, u32[]{:S(2)}) async-start(bf16[64,16,128]{2,1,0:T(8,128)(2,1)} %get-tuple-element.86), calls=%async_computation.1 | async-start | bytes 524288 | tf_op jit(solution)/shard_map/all_to_all | solution.py:687
  69.7 8.1 %text.1 = (bf16[8,80,512]{2,1,0:T(8,128)(2,1)}, bf16[8,80,512]{2,1,0:T(8,128)(2,1)}) custom-call(bf16[616,768]{1,0:T(8,128)(2,1)} %bitcast.51, bf16[320,768]{1,0:T(8,128)(2,1)} %bitcast.53, bf16[320,768]{1,0:T(8,128)(2,1)} %bitcast.54), custom_call_target="tpu_custom_call" | custom-call | tf_op jit(solution)/shard_map/text/pallas_call | solution.py:132
  77.8 2.1 %all-to-all-done.1 = bf16[64,16,128]{2,1,0:T(8,128)(2,1)S(1)} async-done(((bf16[64,16,128]{2,1,0:T(8,128)(2,1)}), bf16[64,16,128]{2,1,0:T(8,128)(2,1)S(1)}, u32[]{:S(2)}, u32[]{:S(2)}) %all-to-all-start.1) | async-done | bytes 262176 | tf_op jit(solution)/shard_map/all_to_all | solution.py:687
  79.9 12.9 %middle.1 = (bf16[256,320]{1,0:T(8,128)(2,1)}, f32[256,320]{1,0:T(8,128)}, bf16[8,8,16,128]{3,2,1,0:T(8,128)(2,1)}) custom-call(s32[8]{0:T(128)S(1)} %copy-done.6, bf16[8,8,16,128]{3,2,1,0:T(8,128)(2,1)S(1)} %bitcast.46, f32[256,320]{1,0:T(8,128)} %get-tuple-element.87.refs_2_.refs_0_, bf16[256,320]{1,0:T(8,128)(2,1)} %bitcast.57, ...), custom_call_target="tpu_custom_call" | custom-call | tf_op jit(solution)/shard_map/middle/pallas_call | solution.py:132
  92.8 7.8 %all-to-all-start.2 = ((bf16[64,16,128]{2,1,0:T(8,128)(2,1)}), bf16[64,16,128]{2,1,0:T(8,128)(2,1)S(1)}, u32[]{:S(2)}, u32[]{:S(2)}) async-start(bf16[64,16,128]{2,1,0:T(8,128)(2,1)} %bitcast.55), calls=%async_computation.2 | async-start | bytes 524288 | tf_op jit(solution)/shard_map/all_to_all | solution.py:687
  101.2 9.1 %all-to-all-done.2.refs_3_ = bf16[64,16,128]{2,1,0:T(8,128)(2,1)S(1)} async-done(((bf16[64,16,128]{2,1,0:T(8,128)(2,1)}), bf16[64,16,128]{2,1,0:T(8,128)(2,1)S(1)}, u32[]{:S(2)}, u32[]{:S(2)}) %all-to-all-start.2) | async-done | bytes 262176 | tf_op jit(solution)/shard_map/all_to_all | solution.py:687
  110.3 15.8 %attend_back.1 = (f32[2048,128]{1,0:T(8,128)S(1)}, bf16[2048,128]{1,0:T(8,128)(2,1)S(1)}) custom-call(bf16[128,4096]{1,0:T(8,128)(2,1)S(1)} %get-tuple-element.97.refs_0_, bf16[128,2048]{1,0:T(8,128)(2,1)S(1)} %get-tuple-element.98.refs_1_, f32[2048,128]{1,0:T(8,128)} %get-tuple-element.99.refs_2_, bf16[64,16,128]{2,1,0:T(8,128)(2,1)S(1)} %all-to-all-done.2.refs_3_, ...), custom_call_target="tpu_custom_call" | custom-call | tf_op jit(solution)/shard_map/attend_back/pallas_call | solution.py:132
  130.2 4.6 %all-to-all-start.3 = ((bf16[64,32,128]{2,1,0:T(8,128)(2,1)}), bf16[64,32,128]{2,1,0:T(8,128)(2,1)S(1)}, u32[]{:S(2)}, u32[]{:S(2)}) async-start(bf16[64,32,128]{2,1,0:T(8,128)(2,1)} %bitcast.18), calls=%async_computation.3 | async-start | bytes 1048576 | tf_op jit(solution)/shard_map/all_to_all | solution.py:687
  134.9 2.0 load_finish.1
  136.8 10.5 %all-to-all-done.3 = bf16[64,32,128]{2,1,0:T(8,128)(2,1)S(1)} async-done(((bf16[64,32,128]{2,1,0:T(8,128)(2,1)}), bf16[64,32,128]{2,1,0:T(8,128)(2,1)S(1)}, u32[]{:S(2)}, u32[]{:S(2)}) %all-to-all-start.3) | async-done | bytes 524320 | tf_op jit(solution)/shard_map/all_to_all | solution.py:687
  147.4 2.6 %finish.1 = (f32[256,320]{1,0:T(8,128)}, bf16[2,3072,128]{2,1,0:T(8,128)(2,1)S(1)}) custom-call(s32[3]{0:T(128)S(1)} %pad_add_fusion.refs_0_, bf16[8,8,32,128]{3,2,1,0:T(8,128)(2,1)S(1)} %bitcast.45, bf16[320,1024]{1,0:T(8,128)(2,1)S(1)} %get-tuple-element.109.refs_2_, f32[256,320]{1,0:T(8,128)S(1)} %get-tuple-element.110.refs_3_, ...), custom_call_target="tpu_custom_call" | custom-call | tf_op jit(solution)/shard_map/finish/pallas_call | solution.py:132
  151.9 1.9 collective-permute-done.6
  154.0 19.7 %all_to_all.31 = bf16[64,48,128]{2,1,0:T(8,128)(2,1)S(1)} all-to-all(bf16[64,48,128]{2,1,0:T(8,128)(2,1)S(1)} %bitcast.50), channel_id=1, replica_groups=mesh['sp'=16,'x'=4,'c'=2] {'sp','x'}, dimensions={0} | all-to-all | bytes 1572864 | tf_op jit(solution)/shard_map/all_to_all | solution.py:687
  173.9 18.3 %all_to_all.32 = bf16[64,48,128]{2,1,0:T(8,128)(2,1)S(1)} all-to-all(bf16[64,48,128]{2,1,0:T(8,128)(2,1)S(1)} %broadcast_in_dim.2), channel_id=1, replica_groups=mesh['sp'=16,'x'=4,'c'=2] {'sp','x'}, dimensions={0} | all-to-all | bytes 1572864 | tf_op jit(solution)/shard_map/all_to_all | solution.py:687
  192.2 3.1 %collective-permute-start.7 = (bf16[3072,128]{1,0:T(8,128)(2,1)S(1)}, bf16[3072,128]{1,0:T(8,128)(2,1)S(1)}, u32[]{:S(2)}, u32[]{:S(2)}) collective-permute-start(bf16[3072,128]{1,0:T(8,128)(2,1)S(1)} %bitcast.43), channel_id=1, source_target_pairs={{0,1},{1,0},{2,3},{3,2},{4,5},{5,4},{6,7},{7,6},{8,9},{9,8},{10,11... | collective-permute-start | bytes 2359304 | tf_op jit(solution)/shard_map/ppermute | solution.py:683
  197.3 3.9 %weights.1 = (f32[192,320]{1,0:T(8,128)}, f32[320]{0:T(512)}, f32[9,320,320]{2,1,0:T(8,128)}, f32[320]{0:T(512)}, f32[320,320]{1,0:T(8,128)}, /*index=5*/f32[320]{0:T(512)}) custom-call(s32[3]{0:T(128)S(1)} %pad_add_fusion.refs_0_, bf16[3072,128]{1,0:T(8,128)(2,1)S(1)} %bitcast.44, bf16[3072,128]{1,0:T(8,128)(2,1)S(1)} %collective-permute-done.7.refs_2_, ...), custom_call_target="tpu_custom_call" | custom-call | tf_op jit(solution)/shard_map/weights/pallas_call | solution.py:132
  (46 shorter events, 14.8 us)
Async XLA Ops:
  1.4 7.0 %collective-permute-start.1 = (bf16[8,1,8,192]{3,2,1,0:T(8,128)(2,1)S(1)}, bf16[8,1,8,192]{3,2,1,0:T(8,128)(2,1)S(1)}, u32[]{:S(2)}, u32[]{:S(2)}) collective-permute-start(bf16[8,1,8,192]{3,2,1,0:T(8,128)(2,1)S(1)} %get-tuple-element.130), channel_id=1, source_target_pairs={{8,0},{16,8},{24,16},{32,24},{40,32},{48,40},{56,48},{64,56},{72,6... | collective-permute-start | bytes 73736 | tf_op jit(solution)/shard_map/ppermute | solution.py:701
  2.7 5.8 %collective-permute-start = (bf16[8,1,8,192]{3,2,1,0:T(8,128)(2,1)S(1)}, bf16[8,1,8,192]{3,2,1,0:T(8,128)(2,1)S(1)}, u32[]{:S(2)}, u32[]{:S(2)}) collective-permute-start(bf16[8,1,8,192]{3,2,1,0:T(8,128)(2,1)S(1)} %get-tuple-element.131), channel_id=1, source_target_pairs={{0,8},{8,16},{16,24},{24,32},{32,40},{40,48},{48,56},{56,64},{64,7... | collective-permute-start | bytes 73736 | tf_op jit(solution)/shard_map/ppermute | solution.py:700
  8.7 9.0 %collective-permute-start.2 = (bf16[48,192]{1,0:T(8,128)(2,1)S(1)}, bf16[48,192]{1,0:T(8,128)(2,1)S(1)}, u32[]{:S(2)}, u32[]{:S(2)}) collective-permute-start(bf16[48,192]{1,0:T(8,128)(2,1)S(1)} %reshape.73), channel_id=1, source_target_pairs={{0,1},{1,2},{2,3},{3,4},{4,5},{5,6},{6,7},{8,9},{9,10},{10,11},{11... | collective-permute-start | bytes 55304 | tf_op jit(solution)/shard_map/ppermute | solution.py:708
  13.5 5.1 %collective-permute-start.3 = (bf16[48,192]{1,0:T(8,128)(2,1)S(1)}, bf16[48,192]{1,0:T(8,128)(2,1)S(1)}, u32[]{:S(2)}, u32[]{:S(2)}) collective-permute-start(bf16[48,192]{1,0:T(8,128)(2,1)S(1)} %reshape.74), channel_id=1, source_target_pairs={{1,0},{2,1},{3,2},{4,3},{5,4},{6,5},{7,6},{9,8},{10,9},{11,10},{12... | collective-permute-start | bytes 55304 | tf_op jit(solution)/shard_map/ppermute | solution.py:709
  15.5 3.1 %copy-start.5 = (s32[8]{0:T(128)S(1)}, s32[8]{0:T(128)}, u32[]{:S(2)}) copy-start(s32[8]{0:T(128)} %refs_1_.4) | copy-start | bytes 100
  49.4 3.6 %collective-permute-start.4 = (bf16[2048,128]{1,0:T(8,128)(2,1)S(1)}, bf16[2048,128]{1,0:T(8,128)(2,1)S(1)}, u32[]{:S(2)}, u32[]{:S(2)}) collective-permute-start(bf16[2048,128]{1,0:T(8,128)(2,1)S(1)} %bitcast.40), channel_id=1, source_target_pairs={{0,1},{1,0},{2,3},{3,2},{4,5},{5,4},{6,7},{7,6},{8,9},{9,8},{10,11... | collective-permute-start | bytes 1572872 | tf_op jit(solution)/shard_map/ppermute | solution.py:683
  53.0 27.0 %copy-start.6 = (s32[8]{0:T(128)S(1)}, s32[8]{0:T(128)}, u32[]{:S(2)}) copy-start(s32[8]{0:T(128)} %refs_0_.5) | copy-start | bytes 100
  64.9 15.0 %all-to-all-start.1 = ((bf16[64,16,128]{2,1,0:T(8,128)(2,1)}), bf16[64,16,128]{2,1,0:T(8,128)(2,1)S(1)}, u32[]{:S(2)}, u32[]{:S(2)}) async-start(bf16[64,16,128]{2,1,0:T(8,128)(2,1)} %get-tuple-element.86), calls=%async_computation.1 | async-start | bytes 524288 | tf_op jit(solution)/shard_map/all_to_all | solution.py:687
  92.8 17.6 %all-to-all-start.2 = ((bf16[64,16,128]{2,1,0:T(8,128)(2,1)}), bf16[64,16,128]{2,1,0:T(8,128)(2,1)S(1)}, u32[]{:S(2)}, u32[]{:S(2)}) async-start(bf16[64,16,128]{2,1,0:T(8,128)(2,1)} %bitcast.55), calls=%async_computation.2 | async-start | bytes 524288 | tf_op jit(solution)/shard_map/all_to_all | solution.py:687
  126.1 3.2 %collective-permute-start.5 = (bf16[2048,128]{1,0:T(8,128)(2,1)S(1)}, bf16[2048,128]{1,0:T(8,128)(2,1)S(1)}, u32[]{:S(2)}, u32[]{:S(2)}) collective-permute-start(bf16[2048,128]{1,0:T(8,128)(2,1)S(1)} %get-tuple-element.103), channel_id=1, source_target_pairs={{0,1},{1,0},{2,3},{3,2},{4,5},{5,4},{6,7},{7,6},{8,9},{9,8},{10,11... | collective-permute-start | bytes 1572872 | tf_op jit(solution)/shard_map/ppermute | solution.py:683
  129.3 5.5 %copy-start = (bf16[320,320]{1,0:T(8,128)(2,1)S(1)}, bf16[320,320]{1,0:T(8,128)(2,1)}, u32[]{:S(2)}) copy-start(bf16[320,320]{1,0:T(8,128)(2,1)} %refs_5_.2) | copy-start | bytes 614404
  129.3 5.6 %copy-start.1 = (bf16[320,320]{1,0:T(8,128)(2,1)S(1)}, bf16[320,320]{1,0:T(8,128)(2,1)}, u32[]{:S(2)}) copy-start(bf16[320,320]{1,0:T(8,128)(2,1)} %refs_6_.3) | copy-start | bytes 614404
  129.3 5.6 %copy-start.2 = (bf16[320,320]{1,0:T(8,128)(2,1)S(1)}, bf16[320,320]{1,0:T(8,128)(2,1)}, u32[]{:S(2)}) copy-start(bf16[320,320]{1,0:T(8,128)(2,1)} %refs_7_.5) | copy-start | bytes 614404
  130.2 17.1 %all-to-all-start.3 = ((bf16[64,32,128]{2,1,0:T(8,128)(2,1)}), bf16[64,32,128]{2,1,0:T(8,128)(2,1)S(1)}, u32[]{:S(2)}, u32[]{:S(2)}) async-start(bf16[64,32,128]{2,1,0:T(8,128)(2,1)} %bitcast.18), calls=%async_computation.3 | async-start | bytes 1048576 | tf_op jit(solution)/shard_map/all_to_all | solution.py:687
  150.0 3.8 %collective-permute-start.6 = (bf16[3072,128]{1,0:T(8,128)(2,1)S(1)}, bf16[3072,128]{1,0:T(8,128)(2,1)S(1)}, u32[]{:S(2)}, u32[]{:S(2)}) collective-permute-start(bf16[3072,128]{1,0:T(8,128)(2,1)S(1)} %slice_bitcast_fusion), channel_id=1, source_target_pairs={{0,1},{1,0},{2,3},{3,2},{4,5},{5,4},{6,7},{7,6},{8,9},{9,8},{10,11... | collective-permute-start | bytes 2359304 | tf_op jit(solution)/shard_map/ppermute | solution.py:683
  173.7 21.7 %copy-start.3 = (bf16[192,320]{1,0:T(8,128)(2,1)S(1)}, bf16[192,320]{1,0:T(8,128)(2,1)}, u32[]{:S(2)}) copy-start(bf16[192,320]{1,0:T(8,128)(2,1)} %refs_1_.6) | copy-start | bytes 368644
  173.7 21.7 %copy-start.4 = (f32[320]{0:T(512)S(1)}, f32[320]{0:T(512)}, u32[]{:S(2)}) copy-start(f32[320]{0:T(512)} %refs_2_.3) | copy-start | bytes 3844
  192.2 5.1 %collective-permute-start.7 = (bf16[3072,128]{1,0:T(8,128)(2,1)S(1)}, bf16[3072,128]{1,0:T(8,128)(2,1)S(1)}, u32[]{:S(2)}, u32[]{:S(2)}) collective-permute-start(bf16[3072,128]{1,0:T(8,128)(2,1)S(1)} %bitcast.43), channel_id=1, source_target_pairs={{0,1},{1,0},{2,3},{3,2},{4,5},{5,4},{6,7},{7,6},{8,9},{9,8},{10,11... | collective-permute-start | bytes 2359304 | tf_op jit(solution)/shard_map/ppermute | solution.py:683

commit v2 on v1

--- a/solution.py
+++ b/solution.py
@@ -317,16 +317,18 @@
 
 
 def attend_kernel(
-    own, other, packed_out, full_out, probs_out,
-    scores_a, scores_b, probs_a, probs_b, turned_a, turned_b, keys_turned, query, output, sems,
+    own, other, packed_out, full_out, probs_out, keys_out, query_out,
+    scores_a, scores_b, probs_a, probs_b, turned_a, turned_b, output, sems,
 ):
     count = HALF // BLOCK
+    keys_turned, query = keys_out.buffer, query_out.buffer
     keys_turned[:, :HALF] = jnp.transpose(own[...])
     keys_turned[:, HALF:] = jnp.transpose(other[...])
+    keys_out.start()
     lane = lane_of((HALF, LANES))
     rows = pltpu.roll(own[...].astype(f32), KEY, 1)
     rows = jnp.where((lane >= KEY) & (lane < VALUE), rows, jnp.where(lane == MASK, 1.0, 0.0))
-    query[...] = jnp.transpose(rows.astype(bf16))
+    query_out[...] = jnp.transpose(rows.astype(bf16))
     chunks = [(ref, at) for ref in (own, other) for at in range(0, HALF, STEP)]
 
     def columns(b):
@@ -494,15 +496,6 @@
 WIDE_STEP = 1024
 
 
-def turn_kernel(own, other, keys_out, query_out):
-    keys_out[:, :HALF] = jnp.transpose(own[...])
-    keys_out[:, HALF:] = jnp.transpose(other[...])
-    lane = lane_of((HALF, LANES))
-    query = pltpu.roll(own[...].astype(f32), KEY, 1)
-    query = jnp.where((lane >= KEY) & (lane < VALUE), query, 0.0).astype(bf16)
-    query_out[...] = jnp.transpose(query)
-
-
 def attend_back_kernel(
     keys_turned, query_turned, full, packed, probs_in, own_out, other_out,
     grads, left, sums, scores, probs_a, probs_b, sems,
@@ -736,12 +729,23 @@
         scalars=2,
         scratch=[pltpu.VMEM((WIDE, C), bf16)],
         vmem=24,
-        store=(1, 2, 3, 4),
-        near=(0,),
+        store=(0, 1, 2, 3, 4),
         held=(2,) + tuple(range(7, 17)),
     )
 
+    rows, text = after(rows, text_states)
+    text_keys, text_values = call(
+        text_kernel,
+        (out(ITEMS, TEXT, 2 * WIDE), out(ITEMS, TEXT, 2 * WIDE)),
+        (text.transpose(1, 0, 2).reshape(-1, text.shape[2]), w_cross_key.T, w_cross_value.T),
+        "text",
+        scratch=[pltpu.VMEM((2 * WIDE, text.shape[2]), bf16)] * 2,
+        fetch=(1, 2, 0),
+        store=(0, 1),
+    )
     own = across(rows.reshape(CHIPS, PART, LANES)).reshape(HALF, LANES)
+    own, text_keys = after(own, text_keys)
+
     other = swap(own)
     _, attn_weight = after(own, w_attn_out)
     w_cross_query_wide, w_cross_out_wide, w_attn_spread = call(
@@ -754,12 +758,14 @@
         near=(2,),
     )
     own, w_attn_spread = after(own, w_attn_spread)
-    packed, full, probs = call(
+    packed, full, probs, keys_turned, query_turned = call(
         attend_kernel,
         (
             out(CHIPS, PART // 2, LANES),
             out(HALF, LANES, dtype=f32),
             out(HALF, 2 * HALF),
+            out(LANES, 2 * HALF),
+            out(LANES, HALF),
         ),
         (own, other),
         "attend",
@@ -770,26 +776,15 @@
             pltpu.VMEM((2 * HALF, BLOCK), bf16),
             pltpu.VMEM((BLOCK, 2 * HALF), bf16),
             pltpu.VMEM((BLOCK, 2 * HALF), bf16),
-            pltpu.VMEM((LANES, 2 * HALF), bf16),
-            pltpu.VMEM((LANES, HALF), bf16),
             pltpu.VMEM((LANES, HALF), f32),
             pltpu.SemaphoreType.DMA((2,)),
         ],
         vmem=32,
-        store=(0, 1),
+        store=(1, 3, 4),
+        near=(0,),
         far=(4,),
     )
 
-    packed, text = after(packed, text_states)
-    text_keys, text_values = call(
-        text_kernel,
-        (out(ITEMS, TEXT, 2 * WIDE), out(ITEMS, TEXT, 2 * WIDE)),
-        (text.transpose(1, 0, 2).reshape(-1, text.shape[2]), w_cross_key.T, w_cross_value.T),
-        "text",
-        scratch=[pltpu.VMEM((2 * WIDE, text.shape[2]), bf16)] * 2,
-        fetch=(1, 2, 0),
-        store=(0, 1),
-    )
     heads_in = across(packed).reshape(ITEMS, HEADS, PART // 2, LANES)
     result, grad_first, heads_out = call(
         middle_kernel,
@@ -804,18 +799,11 @@
         scratch=[pltpu.VMEM((ITEMS, HEADS * PART, TEXT), f32)],
         vmem=32,
         fetch=(2, 7, 8, 4, 5, 9, 10, 3, 11, 12, 13, 14),
-        store=(0, 1, 2),
+        store=(0, 1),
+        near=(2,),
         held=(6,),
     )
 
-    heads_out, own_again = after(heads_out, own)
-    keys_turned, query_turned = bring(
-        [],
-        "turn",
-        turn_kernel,
-        (out(LANES, 2 * HALF), out(LANES, HALF)),
-        (own_again, other),
-    )
     grads_in = across(heads_out.reshape(CHIPS, PART // 2, LANES))
     own_grads, other_grads = call(
         attend_back_kernel,
@@ -833,33 +821,31 @@
         ],
         vmem=36,
         near=(0, 1),
-        held=(0, 1),
-        fetch=(2,),
         far=(4,),
     )
-    row_grads = (own_grads + swap(other_grads).astype(f32)).astype(bf16)
-
-    row_grads, query_weight = after(row_grads, w_query)
-    mixed_here, grad_here, w_out_here, slope_here, smooth_here, w_joined = bring(
-        [mixed, grad_first, w_out, slope, smooth],
-        "load_finish",
+
+    _, query_weight = after(other_grads, w_query)
+    (w_joined,) = call(
         join_kernel,
         (out(C, HEADS * LANES),),
         (query_weight, w_key, w_value),
-    )
+        "join",
+        fetch=(0, 1, 2),
+        near=(0,),
+    )
+    own_grads, w_joined = after(own_grads, w_joined)
+    row_grads = (own_grads + swap(other_grads).astype(f32)).astype(bf16)
     row_grads = across(row_grads.reshape(CHIPS, PART, LANES))
     latent_grad, parts = call(
         finish_kernel,
         (out(CELLS, C, dtype=f32), out(2, SUM_ROWS, LANES)),
         (
-            place, row_grads.reshape(ITEMS, HEADS, PART, LANES), w_joined, mixed_here, grad_here,
-            slope_here, smooth_here, cond, w_out_here,
+            place, row_grads.reshape(ITEMS, HEADS, PART, LANES), w_joined, mixed, grad_first,
+            slope, smooth, cond, w_out,
         ),
         "finish",
         scalars=1,
         store=(0,),
-        fetch=(7,),
-        held=(2, 3, 4, 5, 6, 8),
     )
 
     shares = (parts[0].astype(f32) + swap(parts[1]).astype(f32)).astype(bf16)

time: 202 us -> 199 us (0.985)
  blocking collectives: 64.1 us -> 83.4 us
  waiting for transfers between devices: 26.5 us -> 7.9 us
  starting transfers between devices: 38.1 us -> 35.2 us
    all_to_all x3 -> x5, blocking collectives: 64.1 us -> 83.4 us  [across(): return lax.all_to_all(blocks, ACROSS, 0, 0, tiled=True)]
    all_to_all x3 -> x1, waiting for transfers between devices: 21.8 us -> 4.75 us  [across(): return lax.all_to_all(blocks, ACROSS, 0, 0, tiled=True)]
    all_to_all x3 -> x1, starting transfers between devices: 17.2 us -> 13.5 us  [across(): return lax.all_to_all(blocks, ACROSS, 0, 0, tiled=True)]
    pallas_call x4 -> x2, Pallas kernels: 6.38 us -> 3.79 us  [bring(): pl.pallas_call(body, out_shape=tuple((pltpu.VMEM(x.shape, x.dtype) for x...]
    pallas_call x8 -> x9, Pallas kernels: 61.8 us -> 64.2 us  [call(): pl.pallas_call(body, out_shape=tuple((made_as(i, made) for i, made in enu...]
  transfers between devices with their start and end apart: 11 -> 9, of which waited for: 7 -> 4; matrix products, arithmetic and copies ran while one was open for 1% -> 1% of each run, Pallas kernels for 8% -> 8%
where the time goes in v2:
time: 199 us; the launch traced here: 198 us
  blocking collectives  83.4 us (42%)
  Pallas kernels  67.9 us (34%)
  starting transfers between devices  35.2 us (18%)
  waiting for transfers between devices  7.9 us (4%)
  local copies, waits for them, and re-layouts  2.17 us (1%)
    all_to_all x5, blocking collectives, across(): return lax.all_to_all(blocks, ACROSS, 0, 0, tiled=True)  83.4 us
    pallas_call x9, Pallas kernels, call(): pl.pallas_call(body, out_shape=tuple((made_as(i, made) for i, made in enu...  64.2 us
    all_to_all x1, starting transfers between devices, across(): return lax.all_to_all(blocks, ACROSS, 0, 0, tiled=True)  13.5 us
    ppermute x4, starting transfers between devices, swap(): return lax.ppermute(array, 'c', [(0, 1), (1, 0)])  8.97 us
    ppermute x1, starting transfers between devices, per_device(): left = lax.ppermute(edge(COLS - 1), ('x', 'c'), right_way)  4.84 us
    all_to_all x1, waiting for transfers between devices, across(): return lax.all_to_all(blocks, ACROSS, 0, 0, tiled=True)  4.75 us
    ppermute x1, starting transfers between devices, per_device(): top = lax.ppermute(condition[:, ROWS - 1:], 'sp', down)  4.66 us
  transfers between devices with their start and end apart: 9, of which 4 were waited for; matrix products, arithmetic and copies ran while one was open for 1% of the time, Pallas kernels for 8%

profile of v2, /device:TPU:1, one launch (start us, length us, event | category | flops | bytes accessed | tf_op | source)
XLA Modules:
  0.0 198.4 jit_solution(9263809111148398345)
XLA Ops:
  2.7 4.7 %collective-permute-start = (bf16[8,1,8,192]{3,2,1,0:T(8,128)(2,1)S(1)}, bf16[8,1,8,192]{3,2,1,0:T(8,128)(2,1)S(1)}, u32[]{:S(2)}, u32[]{:S(2)}) collective-permute-start(bf16[8,1,8,192]{3,2,1,0:T(8,128)(2,1)S(1)} %get-tuple-element.121), channel_id=1, source_target_pairs={{0,8},{8,16},{16,24},{24,32},{32,40},{40,48},{48,56},{56,64},{64,7... | collective-permute-start | bytes 73736 | tf_op jit(solution)/shard_map/ppermute | solution.py:693
  8.7 4.8 %collective-permute-start.2 = (bf16[48,192]{1,0:T(8,128)(2,1)S(1)}, bf16[48,192]{1,0:T(8,128)(2,1)S(1)}, u32[]{:S(2)}, u32[]{:S(2)}) collective-permute-start(bf16[48,192]{1,0:T(8,128)(2,1)S(1)} %reshape.73), channel_id=1, source_target_pairs={{0,1},{1,2},{2,3},{3,4},{4,5},{5,6},{6,7},{8,9},{9,10},{10,11},{11... | collective-permute-start | bytes 55304 | tf_op jit(solution)/shard_map/ppermute | solution.py:701
  13.5 1.9 collective-permute-start.3
  15.5 2.1 %load_adapter.1 = (bf16[192,320]{1,0:T(8,128)(2,1)S(1)}, f32[320]{0:T(512)S(1)}, bf16[9,320,320]{2,1,0:T(8,128)(2,1)S(1)}, bf16[8,4,8,192]{3,2,1,0:T(8,128)(2,1)...) custom-call(bf16[192,320]{1,0:T(8,128)(2,1)} %refs_1_.8, ...), custom_call_target="tpu_custom_call" | custom-call | tf_op jit(solution)/shard_map/load_adapter/pallas_call | solution.py:167
  18.7 5.0 %adapter.1 = (bf16[8,8,32,128]{3,2,1,0:T(8,128)(2,1)}, f32[256,320]{1,0:T(8,128)}, bf16[256,320]{1,0:T(8,128)(2,1)}, f32[256,320]{1,0:T(8,128)}, bf16[9,256,256]{2,1,0:T(8,128)(2,1)}) custom-call(s32[3]{0:T(128)S(1)} %pad_add_fusion.refs_0_, s32[8]{0:T(128)S(1)} %copy-done.11, bf16[8,4,8,192]{3,2,1,0:T(8,128)(2,1)S(1)} %get-tuple-element.64.refs_2_, ...), custom_call_target="tpu_custom_call" | custom-call | tf_op jit(solution)/shard_map/adapter/pallas_call | solution.py:132
  23.7 13.5 %all-to-all-start = ((bf16[64,32,128]{2,1,0:T(8,128)(2,1)}), bf16[64,32,128]{2,1,0:T(8,128)(2,1)S(1)}, u32[]{:S(2)}, u32[]{:S(2)}) async-start(bf16[64,32,128]{2,1,0:T(8,128)(2,1)} %bitcast.53), calls=%async_computation | async-start | bytes 1048576 | tf_op jit(solution)/shard_map/all_to_all | solution.py:680
  37.2 8.1 %text.1 = (bf16[8,80,512]{2,1,0:T(8,128)(2,1)}, bf16[8,80,512]{2,1,0:T(8,128)(2,1)}) custom-call(bf16[616,768]{1,0:T(8,128)(2,1)} %bitcast.51, bf16[320,768]{1,0:T(8,128)(2,1)} %bitcast.54, bf16[320,768]{1,0:T(8,128)(2,1)} %bitcast.55), custom_call_target="tpu_custom_call" | custom-call | tf_op jit(solution)/shard_map/text/pallas_call | solution.py:132
  45.2 4.7 %all-to-all-done = bf16[64,32,128]{2,1,0:T(8,128)(2,1)S(1)} async-done(((bf16[64,32,128]{2,1,0:T(8,128)(2,1)}), bf16[64,32,128]{2,1,0:T(8,128)(2,1)S(1)}, u32[]{:S(2)}, u32[]{:S(2)}) %all-to-all-start) | async-done | bytes 524320 | tf_op jit(solution)/shard_map/all_to_all | solution.py:680
  51.5 2.1 %form.1 = (bf16[320,512]{1,0:T(8,128)(2,1)}, bf16[512,320]{1,0:T(8,128)(2,1)}, bf16[1024,768]{1,0:T(8,128)(2,1)S(1)}) custom-call(bf16[320,320]{1,0:T(8,128)(2,1)} %refs_0_.4, bf16[320,320]{1,0:T(8,128)(2,1)} %refs_1_.6, bf16[320,320]{1,0:T(8,128)(2,1)} %refs_2_.1), custom_call_target="tpu_custom_call" | custom-call | tf_op jit(solution)/shard_map/form/pallas_call | solution.py:132
  53.6 11.9 %attend.1 = (bf16[64,16,128]{2,1,0:T(8,128)(2,1)S(1)}, f32[2048,128]{1,0:T(8,128)}, bf16[2048,4096]{1,0:T(8,128)(2,1)}, bf16[128,4096]{1,0:T(8,128)(2,1)}, bf16[128,2048]{1,0:T(8,128)(2,1)}) custom-call(bf16[2048,128]{1,0:T(8,128)(2,1)S(1)} %bitcast.44, bf16[2048,128]{1,0:T(8,128)(2,1)S(1)} %collective-permute-done.4.refs_1_), custom_call_target="tpu_custom_call" | custom-call | tf_op jit(solution)/shard_map/attend/pallas_call | solution.py:132
  65.5 14.4 %all_to_all.30 = bf16[64,16,128]{2,1,0:T(8,128)(2,1)S(1)} all-to-all(bf16[64,16,128]{2,1,0:T(8,128)(2,1)S(1)} %get-tuple-element.84), channel_id=1, replica_groups=mesh['sp'=16,'x'=4,'c'=2] {'sp','x'}, dimensions={0} | all-to-all | bytes 524288 | tf_op jit(solution)/shard_map/all_to_all | solution.py:680
  79.8 12.8 %middle.1 = (bf16[256,320]{1,0:T(8,128)(2,1)}, f32[256,320]{1,0:T(8,128)}, bf16[8,8,16,128]{3,2,1,0:T(8,128)(2,1)S(1)}) custom-call(s32[8]{0:T(128)S(1)} %copy-done.12, bf16[8,8,16,128]{3,2,1,0:T(8,128)(2,1)S(1)} %bitcast.45, f32[256,320]{1,0:T(8,128)} %get-tuple-element.85.refs_2_.refs_3_, bf16[256,320]{1,0:T(8,128)(2,1)} %bitcast.57, ...), custom_call_target="tpu_custom_call" | custom-call | tf_op jit(solution)/shard_map/middle/pallas_call | solution.py:132
  92.6 14.0 %all_to_all.31.refs_3_ = bf16[64,16,128]{2,1,0:T(8,128)(2,1)S(1)} all-to-all(bf16[64,16,128]{2,1,0:T(8,128)(2,1)S(1)} %bitcast.46), channel_id=1, replica_groups=mesh['sp'=16,'x'=4,'c'=2] {'sp','x'}, dimensions={0} | all-to-all | bytes 524288 | tf_op jit(solution)/shard_map/all_to_all | solution.py:680
  106.7 15.9 %attend_back.1 = (f32[2048,128]{1,0:T(8,128)S(1)}, bf16[2048,128]{1,0:T(8,128)(2,1)S(1)}) custom-call(bf16[128,4096]{1,0:T(8,128)(2,1)S(1)} %copy-done.3, bf16[128,2048]{1,0:T(8,128)(2,1)S(1)} %copy-done.6, f32[2048,128]{1,0:T(8,128)S(1)} %copy-done.2, bf16[64,16,128]{2,1,0:T(8,128)(2,1)S(1)} %all_to_all.31.refs_3_, bf16[2048,4096]{1,0:T(8,128)(2,1)} %get-tuple-element.96.refs_4_), custom_call_target="tpu_custom_call" | custom-call | tf_op jit(solution)/shard_map/attend_back/pallas_call | solution.py:132
  122.6 2.8 %collective-permute-start.5 = (bf16[2048,128]{1,0:T(8,128)(2,1)S(1)}, bf16[2048,128]{1,0:T(8,128)(2,1)S(1)}, u32[]{:S(2)}, u32[]{:S(2)}) collective-permute-start(bf16[2048,128]{1,0:T(8,128)(2,1)S(1)} %get-tuple-element.98), channel_id=1, source_target_pairs={{0,1},{1,0},{2,3},{3,2},{4,5},{5,4},{6,7},{7,6},{8,9},{9,8},{10,11... | collective-permute-start | bytes 1572872 | tf_op jit(solution)/shard_map/ppermute | solution.py:676
  125.3 1.9 join.1.refs_2_
  127.4 17.3 %all_to_all.32 = bf16[64,32,128]{2,1,0:T(8,128)(2,1)S(1)} all-to-all(bf16[64,32,128]{2,1,0:T(8,128)(2,1)S(1)} %bitcast.50), channel_id=1, replica_groups=mesh['sp'=16,'x'=4,'c'=2] {'sp','x'}, dimensions={0} | all-to-all | bytes 1048576 | tf_op jit(solution)/shard_map/all_to_all | solution.py:680
  144.8 2.7 %finish.1 = (f32[256,320]{1,0:T(8,128)}, bf16[2,3072,128]{2,1,0:T(8,128)(2,1)S(1)}) custom-call(s32[3]{0:T(128)S(1)} %pad_add_fusion.refs_0_, bf16[8,8,32,128]{3,2,1,0:T(8,128)(2,1)S(1)} %bitcast.42, bf16[320,1024]{1,0:T(8,128)(2,1)S(1)} %join.1.refs_2_, f32[256,320]{1,0:T(8,128)S(1)} %copy-done, f32[256,320]{1,0:T(8,128)S(1)} %copy-done.8, ...), custom_call_target="tpu_custom_call" | custom-call | tf_op jit(solution)/shard_map/finish/pallas_call | solution.py:132
  149.1 1.9 collective-permute-done.6
  151.2 19.4 %all_to_all.33 = bf16[64,48,128]{2,1,0:T(8,128)(2,1)S(1)} all-to-all(bf16[64,48,128]{2,1,0:T(8,128)(2,1)S(1)} %bitcast.49), channel_id=1, replica_groups=mesh['sp'=16,'x'=4,'c'=2] {'sp','x'}, dimensions={0} | all-to-all | bytes 1572864 | tf_op jit(solution)/shard_map/all_to_all | solution.py:680
  170.9 18.3 %all_to_all.34 = bf16[64,48,128]{2,1,0:T(8,128)(2,1)S(1)} all-to-all(bf16[64,48,128]{2,1,0:T(8,128)(2,1)S(1)} %broadcast_in_dim.2), channel_id=1, replica_groups=mesh['sp'=16,'x'=4,'c'=2] {'sp','x'}, dimensions={0} | all-to-all | bytes 1572864 | tf_op jit(solution)/shard_map/all_to_all | solution.py:680
  189.2 3.1 %collective-permute-start.7 = (bf16[3072,128]{1,0:T(8,128)(2,1)S(1)}, bf16[3072,128]{1,0:T(8,128)(2,1)S(1)}, u32[]{:S(2)}, u32[]{:S(2)}) collective-permute-start(bf16[3072,128]{1,0:T(8,128)(2,1)S(1)} %bitcast.40), channel_id=1, source_target_pairs={{0,1},{1,0},{2,3},{3,2},{4,5},{5,4},{6,7},{7,6},{8,9},{9,8},{10,11... | collective-permute-start | bytes 2359304 | tf_op jit(solution)/shard_map/ppermute | solution.py:676
  192.4 1.6 load_weights.1
  194.3 3.9 %weights.1 = (f32[192,320]{1,0:T(8,128)}, f32[320]{0:T(512)}, f32[9,320,320]{2,1,0:T(8,128)}, f32[320]{0:T(512)}, f32[320,320]{1,0:T(8,128)}, /*index=5*/f32[320]{0:T(512)}) custom-call(s32[3]{0:T(128)S(1)} %pad_add_fusion.refs_0_, bf16[3072,128]{1,0:T(8,128)(2,1)S(1)} %bitcast.41, bf16[3072,128]{1,0:T(8,128)(2,1)S(1)} %collective-permute-done.7.refs_2_, ...), custom_call_target="tpu_custom_call" | custom-call | tf_op jit(solution)/shard_map/weights/pallas_call | solution.py:132
  (55 shorter events, 8.3 us)
Async XLA Ops:
  1.4 7.0 %collective-permute-start.1 = (bf16[8,1,8,192]{3,2,1,0:T(8,128)(2,1)S(1)}, bf16[8,1,8,192]{3,2,1,0:T(8,128)(2,1)S(1)}, u32[]{:S(2)}, u32[]{:S(2)}) collective-permute-start(bf16[8,1,8,192]{3,2,1,0:T(8,128)(2,1)S(1)} %get-tuple-element.120), channel_id=1, source_target_pairs={{8,0},{16,8},{24,16},{32,24},{40,32},{48,40},{56,48},{64,56},{72,6... | collective-permute-start | bytes 73736 | tf_op jit(solution)/shard_map/ppermute | solution.py:694
  2.7 5.8 %collective-permute-start = (bf16[8,1,8,192]{3,2,1,0:T(8,128)(2,1)S(1)}, bf16[8,1,8,192]{3,2,1,0:T(8,128)(2,1)S(1)}, u32[]{:S(2)}, u32[]{:S(2)}) collective-permute-start(bf16[8,1,8,192]{3,2,1,0:T(8,128)(2,1)S(1)} %get-tuple-element.121), channel_id=1, source_target_pairs={{0,8},{8,16},{16,24},{24,32},{32,40},{40,48},{48,56},{56,64},{64,7... | collective-permute-start | bytes 73736 | tf_op jit(solution)/shard_map/ppermute | solution.py:693
  8.7 9.0 %collective-permute-start.2 = (bf16[48,192]{1,0:T(8,128)(2,1)S(1)}, bf16[48,192]{1,0:T(8,128)(2,1)S(1)}, u32[]{:S(2)}, u32[]{:S(2)}) collective-permute-start(bf16[48,192]{1,0:T(8,128)(2,1)S(1)} %reshape.73), channel_id=1, source_target_pairs={{0,1},{1,2},{2,3},{3,4},{4,5},{5,6},{6,7},{8,9},{9,10},{10,11},{11... | collective-permute-start | bytes 55304 | tf_op jit(solution)/shard_map/ppermute | solution.py:701
  13.5 5.1 %collective-permute-start.3 = (bf16[48,192]{1,0:T(8,128)(2,1)S(1)}, bf16[48,192]{1,0:T(8,128)(2,1)S(1)}, u32[]{:S(2)}, u32[]{:S(2)}) collective-permute-start(bf16[48,192]{1,0:T(8,128)(2,1)S(1)} %reshape.74), channel_id=1, source_target_pairs={{1,0},{2,1},{3,2},{4,3},{5,4},{6,5},{7,6},{9,8},{10,9},{11,10},{12... | collective-permute-start | bytes 55304 | tf_op jit(solution)/shard_map/ppermute | solution.py:702
  15.5 3.1 %copy-start.11 = (s32[8]{0:T(128)S(1)}, s32[8]{0:T(128)}, u32[]{:S(2)}) copy-start(s32[8]{0:T(128)} %refs_1_.5) | copy-start | bytes 100
  23.7 26.3 %all-to-all-start = ((bf16[64,32,128]{2,1,0:T(8,128)(2,1)}), bf16[64,32,128]{2,1,0:T(8,128)(2,1)S(1)}, u32[]{:S(2)}, u32[]{:S(2)}) async-start(bf16[64,32,128]{2,1,0:T(8,128)(2,1)} %bitcast.53), calls=%async_computation | async-start | bytes 1048576 | tf_op jit(solution)/shard_map/all_to_all | solution.py:680
  45.2 34.6 %copy-start.12 = (s32[8]{0:T(128)S(1)}, s32[8]{0:T(128)}, u32[]{:S(2)}) copy-start(s32[8]{0:T(128)} %refs_0_.5) | copy-start | bytes 100
  50.0 3.6 %collective-permute-start.4 = (bf16[2048,128]{1,0:T(8,128)(2,1)S(1)}, bf16[2048,128]{1,0:T(8,128)(2,1)S(1)}, u32[]{:S(2)}, u32[]{:S(2)}) collective-permute-start(bf16[2048,128]{1,0:T(8,128)(2,1)S(1)} %bitcast.43), channel_id=1, source_target_pairs={{0,1},{1,0},{2,3},{3,2},{4,5},{5,4},{6,7},{7,6},{8,9},{9,8},{10,11... | collective-permute-start | bytes 1572872 | tf_op jit(solution)/shard_map/ppermute | solution.py:676
  79.8 26.8 %copy-start.2 = (f32[2048,128]{1,0:T(8,128)S(1)}, f32[2048,128]{1,0:T(8,128)}, u32[]{:S(2)}) copy-start(f32[2048,128]{1,0:T(8,128)} %get-tuple-element.94.refs_2_) | copy-start | bytes 3145732
  79.8 26.8 %copy-start.3 = (bf16[128,4096]{1,0:T(8,128)(2,1)S(1)}, bf16[128,4096]{1,0:T(8,128)(2,1)}, u32[]{:S(2)}) copy-start(bf16[128,4096]{1,0:T(8,128)(2,1)} %get-tuple-element.92.refs_0_) | copy-start | bytes 3145732
  79.8 26.8 %copy-start.6 = (bf16[128,2048]{1,0:T(8,128)(2,1)S(1)}, bf16[128,2048]{1,0:T(8,128)(2,1)}, u32[]{:S(2)}) copy-start(bf16[128,2048]{1,0:T(8,128)(2,1)} %get-tuple-element.93.refs_1_) | copy-start | bytes 1572868
  122.6 4.7 %collective-permute-start.5 = (bf16[2048,128]{1,0:T(8,128)(2,1)S(1)}, bf16[2048,128]{1,0:T(8,128)(2,1)S(1)}, u32[]{:S(2)}, u32[]{:S(2)}) collective-permute-start(bf16[2048,128]{1,0:T(8,128)(2,1)S(1)} %get-tuple-element.98), channel_id=1, source_target_pairs={{0,1},{1,0},{2,3},{3,2},{4,5},{5,4},{6,7},{7,6},{8,9},{9,8},{10,11... | collective-permute-start | bytes 1572872 | tf_op jit(solution)/shard_map/ppermute | solution.py:676
  127.2 17.5 %copy-start = (f32[256,320]{1,0:T(8,128)S(1)}, f32[256,320]{1,0:T(8,128)}, u32[]{:S(2)}) copy-start(f32[256,320]{1,0:T(8,128)} %get-tuple-element.85.refs_2_.refs_3_) | copy-start | bytes 983044
  127.2 17.5 %copy-start.1 = (bf16[9,256,256]{2,1,0:T(8,128)(2,1)S(1)}, bf16[9,256,256]{2,1,0:T(8,128)(2,1)}, u32[]{:S(2)}) copy-start(bf16[9,256,256]{2,1,0:T(8,128)(2,1)} %get-tuple-element.105.refs_7_) | copy-start | bytes 3538948
  127.3 17.5 %copy-start.4 = (bf16[320,320]{1,0:T(8,128)(2,1)S(1)}, bf16[320,320]{1,0:T(8,128)(2,1)}, u32[]{:S(2)}) copy-start(bf16[320,320]{1,0:T(8,128)(2,1)} %refs_8_.3) | copy-start | bytes 614404
  127.3 17.5 %copy-start.7 = (f32[256,320]{1,0:T(8,128)S(1)}, f32[256,320]{1,0:T(8,128)}, u32[]{:S(2)}) copy-start(f32[256,320]{1,0:T(8,128)} %get-tuple-element.103.refs_5_) | copy-start | bytes 983044
  127.3 17.5 %copy-start.8 = (f32[256,320]{1,0:T(8,128)S(1)}, f32[256,320]{1,0:T(8,128)}, u32[]{:S(2)}) copy-start(f32[256,320]{1,0:T(8,128)} %get-tuple-element.102.refs_4_) | copy-start | bytes 983044
  127.3 17.5 %copy-start.9 = (bf16[256,320]{1,0:T(8,128)(2,1)S(1)}, bf16[256,320]{1,0:T(8,128)(2,1)}, u32[]{:S(2)}) copy-start(bf16[256,320]{1,0:T(8,128)(2,1)} %get-tuple-element.104.refs_6_) | copy-start | bytes 491524
  147.5 3.5 %collective-permute-start.6 = (bf16[3072,128]{1,0:T(8,128)(2,1)S(1)}, bf16[3072,128]{1,0:T(8,128)(2,1)S(1)}, u32[]{:S(2)}, u32[]{:S(2)}) collective-permute-start(bf16[3072,128]{1,0:T(8,128)(2,1)S(1)} %slice_bitcast_fusion), channel_id=1, source_target_pairs={{0,1},{1,0},{2,3},{3,2},{4,5},{5,4},{6,7},{7,6},{8,9},{9,8},{10,11... | collective-permute-start | bytes 2359304 | tf_op jit(solution)/shard_map/ppermute | solution.py:676
  170.7 21.7 %copy-start.5 = (bf16[192,320]{1,0:T(8,128)(2,1)S(1)}, bf16[192,320]{1,0:T(8,128)(2,1)}, u32[]{:S(2)}) copy-start(bf16[192,320]{1,0:T(8,128)(2,1)} %refs_1_.8) | copy-start | bytes 368644
  170.7 21.7 %copy-start.10 = (f32[320]{0:T(512)S(1)}, f32[320]{0:T(512)}, u32[]{:S(2)}) copy-start(f32[320]{0:T(512)} %refs_2_.3) | copy-start | bytes 3844
  189.2 5.1 %collective-permute-start.7 = (bf16[3072,128]{1,0:T(8,128)(2,1)S(1)}, bf16[3072,128]{1,0:T(8,128)(2,1)S(1)}, u32[]{:S(2)}, u32[]{:S(2)}) collective-permute-start(bf16[3072,128]{1,0:T(8,128)(2,1)S(1)} %bitcast.40), channel_id=1, source_target_pairs={{0,1},{1,0},{2,3},{3,2},{4,5},{5,4},{6,7},{7,6},{8,9},{9,8},{10,11... | collective-permute-start | bytes 2359304 | tf_op jit(solution)/shard_map/ppermute | solution.py:676

commit v3 on v2

--- a/solution.py
+++ b/solution.py
@@ -6,12 +6,12 @@
 from jax.sharding import Mesh
 from jax.sharding import PartitionSpec as P
 
-ITEMS, ROWS, COLS, C, CIN, HEADS, HEAD, FF = 8, 4, 8, 320, 192, 8, 40, 1280
-CELLS = ITEMS * ROWS * COLS
+STRIPS, ROWS, COLS, C, CIN, HEADS, HEAD, FF = 8, 4, 8, 320, 192, 8, 40, 1280
+CELLS = STRIPS * ROWS * COLS
 PART = ROWS * COLS
 CHIPS = 64
 HALF = CHIPS * PART
-TEXT = 80
+TEXT = 128
 LANES = 128
 WIDE = 256
 GROUP = 160
@@ -20,7 +20,8 @@
 EPS = 1e-5
 MASKED = -1e30
 KEY, VALUE, MASK = HEAD, 2 * HEAD, 3 * HEAD
-ACROSS = ("sp", "x")
+GROUP_OF_ITEM, CHIPS_ALL = ("b", "x"), ("a", "b", "x")
+LATENT, COTANGENT = 256, 640
 SUM_ROWS = 3072
 
 bf16, f32 = jnp.bfloat16, jnp.float32
@@ -83,7 +84,7 @@
 
 
 def call(kernel, outs, ins, name, scalars=0, scratch=(), vmem=16, fetch=(), store=(), far=(),
-    near=(), held=(),
+    near=(), held=(), cost=None,
 ):
     fetch, store = list(fetch), list(store)
     far_in = [i for i in far if i < len(ins)]
@@ -136,6 +137,7 @@
         out_specs=tuple(out_spec(i) for i in range(len(outs))),
         scratch_shapes=list(scratch) + extra,
         compiler_params=pltpu.CompilerParams(vmem_limit_bytes=vmem << 20),
+        cost_estimate=cost,
         name=name,
     )(
         *(
@@ -196,22 +198,27 @@
 
 
 def adapter_kernel(
-    place, valid, center, top, bottom, left, right, latent, w_in, b_in, w_conv, b_conv, w_out,
+    place, valid, cells, beside, left, right, w_in, b_in, w_conv, b_conv, w_out,
     b_out, w_query, w_key, w_value, rows_out, mixed_out, smooth_out, slope_out, cond_out,
     w_wide,
 ):
-    span = ITEMS * (ROWS + 2)
+    span = STRIPS * (ROWS + 2)
     w_wide[:CIN, :] = w_in[...]
     w_wide[CIN:, :] = bias_rows(b_in[...])
-
-    def widen(values):
-        blank = jnp.zeros(values.shape[:-1] + (WIDE - CIN,), f32)
-        return jnp.concatenate([values.astype(f32), blank], axis=-1)
-
-    block = jnp.concatenate([top[...], center[...], bottom[...]], axis=1)
-    block = widen(block.reshape(span, COLS, CIN))
-    shape = (ITEMS, ROWS + 2, COLS, WIDE)
-    row = lax.broadcasted_iota(jnp.int32, shape, 1) + ROWS * place[0] - 1
+    upper = place[3] == 0
+
+    def tall(own, first, last):
+        blank = jnp.zeros_like(first[:1])
+        above = jnp.where(upper, jnp.concatenate([blank, last[:-1]], axis=0), last)
+        below = jnp.where(upper, first, jnp.concatenate([first[1:], blank], axis=0))
+        return jnp.concatenate([above, own, below], axis=1)
+
+    own = cells[:, :, :WIDE].astype(f32).reshape(STRIPS, ROWS, COLS, WIDE)
+    other = beside[...].astype(f32)
+    block = tall(own, other[:, :1], other[:, 1:]).reshape(span, COLS, WIDE)
+    shape = (STRIPS, ROWS + 2, COLS, WIDE)
+    row = 2 * ROWS * lax.broadcasted_iota(jnp.int32, shape, 0) + ROWS * place[3] - 1
+    row += lax.broadcasted_iota(jnp.int32, shape, 1)
     inside = (row >= 0) & (row < ROWS * 16)
     inside = jnp.where(inside, 1.0, 0.0).reshape(span, COLS, WIDE)
     lane = lane_of((span, COLS, WIDE))
@@ -220,7 +227,10 @@
     edges = []
     for n, side in enumerate((left, right)):
         there = (at > 0) if n == 0 else (at < COLS * 7)
-        edges.append((widen(side[...]).reshape(span, 1, WIDE), jnp.where(there, inside, 0.0)))
+        side = side[...].astype(f32).reshape(span, 1, WIDE)
+        side = side.reshape(STRIPS, ROWS + 2, 1, WIDE)
+        side = tall(side[:, :ROWS], side[:, ROWS : ROWS + 1], side[:, ROWS + 1 :])
+        edges.append((side.reshape(span, 1, WIDE), jnp.where(there, inside, 0.0)))
     near = jnp.where(col == 0, edges[0][0], pltpu.roll(block, 1, 1))
     near_inside = jnp.where(col == 0, edges[0][1], inside)
     far = jnp.where(col == COLS - 1, edges[1][0], pltpu.roll(block, COLS - 1, 1))
@@ -232,8 +242,8 @@
     for j, (moved, present) in enumerate(moves):
         moved = jnp.where(one, present, moved)
         start = dot(moved.reshape(span * COLS, WIDE).astype(bf16), w_wide[...])
-        start = start.reshape(ITEMS, ROWS + 2, COLS, C)
-        moved = moved.reshape(ITEMS, ROWS + 2, COLS, WIDE)
+        start = start.reshape(STRIPS, ROWS + 2, COLS, C)
+        moved = moved.reshape(STRIPS, ROWS + 2, COLS, WIDE)
         for i in range(3):
             patch = start[:, i : i + ROWS].reshape(CELLS, C).astype(bf16)
             if i == 1 and j == 1:
@@ -245,47 +255,34 @@
     smooth = (inner * gate).astype(bf16)
     smooth_out[...] = smooth
     slope_out[...] = gate * (1.0 + inner * (1.0 - gate))
-    mixed = latent[...].astype(f32) + (start_here + dot(smooth, w_out[...]) + b_out[...])
+    latent = cells[:, :, LATENT : LATENT + C].astype(f32).reshape(CELLS, C)
+    mixed = latent + (start_here + dot(smooth, w_out[...]) + b_out[...])
     mixed_out[...] = mixed
     normed = moments(mixed)[0].astype(bf16)
     projected = [dot(normed, w[...]) for w in (w_query, w_key, w_value)]
     projected[0] *= SCALE * LOG2E
-    lane = lane_of((PART, LANES - MASK))
-    row = lax.broadcasted_iota(jnp.int32, (PART, LANES - MASK), 0) // COLS + ROWS * place[0]
-    extras = []
-    for item in range(ITEMS):
-        hidden = jnp.where(row >= valid[item], MASKED, 0.0)
-        extras.append(jnp.where(lane == 0, hidden, 1.0))
-    extras = jnp.concatenate(extras, axis=0)
+    shape = (STRIPS, ROWS, COLS, LANES - MASK)
+    row = 2 * ROWS * lax.broadcasted_iota(jnp.int32, shape, 0) + ROWS * place[3]
+    row += lax.broadcasted_iota(jnp.int32, shape, 1)
+    hidden = jnp.where(row >= valid[place[0]], MASKED, 0.0)
+    extras = jnp.where(lane_of(shape) == 0, hidden, 1.0).reshape(CELLS, LANES - MASK)
     for head in range(HEADS):
         at = slice(head * HEAD, (head + 1) * HEAD)
         joined = jnp.concatenate([part[:, at] for part in projected] + [extras], axis=1)
-        rows_out[:, head] = joined.astype(bf16).reshape(ITEMS, PART, LANES)
+        rows_out[head] = joined.astype(bf16)
 
 
 def text_kernel(
     text, w_key_turned, w_value_turned, keys_out, values_out, wide_key, wide_value
 ):
-    count = text.shape[0]
-    token = lax.broadcasted_iota(jnp.int32, (TEXT, count), 0)
-    place = lane_of((TEXT, count))
     blank = jnp.zeros((WIDE - GROUP, text.shape[1]), bf16)
-    for source, wide in ((w_key_turned, wide_key), (w_value_turned, wide_value)):
+    states = text[...]
+    both = ((w_key_turned, wide_key, keys_out), (w_value_turned, wide_value, values_out))
+    for source, wide, target in both:
         for g in range(2):
             wide[g * WIDE : g * WIDE + GROUP, :] = source[g * GROUP : (g + 1) * GROUP, :]
             wide[g * WIDE + GROUP : (g + 1) * WIDE, :] = blank
-    text[:16]
-
-    def body(item, carry):
-        pick = jnp.where(place == token * ITEMS + item, 1.0, 0.0).astype(bf16)
-        states = dot(pick, text[...]).astype(bf16)
-        keys_out.buffer[item] = dot_nt(states, wide_key[...]).astype(bf16)
-        values_out.buffer[item] = dot_nt(states, wide_value[...]).astype(bf16)
-        return carry
-
-    lax.fori_loop(0, ITEMS, body, 0)
-    keys_out.start()
-    values_out.start()
+        target[...] = dot_nt(states, wide[...]).astype(bf16)
 
 
 def form_kernel(w_query, w_cross_out, w_attn, query_out, cross_out, spread_out):
@@ -394,102 +391,91 @@
 
 
 def middle_kernel(
-    lengths, heads_in, mixed, cotangent, text_keys, text_values, w_attn, b_attn, w_cross_query,
-    w_cross_out, b_cross, w_ff_in, b_ff_in, w_ff_turned, b_ff_out, result_out, grad_out, heads_out,
-    probs_keep,
+    place, lengths, heads_in, mixed, cells, text_keys, text_values, w_attn, b_attn,
+    w_cross_query, w_cross_out, b_cross, w_ff_in, b_ff_in, w_ff_turned, b_ff_out, result_out,
+    grad_out, heads_out, probs_keep,
 ):
     half = CELLS // 2
     split = w_attn.shape[1] // 2
-    packed = jnp.concatenate(
-        [heads_in[:, head].reshape(half, LANES) for head in range(HEADS)], axis=1
-    )
+    packed = jnp.concatenate([heads_in[head] for head in range(HEADS)], axis=1)
     both = dot(packed, w_attn[...])
-    shape = (ITEMS, 1, PART // 2, C)
+    shape = (STRIPS, 1, PART // 2, C)
     attended = jnp.concatenate(
         [both[:, :C].reshape(shape), both[:, split : split + C].reshape(shape)], axis=1
     ).reshape(CELLS, C)
     first = mixed[...] + attended + b_attn[...]
     unit_two, rate_two = moments(first)
     cross_query = dot(unit_two.astype(bf16), w_cross_query[...]).astype(bf16)
-    lane = lane_of((PART, WIDE))
+    lane = lane_of((TEXT, WIDE))
     in_head = [(lane >= HEAD * h) & (lane < HEAD * (h + 1)) for h in range(HEADS // 2)]
     groups = [slice(0, WIDE), slice(WIDE, 2 * WIDE)]
-    half_rows = HEADS * PART // 2
-
-    def by_head(values, others):
-        parts = []
+
+    def by_head(text):
+        kept = []
         for lanes in groups:
-            here = values[:, lanes]
-            rows = [jnp.where(mask, here, jnp.zeros_like(here)) for mask in in_head]
-            parts.append(dot_nt(jnp.concatenate(rows, axis=0), others[:, lanes]))
-        return jnp.concatenate(parts, axis=0)
-
-    def by_cell(weights, others):
-        parts = []
-        for g, lanes in enumerate(groups):
-            rows = dot(weights[g * half_rows : (g + 1) * half_rows], others[:, lanes])
-            total = jnp.zeros((PART, WIDE), f32)
-            for h, mask in enumerate(in_head):
-                total = jnp.where(mask, rows[h * PART : (h + 1) * PART], total)
-            parts.append(total)
-        return jnp.concatenate(parts, axis=1)
-
-    token = lane_of((HEADS * PART, TEXT))
-    outs = []
-    for item in range(ITEMS):
-        cells = slice(item * PART, (item + 1) * PART)
-        scores = by_head(cross_query[cells], text_keys[item]) * SCALE
-        scores = jnp.where(token < lengths[item], scores, MASKED)
-        weights = jnp.exp(scores - jnp.max(scores, -1, keepdims=True))
-        probs = weights / jnp.sum(weights, -1, keepdims=True)
-        probs_keep[item] = probs
-        outs.append(by_cell(probs.astype(bf16), text_values[item]))
-    cross = jnp.concatenate(outs, axis=0).astype(bf16)
+            here = text[:, lanes]
+            kept.append(
+                jnp.concatenate([jnp.where(m, here, jnp.zeros_like(here)) for m in in_head], 0)
+            )
+        return kept
+
+    keys, values = by_head(text_keys), by_head(text_values)
+    spans = [slice(g * HEADS // 2 * TEXT, (g + 1) * HEADS // 2 * TEXT) for g in range(2)]
+    heads = [slice(h * TEXT, (h + 1) * TEXT) for h in range(HEADS)]
+    token = lane_of((CELLS, TEXT)) < lengths[place[0]]
+    scores = [dot_nt(cross_query[:, groups[g]], keys[g]) * SCALE for g in range(2)]
+    scores = jnp.concatenate(scores, axis=1)
+    for at in heads:
+        part = jnp.where(token, scores[:, at], MASKED)
+        weights = jnp.exp(part - jnp.max(part, -1, keepdims=True))
+        probs_keep[:, at] = weights / jnp.sum(weights, -1, keepdims=True)
+    cross = [dot(probs_keep[:, spans[g]].astype(bf16), values[g]) for g in range(2)]
+    cross = jnp.concatenate(cross, axis=1).astype(bf16)
     second = first + dot(cross, w_cross_out[...]) + b_cross[...]
     unit_three, rate_three = moments(second)
     normed_three = unit_three.astype(bf16)
-    upstream = cotangent[...]
+    upstream = cells[:, :, COTANGENT : COTANGENT + C].reshape(CELLS, C)
     result = second + b_ff_out[...]
     grad_normed = jnp.zeros((CELLS, C), f32)
     step = 256
     for at in range(0, FF, step):
-        values, gates = slice(at, at + step), slice(FF + at, FF + at + step)
-        value = dot(normed_three, w_ff_in[:, values]) + b_ff_in[values]
+        ups, gates = slice(at, at + step), slice(FF + at, FF + at + step)
+        value = dot(normed_three, w_ff_in[:, ups]) + b_ff_in[ups]
         gate = dot(normed_three, w_ff_in[:, gates]) + b_ff_in[gates]
         normal = 0.5 + 0.5 * lax.erf(gate * (0.5**0.5))
         density = jnp.exp(gate * gate * -0.5) * 0.3989422804014327
         gelu = gate * normal
-        result += dot_nt((value * gelu).astype(bf16), w_ff_turned[:, values])
-        grad_act = dot(upstream, w_ff_turned[:, values])
+        result += dot_nt((value * gelu).astype(bf16), w_ff_turned[:, ups])
+        grad_act = dot(upstream, w_ff_turned[:, ups])
         grad_value = (grad_act * gelu).astype(bf16)
         grad_gate = (grad_act * value * (normal + gate * density)).astype(bf16)
-        grad_normed += dot_nt(grad_value, w_ff_in[:, values])
+        grad_normed += dot_nt(grad_value, w_ff_in[:, ups])
         grad_normed += dot_nt(grad_gate, w_ff_in[:, gates])
     result_out[...] = result.astype(bf16)
     grad_second = upstream.astype(f32) + norm_back(unit_three, rate_three, grad_normed)
     grad_cross = dot_nt(grad_second.astype(bf16), w_cross_out[...]).astype(bf16)
-    outs = []
-    for item in range(ITEMS):
-        cells = slice(item * PART, (item + 1) * PART)
-        grad_probs = by_head(grad_cross[cells], text_values[item])
-        probs = probs_keep[item]
-        weighted = jnp.sum(probs * grad_probs, -1, keepdims=True)
-        grad_scores = (probs * (grad_probs - weighted)).astype(bf16)
-        outs.append(by_cell(grad_scores, text_keys[item]))
-    grad_query = (jnp.concatenate(outs, axis=0) * SCALE).astype(bf16)
+    grad_probs = [dot_nt(grad_cross[:, groups[g]], values[g]) for g in range(2)]
+    grad_probs = jnp.concatenate(grad_probs, axis=1)
+    grad_scores = []
+    for at in heads:
+        probs, grads = probs_keep[:, at], grad_probs[:, at]
+        weighted = jnp.sum(probs * grads, -1, keepdims=True)
+        grad_scores.append((probs * (grads - weighted)).astype(bf16))
+    grad_scores = jnp.concatenate(grad_scores, axis=1)
+    grad_query = [dot(grad_scores[:, spans[g]], keys[g]) for g in range(2)]
+    grad_query = (jnp.concatenate(grad_query, axis=1) * SCALE).astype(bf16)
     grad_first = grad_second + norm_back(
         unit_two, rate_two, dot_nt(grad_query, w_cross_query[...])
     )
     grad_out[...] = grad_first
-    pairs = grad_first.reshape(ITEMS, 2, PART // 2, C)
+    pairs = grad_first.reshape(STRIPS, 2, PART // 2, C)
     gap = jnp.zeros((half, split - C), f32)
     both = jnp.concatenate(
         [pairs[:, 0].reshape(half, C), gap, pairs[:, 1].reshape(half, C), gap], axis=1
     ).astype(bf16)
     packed = dot_nt(both, w_attn[...]).astype(bf16)
     for head in range(HEADS):
-        piece = packed[:, head * LANES : (head + 1) * LANES]
-        heads_out[:, head] = piece.reshape(ITEMS, PART // 2, LANES)
+        heads_out[head] = packed[:, head * LANES : (head + 1) * LANES]
 
 
 WIDE_BLOCK = 512
@@ -588,15 +574,15 @@
 
 
 def finish_kernel(
-    place, rows, w_qkv, mixed, grad_first, slope, smooth, cond, w_out, latent_out, parts_out
+    place, rows, w_qkv, mixed, grad_first, slope, smooth, cond, w_out, result, back_out, parts_out
 ):
-    joined = jnp.concatenate(
-        [rows[:, head].reshape(CELLS, LANES) for head in range(HEADS)], axis=1
-    )
+    joined = jnp.concatenate([rows[head] for head in range(HEADS)], axis=1)
     unit, rate = moments(mixed[...])
     latent = grad_first[...] + norm_back(unit, rate, dot_nt(joined, w_qkv[...]))
-    latent_out[...] = latent
     branch = latent.astype(bf16)
+    blank = jnp.zeros((CELLS, 384 - C), bf16)
+    back = jnp.concatenate([result[...], blank, branch, blank], axis=1)
+    back_out[...] = back.reshape(STRIPS, PART, 768)
     inner = (dot_nt(branch, w_out[...]) * slope[...]).astype(bf16)
     inner_turned = jnp.transpose(inner)
     branch_turned = jnp.transpose(branch)
@@ -676,8 +662,8 @@
     return lax.ppermute(array, "c", [(0, 1), (1, 0)])
 
 
-def across(blocks):
-    return lax.all_to_all(blocks, ACROSS, 0, 0, tiled=True)
+def across(blocks, axes):
+    return lax.all_to_all(blocks, axes, 0, 0, tiled=True)
 
 
 def per_device(
@@ -685,66 +671,78 @@
     b_out, w_query, w_key, w_value, w_attn_out, b_attn_out, w_cross_query, w_cross_key,
     w_cross_value, w_cross_out, b_cross_out, w_ff_in, b_ff_in, w_ff_out, b_ff_out, cotangent,
 ):
-    core = lax.axis_index("c")
-    place = jnp.stack([lax.axis_index("sp"), core, 2 * lax.axis_index("x") + core])
-    place = place.astype(jnp.int32)
-
-    down = [(i, i + 1) for i in range(15)]
-    top = lax.ppermute(condition[:, ROWS - 1 :], "sp", down)
-    bottom = lax.ppermute(condition[:, :1], "sp", [(b, a) for a, b in down])
+    core, column = lax.axis_index("c"), 2 * lax.axis_index("x") + lax.axis_index("c")
+    item, lower = lax.axis_index("a"), lax.axis_index("b")
+    place = jnp.stack([item, core, column, lower]).astype(jnp.int32)
+
+    wide = [
+        jnp.pad(x.reshape(STRIPS, PART, -1), ((0, 0), (0, 0), (0, lanes - x.shape[-1])))
+        for x, lanes in ((condition, 256), (latent, 384), (cotangent, 384))
+    ]
+    cells = across(jnp.concatenate(wide, axis=-1), "a")
+
+    text = lax.dynamic_index_in_dim(text_states, item, 0, keepdims=False)
+    text = jnp.pad(text, ((0, TEXT - text.shape[0]), (0, 0)))
+    text_keys, text_values = call(
+        text_kernel,
+        (out(TEXT, 2 * WIDE), out(TEXT, 2 * WIDE)),
+        (text, w_cross_key.T, w_cross_value.T),
+        "text",
+        scratch=[pltpu.VMEM((2 * WIDE, text.shape[1]), bf16)] * 2,
+        fetch=(0, 1, 2),
+        store=(0, 1),
+        cost=pl.CostEstimate(flops=4 * 10**9, bytes_accessed=2 * 10**6, transcendentals=0),
+    )
+    (w_turned,) = call(
+        widen_kernel, (out(C, WIDE),), (w_in, b_in), "widen", fetch=(0, 1), store=(0,)
+    )
+    cells, text_keys, w_turned = after(cells, text_keys, w_turned)
+
+    here = cells[:, :, :WIDE].reshape(STRIPS, ROWS, COLS, WIDE)
+    ends = jnp.concatenate([here[:, :1], here[:, ROWS - 1 :]], axis=1)
+    beside = lax.ppermute(ends, "b", [(0, 1), (1, 0)])
     right_way = [(i, i + 1) for i in range(7)]
 
     def edge(col):
-        tall = jnp.concatenate([top[:, :, col], condition[:, :, col], bottom[:, :, col]], axis=1)
-        return tall.reshape(ITEMS * (ROWS + 2), CIN)
+        rows = jnp.concatenate([here[:, :, col], beside[:, :, col]], axis=1)
+        return rows.reshape(STRIPS * (ROWS + 2), WIDE)
 
     left = lax.ppermute(edge(COLS - 1), ("x", "c"), right_way)
     right = lax.ppermute(edge(0), ("x", "c"), [(b, a) for a, b in right_way])
-    top, first_bias = after(top, b_in)
-    adapter_arrays = bring(
+    beside, first_bias = after(beside, b_in)
+    (
+        w_in_here, b_in_here, taps_here, b_conv_here, w_out_here, b_out_here, w_query_here,
+        w_key_here, w_value_here,
+    ) = bring(
         [
-            w_in, first_bias, w_conv.reshape(9, C, C), condition, latent.reshape(CELLS, C),
-            b_conv, w_out, b_out, w_query, w_key, w_value,
+            w_in, first_bias, w_conv.reshape(9, C, C), b_conv, w_out, b_out, w_query, w_key,
+            w_value,
         ],
         "load_adapter",
     )
-    (w_in_here, b_in_here, taps_here, condition_here, latent_here, b_conv_here) = adapter_arrays[:6]
-    (w_out_here, b_out_here, w_query_here, w_key_here, w_value_here) = adapter_arrays[6:]
-
     rows, mixed, smooth, slope, cond = call(
         adapter_kernel,
         (
-            out(ITEMS, HEADS, PART, LANES),
+            out(HEADS, CELLS, LANES),
             out(CELLS, C, dtype=f32),
             out(CELLS, C),
             out(CELLS, C, dtype=f32),
             out(9, CELLS, WIDE),
         ),
         (
-            place, valid_rows, condition_here, top, bottom, left, right, latent_here, w_in_here,
-            b_in_here, taps_here, b_conv_here, w_out_here, b_out_here, w_query_here, w_key_here,
-            w_value_here,
+            place, valid_rows, cells, beside, left, right, w_in_here, b_in_here, taps_here,
+            b_conv_here, w_out_here, b_out_here, w_query_here, w_key_here, w_value_here,
         ),
         "adapter",
         scalars=2,
         scratch=[pltpu.VMEM((WIDE, C), bf16)],
         vmem=24,
-        store=(0, 1, 2, 3, 4),
-        held=(2,) + tuple(range(7, 17)),
-    )
-
-    rows, text = after(rows, text_states)
-    text_keys, text_values = call(
-        text_kernel,
-        (out(ITEMS, TEXT, 2 * WIDE), out(ITEMS, TEXT, 2 * WIDE)),
-        (text.transpose(1, 0, 2).reshape(-1, text.shape[2]), w_cross_key.T, w_cross_value.T),
-        "text",
-        scratch=[pltpu.VMEM((2 * WIDE, text.shape[2]), bf16)] * 2,
-        fetch=(1, 2, 0),
-        store=(0, 1),
-    )
-    own = across(rows.reshape(CHIPS, PART, LANES)).reshape(HALF, LANES)
-    own, text_keys = after(own, text_keys)
+        store=(1, 2, 3, 4),
+        near=(0,),
+        held=tuple(range(6, 15)),
+    )
+
+    own = across(rows, GROUP_OF_ITEM).reshape(HALF, LANES)
 
     other = swap(own)
     _, attn_weight = after(own, w_attn_out)
@@ -785,26 +783,26 @@
         far=(4,),
     )
 
-    heads_in = across(packed).reshape(ITEMS, HEADS, PART // 2, LANES)
+    heads_in = across(packed.reshape(HEADS, CELLS // 2, LANES), GROUP_OF_ITEM)
     result, grad_first, heads_out = call(
         middle_kernel,
-        (out(CELLS, C), out(CELLS, C, dtype=f32), out(ITEMS, HEADS, PART // 2, LANES)),
+        (out(CELLS, C), out(CELLS, C, dtype=f32), out(HEADS, CELLS // 2, LANES)),
         (
-            text_lengths, heads_in, mixed, cotangent.reshape(CELLS, C), text_keys, text_values,
+            place, text_lengths, heads_in, mixed, cells, text_keys, text_values,
             w_attn_spread, b_attn_out, w_cross_query_wide, w_cross_out_wide, b_cross_out,
             w_ff_in, b_ff_in, w_ff_out.T, b_ff_out,
         ),
         "middle",
-        scalars=1,
-        scratch=[pltpu.VMEM((ITEMS, HEADS * PART, TEXT), f32)],
+        scalars=2,
+        scratch=[pltpu.VMEM((CELLS, HEADS * TEXT), f32)],
         vmem=32,
-        fetch=(2, 7, 8, 4, 5, 9, 10, 3, 11, 12, 13, 14),
+        fetch=(3, 8, 9, 5, 6, 10, 11, 12, 13, 14, 15),
         store=(0, 1),
         near=(2,),
-        held=(6,),
-    )
-
-    grads_in = across(heads_out.reshape(CHIPS, PART // 2, LANES))
+        held=(7,),
+    )
+
+    grads_in = across(heads_out, GROUP_OF_ITEM).reshape(CHIPS, PART // 2, LANES)
     own_grads, other_grads = call(
         attend_back_kernel,
         (out(HALF, LANES, dtype=f32), out(HALF, LANES)),
@@ -835,13 +833,12 @@
     )
     own_grads, w_joined = after(own_grads, w_joined)
     row_grads = (own_grads + swap(other_grads).astype(f32)).astype(bf16)
-    row_grads = across(row_grads.reshape(CHIPS, PART, LANES))
-    latent_grad, parts = call(
+    row_grads = across(row_grads.reshape(HEADS, CELLS, LANES), GROUP_OF_ITEM)
+    back, parts = call(
         finish_kernel,
-        (out(CELLS, C, dtype=f32), out(2, SUM_ROWS, LANES)),
+        (out(STRIPS, PART, 768), out(2, SUM_ROWS, LANES)),
         (
-            place, row_grads.reshape(ITEMS, HEADS, PART, LANES), w_joined, mixed, grad_first,
-            slope, smooth, cond, w_out,
+            place, row_grads, w_joined, mixed, grad_first, slope, smooth, cond, w_out, result,
         ),
         "finish",
         scalars=1,
@@ -849,17 +846,13 @@
     )
 
     shares = (parts[0].astype(f32) + swap(parts[1]).astype(f32)).astype(bf16)
-    shares, last_bias = after(shares, b_in)
-    taps_last, w_turned = bring(
-        [w_conv.reshape(9, C, C)],
-        "load_weights",
-        widen_kernel,
-        (out(C, WIDE),),
-        (w_in, last_bias),
-    )
-    shares = across(shares.reshape(CHIPS, SUM_ROWS // CHIPS, LANES))
+    shares = across(shares.reshape(CHIPS, SUM_ROWS // CHIPS, LANES), CHIPS_ALL)
     share = jnp.sum(shares.astype(f32), axis=0).astype(bf16)
-    mine = across(jnp.broadcast_to(share[None], shares.shape)).reshape(SUM_ROWS, LANES)
+    mine = across(jnp.broadcast_to(share[None], shares.shape), CHIPS_ALL)
+    mine = mine.reshape(SUM_ROWS, LANES)
+
+    mine, back = after(mine, back)
+    back = across(back, "a")
     theirs = swap(mine)
     grad_w_in, grad_b_in, grad_w_conv, grad_b_conv, grad_w_out, grad_b_out = call(
         weights_kernel,
@@ -871,7 +864,7 @@
             out(C, C, dtype=f32),
             out(C, dtype=f32),
         ),
-        (place, mine, theirs, w_turned, taps_last),
+        (place, mine, theirs, w_turned, w_conv.reshape(9, C, C)),
         "weights",
         scalars=1,
         scratch=[
@@ -879,14 +872,16 @@
             pltpu.SemaphoreType.DMA((9,)),
         ],
         vmem=24,
+        fetch=(3, 4),
         store=(0, 4),
         far=(7,),
-        held=(3, 4),
-    )
-    grid = (ITEMS, ROWS, COLS, C)
+        cost=pl.CostEstimate(flops=6 * 10**9, bytes_accessed=2 * 10**7, transcendentals=0),
+    )
+    back, grad_b_in = after(back, grad_b_in)
+    grid = (STRIPS, ROWS, COLS, C)
     return (
-        result.reshape(grid),
-        latent_grad.reshape(grid),
+        back[:, :, :C].reshape(grid),
+        back[:, :, 384 : 384 + C].reshape(grid).astype(f32),
         grad_w_in,
         grad_b_in,
         grad_w_conv.reshape(3, 3, C, C),
@@ -897,8 +892,8 @@
 
 
 def solution(mesh):
-    split = Mesh(mesh.devices.reshape(16, 4, 2), ("sp", "x", "c"))
-    cells = P(None, "sp", ("x", "c"), None)
+    split = Mesh(mesh.devices.reshape(8, 2, 4, 2), ("a", "b", "x", "c"))
+    cells = P(None, ("a", "b"), ("x", "c"), None)
     in_specs = (cells, cells) + (P(),) * 23 + (cells,)
     out_specs = (cells, cells) + (P(),) * 6
     return jax.shard_map(

time: 199 us -> 193 us (0.970)
  starting transfers between devices: 35.2 us -> 27.1 us
  waiting for transfers between devices: 7.9 us -> 15.7 us
  Pallas kernels: 67.9 us -> 60.4 us
  other arithmetic: 0.56 us -> 3.49 us
    pallas_call x9 -> x10, Pallas kernels: 64.2 us -> 58.3 us  [call(): pl.pallas_call(body, out_shape=tuple((made_as(i, made) for i, made in enu...]
    ppermute x2 -> x1, starting transfers between devices: 5.94 us -> 0.48 us  [per_device(): beside = lax.ppermute(ends, 'b', [(0, 1), (1, 0)])]
    all_to_all x1 -> x2, waiting for transfers between devices: 4.75 us -> 9.97 us  [across(): return lax.all_to_all(blocks, axes, 0, 0, tiled=True)]
    ppermute x2 -> x1, waiting for transfers between devices: 0.01 us -> 2.7 us  [per_device(): beside = lax.ppermute(ends, 'b', [(0, 1), (1, 0)])]
    ppermute x4, starting transfers between devices: 8.97 us -> 6.71 us  [swap(): return lax.ppermute(array, 'c', [(0, 1), (1, 0)])]
    concatenate x2 -> x4, other arithmetic: 0.02 us -> 2.07 us  [the longest x1 2.05 us: per_device(): cells = across(jnp.concatenate(wide, axis=-1), 'a')]
    all_to_all x1 -> x2, starting transfers between devices: 13.5 us -> 11.9 us  [across(): return lax.all_to_all(blocks, axes, 0, 0, tiled=True)]
    all_to_all x5 -> x6, blocking collectives: 83.4 us -> 83.5 us  [across(): return lax.all_to_all(blocks, axes, 0, 0, tiled=True)]
  transfers between devices with their start and end apart: 9 -> 9, of which waited for: 4 -> 5; matrix products, arithmetic and copies ran while one was open for 1% -> 1% of each run, Pallas kernels for 8% -> 8%
where the time goes in v3:
time: 193 us
  blocking collectives  83.5 us (43%)
  Pallas kernels  60.4 us (31%)
  starting transfers between devices  27.1 us (14%)
  waiting for transfers between devices  15.7 us (8%)
  other arithmetic  3.49 us (2%)
    all_to_all x6, blocking collectives, across(): return lax.all_to_all(blocks, axes, 0, 0, tiled=True)  83.5 us
    pallas_call x10, Pallas kernels, call(): pl.pallas_call(body, out_shape=tuple((made_as(i, made) for i, made in enu...  58.3 us
    all_to_all x2, starting transfers between devices, across(): return lax.all_to_all(blocks, axes, 0, 0, tiled=True)  11.9 us
    all_to_all x2, waiting for transfers between devices, across(): return lax.all_to_all(blocks, axes, 0, 0, tiled=True)  9.97 us
    ppermute x4, starting transfers between devices, swap(): return lax.ppermute(array, 'c', [(0, 1), (1, 0)])  6.71 us
    ppermute x1, starting transfers between devices, per_device(): left = lax.ppermute(edge(COLS - 1), ('x', 'c'), right_way)  6.02 us
  transfers between devices with their start and end apart: 9, of which 5 were waited for; matrix products, arithmetic and copies ran while one was open for 1% of the time, Pallas kernels for 8%

profile of v3, /device:TPU:1, one launch (start us, length us, event | category | flops | bytes accessed | tf_op | source)
XLA Modules:
  0.0 192.6 jit_solution(2776801681641935327)
XLA Ops:
  0.6 2.0 %fusion.6 = bf16[8,32,1024]{2,1,0:T(8,128)(2,1)} fusion(bf16[8,32,320]{2,1,0:T(8,128)(2,1)} %bitcast.53, bf16[8,32,320]{2,1,0:T(8,128)(2,1)} %bitcast.54, bf16[8,32,192]{2,1,0:T(8,128)(2,1)} %bitcast.55), kind=kLoop, calls=%fused_computation.13 | loop fusion | flops 3670016 | bytes 950272 | tf_op jit(solution)/shard_map/concatenate | solution.py:682
  2.7 8.5 %all-to-all-start = ((bf16[8,32,1024]{2,1,0:T(8,128)(2,1)}), bf16[8,32,1024]{2,1,0:T(8,128)(2,1)S(1)}, u32[]{:S(2)}, u32[]{:S(2)}) async-start(bf16[8,32,1024]{2,1,0:T(8,128)(2,1)} %fusion.6), calls=%async_computation | async-start | bytes 1048576 | tf_op jit(solution)/shard_map/all_to_all | solution.py:666
  13.9 2.6 %text.1 = (bf16[128,512]{1,0:T(8,128)(2,1)}, bf16[128,512]{1,0:T(8,128)(2,1)}) custom-call(bf16[128,768]{1,0:T(8,128)(2,1)} %pad.18.refs_0_, bf16[320,768]{1,0:T(8,128)(2,1)} %bitcast.56, bf16[320,768]{1,0:T(8,128)(2,1)} %bitcast.57), custom_call_target="tpu_custom_call" | custom-call | flops 4000000000 | bytes 2000000 | tf_op jit(solution)/shard_map/text/pallas_call | solution.py:133
  16.5 5.3 %all-to-all-done.refs_2_.refs_4_ = bf16[8,32,1024]{2,1,0:T(8,128)(2,1)S(1)} async-done(((bf16[8,32,1024]{2,1,0:T(8,128)(2,1)}), bf16[8,32,1024]{2,1,0:T(8,128)(2,1)S(1)}, u32[]{:S(2)}, u32[]{:S(2)}) %all-to-all-start) | async-done | bytes 524320 | tf_op jit(solution)/shard_map/all_to_all | solution.py:666
  22.5 2.7 %collective-permute-done.refs_3_ = bf16[8,2,8,256]{3,2,1,0:T(8,128)(2,1)S(1)} collective-permute-done((bf16[8,2,8,256]{3,2,1,0:T(8,128)(2,1)S(1)}, bf16[8,2,8,256]{3,2,1,0:T(8,128)(2,1)S(1)}, u32[]{:S(2)}, u32[]{:S(2)}) %collective-permute-start) | collective-permute-done | bytes 65568 | tf_op jit(solution)/shard_map/ppermute | solution.py:703
  25.3 6.0 %collective-permute-start.1 = (bf16[48,256]{1,0:T(8,128)(2,1)S(1)}, bf16[48,256]{1,0:T(8,128)(2,1)S(1)}, u32[]{:S(2)}, u32[]{:S(2)}) collective-permute-start(bf16[48,256]{1,0:T(8,128)(2,1)S(1)} %reshape.72), channel_id=1, source_target_pairs={{0,1},{1,2},{2,3},{3,4},{4,5},{5,6},{6,7},{8,9},{9,10},{10,11},{11... | collective-permute-start | bytes 73736 | tf_op jit(solution)/shard_map/ppermute | solution.py:710
  33.4 2.0 %load_adapter.1 = (bf16[192,320]{1,0:T(8,128)(2,1)S(1)}, f32[320]{0:T(512)S(1)}, bf16[9,320,320]{2,1,0:T(8,128)(2,1)S(1)}, f32[320]{0:T(512)S(1)}, bf16[320,320]...) custom-call(bf16[192,320]{1,0:T(8,128)(2,1)} %refs_0_.4, ...), custom_call_target="tpu_custom_call" | custom-call | tf_op jit(solution)/shard_map/load_adapter/pallas_call | solution.py:169
  36.5 4.6 %adapter.1 = (bf16[8,256,128]{2,1,0:T(8,128)(2,1)S(1)}, f32[256,320]{1,0:T(8,128)}, bf16[256,320]{1,0:T(8,128)(2,1)}, f32[256,320]{1,0:T(8,128)}, bf16[9,256,256]{2,1,0:T(8,128)(2,1)}) custom-call(s32[4]{0:T(128)S(1)} %pad_add_fusion.refs_0_, s32[8]{0:T(128)S(1)} %copy-done.11, bf16[8,32,1024]{2,1,0:T(8,128)(2,1)S(1)} %all-to-all-done.refs_2_.refs_4_, ...), custom_call_target="tpu_custom_call" | custom-call | tf_op jit(solution)/shard_map/adapter/pallas_call | solution.py:133
  41.1 13.9 %all_to_all.40 = bf16[8,256,128]{2,1,0:T(8,128)(2,1)S(1)} all-to-all(bf16[8,256,128]{2,1,0:T(8,128)(2,1)S(1)} %get-tuple-element.73), channel_id=1, replica_groups=mesh['a'=8,'b'=2,'x'=4,'c'=2] {'b','x'}, dimensions={0} | all-to-all | bytes 1048576 | tf_op jit(solution)/shard_map/all_to_all | solution.py:666
  55.8 2.1 %form.1 = (bf16[320,512]{1,0:T(8,128)(2,1)}, bf16[512,320]{1,0:T(8,128)(2,1)}, bf16[1024,768]{1,0:T(8,128)(2,1)S(1)}) custom-call(bf16[320,320]{1,0:T(8,128)(2,1)} %refs_0_.5, bf16[320,320]{1,0:T(8,128)(2,1)} %refs_1_.8, bf16[320,320]{1,0:T(8,128)(2,1)} %refs_2_.1), custom_call_target="tpu_custom_call" | custom-call | tf_op jit(solution)/shard_map/form/pallas_call | solution.py:133
  57.9 11.8 %attend.1 = (bf16[64,16,128]{2,1,0:T(8,128)(2,1)S(1)}, f32[2048,128]{1,0:T(8,128)}, bf16[2048,4096]{1,0:T(8,128)(2,1)}, bf16[128,4096]{1,0:T(8,128)(2,1)}, bf16[128,2048]{1,0:T(8,128)(2,1)}) custom-call(bf16[2048,128]{1,0:T(8,128)(2,1)S(1)} %bitcast.42, bf16[2048,128]{1,0:T(8,128)(2,1)S(1)} %collective-permute-done.3.refs_1_), custom_call_target="tpu_custom_call" | custom-call | tf_op jit(solution)/shard_map/attend/pallas_call | solution.py:133
  69.7 9.9 %all_to_all.41.refs_2_ = bf16[8,128,128]{2,1,0:T(8,128)(2,1)S(1)} all-to-all(bf16[8,128,128]{2,1,0:T(8,128)(2,1)S(1)} %bitcast.46), channel_id=1, replica_groups=mesh['a'=8,'b'=2,'x'=4,'c'=2] {'b','x'}, dimensions={0} | all-to-all | bytes 524288 | tf_op jit(solution)/shard_map/all_to_all | solution.py:666
  79.6 9.3 %middle.1 = (bf16[256,320]{1,0:T(8,128)(2,1)}, f32[256,320]{1,0:T(8,128)}, bf16[8,128,128]{2,1,0:T(8,128)(2,1)S(1)}) custom-call(s32[4]{0:T(128)S(1)} %pad_add_fusion.refs_0_, s32[8]{0:T(128)S(1)} %copy-done.12, bf16[8,128,128]{2,1,0:T(8,128)(2,1)S(1)} %all_to_all.41.refs_2_, f32[256,320]{1,0:T(8,128)} %get-tuple-element.81.refs_3_, ...), custom_call_target="tpu_custom_call" | custom-call | tf_op jit(solution)/shard_map/middle/pallas_call | solution.py:133
  88.9 8.7 %all_to_all.42 = bf16[8,128,128]{2,1,0:T(8,128)(2,1)S(1)} all-to-all(bf16[8,128,128]{2,1,0:T(8,128)(2,1)S(1)} %get-tuple-element.87), channel_id=1, replica_groups=mesh['a'=8,'b'=2,'x'=4,'c'=2] {'b','x'}, dimensions={0} | all-to-all | bytes 524288 | tf_op jit(solution)/shard_map/all_to_all | solution.py:666
  97.7 16.0 %attend_back.1 = (f32[2048,128]{1,0:T(8,128)S(1)}, bf16[2048,128]{1,0:T(8,128)(2,1)S(1)}) custom-call(bf16[128,4096]{1,0:T(8,128)(2,1)S(1)} %copy-done.4, bf16[128,2048]{1,0:T(8,128)(2,1)S(1)} %copy-done.6, f32[2048,128]{1,0:T(8,128)S(1)} %copy-done.3, bf16[64,16,128]{2,1,0:T(8,128)(2,1)S(1)} %bitcast.43, bf16[2048,4096]{1,0:T(8,128)(2,1)} %get-tuple-element.88.refs_4_), custom_call_target="tpu_custom_call" | custom-call | tf_op jit(solution)/shard_map/attend_back/pallas_call | solution.py:133
  113.6 2.0 %collective-permute-start.4 = (bf16[2048,128]{1,0:T(8,128)(2,1)S(1)}, bf16[2048,128]{1,0:T(8,128)(2,1)S(1)}, u32[]{:S(2)}, u32[]{:S(2)}) collective-permute-start(bf16[2048,128]{1,0:T(8,128)(2,1)S(1)} %get-tuple-element.90), channel_id=1, source_target_pairs={{0,1},{1,0},{2,3},{3,2},{4,5},{5,4},{6,7},{7,6},{8,9},{9,8},{10,11... | collective-permute-start | bytes 1572872 | tf_op jit(solution)/shard_map/ppermute | solution.py:662
  117.8 12.9 %all_to_all.43.refs_1_ = bf16[8,256,128]{2,1,0:T(8,128)(2,1)S(1)} all-to-all(bf16[8,256,128]{2,1,0:T(8,128)(2,1)S(1)} %bitcast.50), channel_id=1, replica_groups=mesh['a'=8,'b'=2,'x'=4,'c'=2] {'b','x'}, dimensions={0} | all-to-all | bytes 1048576 | tf_op jit(solution)/shard_map/all_to_all | solution.py:666
  130.7 2.7 %finish.1 = (bf16[8,32,768]{2,1,0:T(8,128)(2,1)}, bf16[2,3072,128]{2,1,0:T(8,128)(2,1)S(1)}) custom-call(s32[4]{0:T(128)S(1)} %pad_add_fusion.refs_0_, bf16[8,256,128]{2,1,0:T(8,128)(2,1)S(1)} %all_to_all.43.refs_1_, bf16[320,1024]{1,0:T(8,128)(2,1)S(1)} %join.1.refs_2_, f32[256,320]{1,0:T(8,128)S(1)} %copy-done.1, f32[256,320]{1,0:T(8,128)S(1)} %copy-done.8, ...), custom_call_target="tpu_custom_call" | custom-call | tf_op jit(solution)/shard_map/finish/pallas_call | solution.py:133
  136.4 19.6 %all_to_all.44 = bf16[64,48,128]{2,1,0:T(8,128)(2,1)S(1)} all-to-all(bf16[64,48,128]{2,1,0:T(8,128)(2,1)S(1)} %bitcast.47), channel_id=1, replica_groups=mesh['a'=8,'b'=2,'x'=4,'c'=2] {'a','b','x'}, dimensions={0} | all-to-all | bytes 1572864 | tf_op jit(solution)/shard_map/all_to_all | solution.py:666
  156.3 18.6 %all_to_all.45 = bf16[64,48,128]{2,1,0:T(8,128)(2,1)S(1)} all-to-all(bf16[64,48,128]{2,1,0:T(8,128)(2,1)S(1)} %broadcast_in_dim.2), channel_id=1, replica_groups=mesh['a'=8,'b'=2,'x'=4,'c'=2] {'a','b','x'}, dimensions={0} | all-to-all | bytes 1572864 | tf_op jit(solution)/shard_map/all_to_all | solution.py:666
  174.8 3.1 %collective-permute-start.6 = (bf16[3072,128]{1,0:T(8,128)(2,1)S(1)}, bf16[3072,128]{1,0:T(8,128)(2,1)S(1)}, u32[]{:S(2)}, u32[]{:S(2)}) collective-permute-start(bf16[3072,128]{1,0:T(8,128)(2,1)S(1)} %bitcast.44), channel_id=1, source_target_pairs={{0,1},{1,0},{2,3},{3,2},{4,5},{5,4},{6,7},{7,6},{8,9},{9,8},{10,11... | collective-permute-start | bytes 2359304 | tf_op jit(solution)/shard_map/ppermute | solution.py:662
  178.0 3.5 %all-to-all-start.7 = ((bf16[8,32,768]{2,1,0:T(8,128)(2,1)}), bf16[8,32,768]{2,1,0:T(8,128)(2,1)S(1)}, u32[]{:S(2)}, u32[]{:S(2)}) async-start(bf16[8,32,768]{2,1,0:T(8,128)(2,1)} %get-tuple-element.101), calls=%async_computation.7 | async-start | bytes 786432 | tf_op jit(solution)/shard_map/all_to_all | solution.py:666
  181.4 5.6 %weights.1 = (f32[192,320]{1,0:T(8,128)}, f32[320]{0:T(512)}, f32[9,320,320]{2,1,0:T(8,128)}, f32[320]{0:T(512)}, f32[320,320]{1,0:T(8,128)}, /*index=5*/f32[320]{0:T(512)}) custom-call(s32[4]{0:T(128)S(1)} %pad_add_fusion.refs_0_, bf16[3072,128]{1,0:T(8,128)(2,1)S(1)} %bitcast.45, bf16[3072,128]{1,0:T(8,128)(2,1)S(1)} %collective-permute-done.6.refs_2_, ...), custom_call_target="tpu_custom_call" | custom-call | flops 6000000000 | bytes 20000000 | tf_op jit(solution)/shard_map/weights/pallas_call | solution.py:133
  187.1 4.6 %all-to-all-done.7 = bf16[8,32,768]{2,1,0:T(8,128)(2,1)S(1)} async-done(((bf16[8,32,768]{2,1,0:T(8,128)(2,1)}), bf16[8,32,768]{2,1,0:T(8,128)(2,1)S(1)}, u32[]{:S(2)}, u32[]{:S(2)}) %all-to-all-start.7) | async-done | bytes 393248 | tf_op jit(solution)/shard_map/all_to_all | solution.py:666
  (61 shorter events, 13.3 us)
Async XLA Ops:
  0.6 10.6 %copy-start = (bf16[8,77,768]{2,0,1:T(8,128)(2,1)S(1)}, bf16[8,77,768]{2,0,1:T(8,128)(2,1)}, u32[]{:S(2)}) copy-start(bf16[8,77,768]{2,0,1:T(8,128)(2,1)} %param.28) | copy-start | bytes 2838532
  2.7 19.2 %all-to-all-start = ((bf16[8,32,1024]{2,1,0:T(8,128)(2,1)}), bf16[8,32,1024]{2,1,0:T(8,128)(2,1)S(1)}, u32[]{:S(2)}, u32[]{:S(2)}) async-start(bf16[8,32,1024]{2,1,0:T(8,128)(2,1)} %fusion.6), calls=%async_computation | async-start | bytes 1048576 | tf_op jit(solution)/shard_map/all_to_all | solution.py:666
  22.0 3.2 %collective-permute-start = (bf16[8,2,8,256]{3,2,1,0:T(8,128)(2,1)S(1)}, bf16[8,2,8,256]{3,2,1,0:T(8,128)(2,1)S(1)}, u32[]{:S(2)}, u32[]{:S(2)}) collective-permute-start(bf16[8,2,8,256]{3,2,1,0:T(8,128)(2,1)S(1)} %pad_maximum_fusion), channel_id=1, source_target_pairs={{0,8},{8,0},{1,9},{9,1},{2,10},{10,2},{3,11},{11,3},{4,12},{12,4},... | collective-permute-start | bytes 196616 | tf_op jit(solution)/shard_map/ppermute | solution.py:703
  25.3 10.1 %collective-permute-start.1 = (bf16[48,256]{1,0:T(8,128)(2,1)S(1)}, bf16[48,256]{1,0:T(8,128)(2,1)S(1)}, u32[]{:S(2)}, u32[]{:S(2)}) collective-permute-start(bf16[48,256]{1,0:T(8,128)(2,1)S(1)} %reshape.72), channel_id=1, source_target_pairs={{0,1},{1,2},{2,3},{3,4},{4,5},{5,6},{6,7},{8,9},{9,10},{10,11},{11... | collective-permute-start | bytes 73736 | tf_op jit(solution)/shard_map/ppermute | solution.py:710
  31.3 5.1 %collective-permute-start.2 = (bf16[48,256]{1,0:T(8,128)(2,1)S(1)}, bf16[48,256]{1,0:T(8,128)(2,1)S(1)}, u32[]{:S(2)}, u32[]{:S(2)}) collective-permute-start(bf16[48,256]{1,0:T(8,128)(2,1)S(1)} %reshape.73), channel_id=1, source_target_pairs={{1,0},{2,1},{3,2},{4,3},{5,4},{6,5},{7,6},{9,8},{10,9},{11,10},{12... | collective-permute-start | bytes 73736 | tf_op jit(solution)/shard_map/ppermute | solution.py:711
  33.4 3.1 %copy-start.11 = (s32[8]{0:T(128)S(1)}, s32[8]{0:T(128)}, u32[]{:S(2)}) copy-start(s32[8]{0:T(128)} %refs_1_.7) | copy-start | bytes 100
  41.1 38.5 %copy-start.12 = (s32[8]{0:T(128)S(1)}, s32[8]{0:T(128)}, u32[]{:S(2)}) copy-start(s32[8]{0:T(128)} %refs_1_.9) | copy-start | bytes 100
  55.0 2.8 %collective-permute-start.3 = (bf16[2048,128]{1,0:T(8,128)(2,1)S(1)}, bf16[2048,128]{1,0:T(8,128)(2,1)S(1)}, u32[]{:S(2)}, u32[]{:S(2)}) collective-permute-start(bf16[2048,128]{1,0:T(8,128)(2,1)S(1)} %bitcast.41), channel_id=1, source_target_pairs={{0,1},{1,0},{2,3},{3,2},{4,5},{5,4},{6,7},{7,6},{8,9},{9,8},{10,11... | collective-permute-start | bytes 1572872 | tf_op jit(solution)/shard_map/ppermute | solution.py:662
  79.6 18.0 %copy-start.3 = (f32[2048,128]{1,0:T(8,128)S(1)}, f32[2048,128]{1,0:T(8,128)}, u32[]{:S(2)}) copy-start(f32[2048,128]{1,0:T(8,128)} %get-tuple-element.79.refs_2_) | copy-start | bytes 3145732
  79.6 18.0 %copy-start.4 = (bf16[128,4096]{1,0:T(8,128)(2,1)S(1)}, bf16[128,4096]{1,0:T(8,128)(2,1)}, u32[]{:S(2)}) copy-start(bf16[128,4096]{1,0:T(8,128)(2,1)} %get-tuple-element.77.refs_0_) | copy-start | bytes 3145732
  79.6 18.0 %copy-start.6 = (bf16[128,2048]{1,0:T(8,128)(2,1)S(1)}, bf16[128,2048]{1,0:T(8,128)(2,1)}, u32[]{:S(2)}) copy-start(bf16[128,2048]{1,0:T(8,128)(2,1)} %get-tuple-element.78.refs_1_) | copy-start | bytes 1572868
  113.6 4.0 %collective-permute-start.4 = (bf16[2048,128]{1,0:T(8,128)(2,1)S(1)}, bf16[2048,128]{1,0:T(8,128)(2,1)S(1)}, u32[]{:S(2)}, u32[]{:S(2)}) collective-permute-start(bf16[2048,128]{1,0:T(8,128)(2,1)S(1)} %get-tuple-element.90), channel_id=1, source_target_pairs={{0,1},{1,0},{2,3},{3,2},{4,5},{5,4},{6,7},{7,6},{8,9},{9,8},{10,11... | collective-permute-start | bytes 1572872 | tf_op jit(solution)/shard_map/ppermute | solution.py:662
  117.5 13.1 %copy-start.1 = (f32[256,320]{1,0:T(8,128)S(1)}, f32[256,320]{1,0:T(8,128)}, u32[]{:S(2)}) copy-start(f32[256,320]{1,0:T(8,128)} %get-tuple-element.81.refs_3_) | copy-start | bytes 983044
  117.6 13.1 %copy-start.2 = (bf16[9,256,256]{2,1,0:T(8,128)(2,1)S(1)}, bf16[9,256,256]{2,1,0:T(8,128)(2,1)}, u32[]{:S(2)}) copy-start(bf16[9,256,256]{2,1,0:T(8,128)(2,1)} %get-tuple-element.97.refs_7_) | copy-start | bytes 3538948
  117.6 13.1 %copy-start.5 = (bf16[320,320]{1,0:T(8,128)(2,1)S(1)}, bf16[320,320]{1,0:T(8,128)(2,1)}, u32[]{:S(2)}) copy-start(bf16[320,320]{1,0:T(8,128)(2,1)} %refs_8_.5) | copy-start | bytes 614404
  117.6 13.1 %copy-start.7 = (f32[256,320]{1,0:T(8,128)S(1)}, f32[256,320]{1,0:T(8,128)}, u32[]{:S(2)}) copy-start(f32[256,320]{1,0:T(8,128)} %get-tuple-element.95.refs_5_) | copy-start | bytes 983044
  117.6 13.1 %copy-start.8 = (f32[256,320]{1,0:T(8,128)S(1)}, f32[256,320]{1,0:T(8,128)}, u32[]{:S(2)}) copy-start(f32[256,320]{1,0:T(8,128)} %get-tuple-element.94.refs_4_) | copy-start | bytes 983044
  117.6 13.1 %copy-start.9 = (bf16[256,320]{1,0:T(8,128)(2,1)S(1)}, bf16[256,320]{1,0:T(8,128)(2,1)}, u32[]{:S(2)}) copy-start(bf16[256,320]{1,0:T(8,128)(2,1)} %get-tuple-element.96.refs_6_) | copy-start | bytes 491524
  117.6 13.1 %copy-start.10 = (bf16[256,320]{1,0:T(8,128)(2,1)S(1)}, bf16[256,320]{1,0:T(8,128)(2,1)}, u32[]{:S(2)}) copy-start(bf16[256,320]{1,0:T(8,128)(2,1)} %get-tuple-element.98.refs_9_) | copy-start | bytes 491524
  133.5 2.7 %collective-permute-start.5 = (bf16[3072,128]{1,0:T(8,128)(2,1)S(1)}, bf16[3072,128]{1,0:T(8,128)(2,1)S(1)}, u32[]{:S(2)}, u32[]{:S(2)}) collective-permute-start(bf16[3072,128]{1,0:T(8,128)(2,1)S(1)} %slice_bitcast_fusion), channel_id=1, source_target_pairs={{0,1},{1,0},{2,3},{3,2},{4,5},{5,4},{6,7},{7,6},{8,9},{9,8},{10,11... | collective-permute-start | bytes 2359304 | tf_op jit(solution)/shard_map/ppermute | solution.py:662
  174.8 6.6 %collective-permute-start.6 = (bf16[3072,128]{1,0:T(8,128)(2,1)S(1)}, bf16[3072,128]{1,0:T(8,128)(2,1)S(1)}, u32[]{:S(2)}, u32[]{:S(2)}) collective-permute-start(bf16[3072,128]{1,0:T(8,128)(2,1)S(1)} %bitcast.44), channel_id=1, source_target_pairs={{0,1},{1,0},{2,3},{3,2},{4,5},{5,4},{6,7},{7,6},{8,9},{9,8},{10,11... | collective-permute-start | bytes 2359304 | tf_op jit(solution)/shard_map/ppermute | solution.py:662
  178.0 13.7 %all-to-all-start.7 = ((bf16[8,32,768]{2,1,0:T(8,128)(2,1)}), bf16[8,32,768]{2,1,0:T(8,128)(2,1)S(1)}, u32[]{:S(2)}, u32[]{:S(2)}) async-start(bf16[8,32,768]{2,1,0:T(8,128)(2,1)} %get-tuple-element.101), calls=%async_computation.7 | async-start | bytes 786432 | tf_op jit(solution)/shard_map/all_to_all | solution.py:666

commit v4 on v3

--- a/solution.py
+++ b/solution.py
@@ -23,6 +23,7 @@
 GROUP_OF_ITEM, CHIPS_ALL = ("b", "x"), ("a", "b", "x")
 LATENT, COTANGENT = 256, 640
 SUM_ROWS = 3072
+SHARE = SUM_ROWS // CHIPS
 
 bf16, f32 = jnp.bfloat16, jnp.float32
 NT = (((1,), (1,)), ((), ()))
@@ -568,6 +569,15 @@
         joined_out[:, head * LANES : (head + 1) * LANES] = joined.astype(bf16)
 
 
+def unpack_kernel(parcel, result_out, latent_out):
+    for item in range(STRIPS):
+        tiles = [
+            parcel[item, SHARE + PART * t : SHARE + PART * (t + 1), :] for t in range(6)
+        ]
+        result_out[item] = jnp.concatenate(tiles[:3], axis=1)[:, :C]
+        latent_out[item] = jnp.concatenate(tiles[3:], axis=1)[:, :C].astype(f32)
+
+
 def widen_kernel(w_in, b_in, turned_out):
     wide = jnp.concatenate([w_in[...], bias_rows(b_in[...])], axis=0)
     turned_out[...] = jnp.transpose(wide)
@@ -582,7 +592,8 @@
     branch = latent.astype(bf16)
     blank = jnp.zeros((CELLS, 384 - C), bf16)
     back = jnp.concatenate([result[...], blank, branch, blank], axis=1)
-    back_out[...] = back.reshape(STRIPS, PART, 768)
+    for t in range(6):
+        back_out[:, t] = back[:, t * LANES : (t + 1) * LANES].reshape(STRIPS, PART, LANES)
     inner = (dot_nt(branch, w_out[...]) * slope[...]).astype(bf16)
     inner_turned = jnp.transpose(inner)
     branch_turned = jnp.transpose(branch)
@@ -836,7 +847,7 @@
     row_grads = across(row_grads.reshape(HEADS, CELLS, LANES), GROUP_OF_ITEM)
     back, parts = call(
         finish_kernel,
-        (out(STRIPS, PART, 768), out(2, SUM_ROWS, LANES)),
+        (out(STRIPS, 6, PART, LANES), out(2, SUM_ROWS, LANES)),
         (
             place, row_grads, w_joined, mixed, grad_first, slope, smooth, cond, w_out, result,
         ),
@@ -846,14 +857,25 @@
     )
 
     shares = (parts[0].astype(f32) + swap(parts[1]).astype(f32)).astype(bf16)
-    shares = across(shares.reshape(CHIPS, SUM_ROWS // CHIPS, LANES), CHIPS_ALL)
+    shares = shares.reshape(8, 8, SHARE, LANES).transpose(1, 0, 2, 3)
+    shares = across(shares.reshape(CHIPS, SHARE, LANES), CHIPS_ALL)
     share = jnp.sum(shares.astype(f32), axis=0).astype(bf16)
-    mine = across(jnp.broadcast_to(share[None], shares.shape), CHIPS_ALL)
-    mine = mine.reshape(SUM_ROWS, LANES)
-
-    mine, back = after(mine, back)
-    back = across(back, "a")
+
+    sums = jnp.broadcast_to(share[None], (STRIPS, SHARE, LANES))
+    parcel = jnp.concatenate([sums, back.reshape(STRIPS, 6 * PART, LANES)], axis=1)
+    parcel = across(parcel, "a")
+    sums = parcel[:, :SHARE].reshape(1, STRIPS * SHARE, LANES)
+    sums = jnp.broadcast_to(sums, (HEADS,) + sums.shape[1:])
+    mine = across(sums, GROUP_OF_ITEM).reshape(SUM_ROWS, LANES)
+    mine, parcel = after(mine, parcel)
     theirs = swap(mine)
+    result, latent_grad = call(
+        unpack_kernel,
+        (out(STRIPS, PART, C), out(STRIPS, PART, C, dtype=f32)),
+        (parcel,),
+        "unpack",
+        store=(0, 1),
+    )
     grad_w_in, grad_b_in, grad_w_conv, grad_b_conv, grad_w_out, grad_b_out = call(
         weights_kernel,
         (
@@ -877,11 +899,10 @@
         far=(7,),
         cost=pl.CostEstimate(flops=6 * 10**9, bytes_accessed=2 * 10**7, transcendentals=0),
     )
-    back, grad_b_in = after(back, grad_b_in)
     grid = (STRIPS, ROWS, COLS, C)
     return (
-        back[:, :, :C].reshape(grid),
-        back[:, :, 384 : 384 + C].reshape(grid).astype(f32),
+        result.reshape(grid),
+        latent_grad.reshape(grid),
         grad_w_in,
         grad_b_in,
         grad_w_conv.reshape(3, 3, C, C),

time: 193 us -> 193 us (level)
  blocking collectives: 83.5 us -> 89 us
  waiting for transfers between devices: 15.7 us -> 12.1 us
  starting transfers between devices: 27.1 us -> 24.5 us
    all_to_all x6 -> x7, blocking collectives: 83.5 us -> 89 us  [across(): return lax.all_to_all(blocks, axes, 0, 0, tiled=True)]
    all_to_all x2 -> x1, waiting for transfers between devices: 9.97 us -> 5.36 us  [across(): return lax.all_to_all(blocks, axes, 0, 0, tiled=True)]
    all_to_all x2 -> x1, starting transfers between devices: 11.9 us -> 8.49 us  [across(): return lax.all_to_all(blocks, axes, 0, 0, tiled=True)]
    pallas_call x10 -> x11, Pallas kernels: 58.3 us -> 59.2 us  [call(): pl.pallas_call(body, out_shape=tuple((made_as(i, made) for i, made in enu...]
  transfers between devices with their start and end apart: 9 -> 8, of which waited for: 5 -> 5; matrix products, arithmetic and copies ran while one was open for 1% -> 1% of each run, Pallas kernels for 8% -> 6%
where the time goes in v4:
time: 193 us; the launch traced here: 192 us
  blocking collectives  89 us (46%)
  Pallas kernels  61.2 us (32%)
  starting transfers between devices  24.5 us (13%)
  waiting for transfers between devices  12.1 us (6%)
  other arithmetic  2.67 us (1%)
    all_to_all x7, blocking collectives, across(): return lax.all_to_all(blocks, axes, 0, 0, tiled=True)  89 us
    pallas_call x11, Pallas kernels, call(): pl.pallas_call(body, out_shape=tuple((made_as(i, made) for i, made in enu...  59.2 us
    all_to_all x1, starting transfers between devices, across(): return lax.all_to_all(blocks, axes, 0, 0, tiled=True)  8.49 us
    ppermute x4, starting transfers between devices, swap(): return lax.ppermute(array, 'c', [(0, 1), (1, 0)])  7.58 us
    ppermute x1, starting transfers between devices, per_device(): left = lax.ppermute(edge(COLS - 1), ('x', 'c'), right_way)  6.02 us
    all_to_all x1, waiting for transfers between devices, across(): return lax.all_to_all(blocks, axes, 0, 0, tiled=True)  5.36 us
  transfers between devices with their start and end apart: 8, of which 5 were waited for; matrix products, arithmetic and copies ran while one was open for 1% of the time, Pallas kernels for 6%

profile of v4, /device:TPU:1, one launch (start us, length us, event | category | flops | bytes accessed | tf_op | source)
XLA Modules:
  0.0 192.2 jit_solution(1059112339096946948)
XLA Ops:
  0.6 2.0 %fusion.6 = bf16[8,32,1024]{2,1,0:T(8,128)(2,1)} fusion(bf16[8,32,320]{2,1,0:T(8,128)(2,1)} %bitcast.58, bf16[8,32,320]{2,1,0:T(8,128)(2,1)} %bitcast.59, bf16[8,32,192]{2,1,0:T(8,128)(2,1)} %bitcast.60), kind=kLoop, calls=%fused_computation.13 | loop fusion | flops 3670016 | bytes 950272 | tf_op jit(solution)/shard_map/concatenate | solution.py:693
  2.7 8.5 %all-to-all-start = ((bf16[8,32,1024]{2,1,0:T(8,128)(2,1)}), bf16[8,32,1024]{2,1,0:T(8,128)(2,1)S(1)}, u32[]{:S(2)}, u32[]{:S(2)}) async-start(bf16[8,32,1024]{2,1,0:T(8,128)(2,1)} %fusion.6), calls=%async_computation | async-start | bytes 1048576 | tf_op jit(solution)/shard_map/all_to_all | solution.py:677
  13.9 2.6 %text.1 = (bf16[128,512]{1,0:T(8,128)(2,1)}, bf16[128,512]{1,0:T(8,128)(2,1)}) custom-call(bf16[128,768]{1,0:T(8,128)(2,1)} %pad.18.refs_0_, bf16[320,768]{1,0:T(8,128)(2,1)} %bitcast.61, bf16[320,768]{1,0:T(8,128)(2,1)} %bitcast.62), custom_call_target="tpu_custom_call" | custom-call | flops 4000000000 | bytes 2000000 | tf_op jit(solution)/shard_map/text/pallas_call | solution.py:134
  16.5 5.4 %all-to-all-done.refs_2_.refs_4_ = bf16[8,32,1024]{2,1,0:T(8,128)(2,1)S(1)} async-done(((bf16[8,32,1024]{2,1,0:T(8,128)(2,1)}), bf16[8,32,1024]{2,1,0:T(8,128)(2,1)S(1)}, u32[]{:S(2)}, u32[]{:S(2)}) %all-to-all-start) | async-done | bytes 524320 | tf_op jit(solution)/shard_map/all_to_all | solution.py:677
  22.5 2.7 %collective-permute-done.refs_3_ = bf16[8,2,8,256]{3,2,1,0:T(8,128)(2,1)S(1)} collective-permute-done((bf16[8,2,8,256]{3,2,1,0:T(8,128)(2,1)S(1)}, bf16[8,2,8,256]{3,2,1,0:T(8,128)(2,1)S(1)}, u32[]{:S(2)}, u32[]{:S(2)}) %collective-permute-start) | collective-permute-done | bytes 65568 | tf_op jit(solution)/shard_map/ppermute | solution.py:714
  25.3 6.0 %collective-permute-start.1 = (bf16[48,256]{1,0:T(8,128)(2,1)S(1)}, bf16[48,256]{1,0:T(8,128)(2,1)S(1)}, u32[]{:S(2)}, u32[]{:S(2)}) collective-permute-start(bf16[48,256]{1,0:T(8,128)(2,1)S(1)} %reshape.80), channel_id=1, source_target_pairs={{0,1},{1,2},{2,3},{3,4},{4,5},{5,6},{6,7},{8,9},{9,10},{10,11},{11... | collective-permute-start | bytes 73736 | tf_op jit(solution)/shard_map/ppermute | solution.py:721
  31.3 1.9 collective-permute-start.2
  33.4 2.0 %load_adapter.1 = (bf16[192,320]{1,0:T(8,128)(2,1)S(1)}, f32[320]{0:T(512)S(1)}, bf16[9,320,320]{2,1,0:T(8,128)(2,1)S(1)}, f32[320]{0:T(512)S(1)}, bf16[320,320]...) custom-call(bf16[192,320]{1,0:T(8,128)(2,1)} %refs_0_.4, ...), custom_call_target="tpu_custom_call" | custom-call | tf_op jit(solution)/shard_map/load_adapter/pallas_call | solution.py:170
  36.5 4.6 %adapter.1 = (bf16[8,256,128]{2,1,0:T(8,128)(2,1)S(1)}, f32[256,320]{1,0:T(8,128)}, bf16[256,320]{1,0:T(8,128)(2,1)}, f32[256,320]{1,0:T(8,128)}, bf16[9,256,256]{2,1,0:T(8,128)(2,1)}) custom-call(s32[4]{0:T(128)S(1)} %pad_add_fusion.refs_0_, s32[8]{0:T(128)S(1)} %copy-done.11, bf16[8,32,1024]{2,1,0:T(8,128)(2,1)S(1)} %all-to-all-done.refs_2_.refs_4_, ...), custom_call_target="tpu_custom_call" | custom-call | tf_op jit(solution)/shard_map/adapter/pallas_call | solution.py:134
  41.1 13.9 %all_to_all.40 = bf16[8,256,128]{2,1,0:T(8,128)(2,1)S(1)} all-to-all(bf16[8,256,128]{2,1,0:T(8,128)(2,1)S(1)} %get-tuple-element.73), channel_id=1, replica_groups=mesh['a'=8,'b'=2,'x'=4,'c'=2] {'b','x'}, dimensions={0} | all-to-all | bytes 1048576 | tf_op jit(solution)/shard_map/all_to_all | solution.py:677
  55.8 2.1 %form.1 = (bf16[320,512]{1,0:T(8,128)(2,1)}, bf16[512,320]{1,0:T(8,128)(2,1)}, bf16[1024,768]{1,0:T(8,128)(2,1)S(1)}) custom-call(bf16[320,320]{1,0:T(8,128)(2,1)} %refs_0_.5, bf16[320,320]{1,0:T(8,128)(2,1)} %refs_1_.8, bf16[320,320]{1,0:T(8,128)(2,1)} %refs_2_.1), custom_call_target="tpu_custom_call" | custom-call | tf_op jit(solution)/shard_map/form/pallas_call | solution.py:134
  57.9 11.8 %attend.1 = (bf16[64,16,128]{2,1,0:T(8,128)(2,1)S(1)}, f32[2048,128]{1,0:T(8,128)}, bf16[2048,4096]{1,0:T(8,128)(2,1)}, bf16[128,4096]{1,0:T(8,128)(2,1)}, bf16[128,2048]{1,0:T(8,128)(2,1)}) custom-call(bf16[2048,128]{1,0:T(8,128)(2,1)S(1)} %bitcast.44, bf16[2048,128]{1,0:T(8,128)(2,1)S(1)} %collective-permute-done.3.refs_1_), custom_call_target="tpu_custom_call" | custom-call | tf_op jit(solution)/shard_map/attend/pallas_call | solution.py:134
  69.7 9.9 %all_to_all.41.refs_2_ = bf16[8,128,128]{2,1,0:T(8,128)(2,1)S(1)} all-to-all(bf16[8,128,128]{2,1,0:T(8,128)(2,1)S(1)} %bitcast.48), channel_id=1, replica_groups=mesh['a'=8,'b'=2,'x'=4,'c'=2] {'b','x'}, dimensions={0} | all-to-all | bytes 524288 | tf_op jit(solution)/shard_map/all_to_all | solution.py:677
  79.6 9.3 %middle.1 = (bf16[256,320]{1,0:T(8,128)(2,1)}, f32[256,320]{1,0:T(8,128)}, bf16[8,128,128]{2,1,0:T(8,128)(2,1)S(1)}) custom-call(s32[4]{0:T(128)S(1)} %pad_add_fusion.refs_0_, s32[8]{0:T(128)S(1)} %copy-done.12, bf16[8,128,128]{2,1,0:T(8,128)(2,1)S(1)} %all_to_all.41.refs_2_, f32[256,320]{1,0:T(8,128)} %get-tuple-element.81.refs_3_, ...), custom_call_target="tpu_custom_call" | custom-call | tf_op jit(solution)/shard_map/middle/pallas_call | solution.py:134
  89.0 8.7 %all_to_all.42 = bf16[8,128,128]{2,1,0:T(8,128)(2,1)S(1)} all-to-all(bf16[8,128,128]{2,1,0:T(8,128)(2,1)S(1)} %get-tuple-element.87), channel_id=1, replica_groups=mesh['a'=8,'b'=2,'x'=4,'c'=2] {'b','x'}, dimensions={0} | all-to-all | bytes 524288 | tf_op jit(solution)/shard_map/all_to_all | solution.py:677
  97.7 16.0 %attend_back.1 = (f32[2048,128]{1,0:T(8,128)S(1)}, bf16[2048,128]{1,0:T(8,128)(2,1)S(1)}) custom-call(bf16[128,4096]{1,0:T(8,128)(2,1)S(1)} %copy-done.4, bf16[128,2048]{1,0:T(8,128)(2,1)S(1)} %copy-done.6, f32[2048,128]{1,0:T(8,128)S(1)} %copy-done.3, bf16[64,16,128]{2,1,0:T(8,128)(2,1)S(1)} %bitcast.45, bf16[2048,4096]{1,0:T(8,128)(2,1)} %get-tuple-element.88.refs_4_), custom_call_target="tpu_custom_call" | custom-call | tf_op jit(solution)/shard_map/attend_back/pallas_call | solution.py:134
  113.6 2.0 %collective-permute-start.4 = (bf16[2048,128]{1,0:T(8,128)(2,1)S(1)}, bf16[2048,128]{1,0:T(8,128)(2,1)S(1)}, u32[]{:S(2)}, u32[]{:S(2)}) collective-permute-start(bf16[2048,128]{1,0:T(8,128)(2,1)S(1)} %get-tuple-element.90), channel_id=1, source_target_pairs={{0,1},{1,0},{2,3},{3,2},{4,5},{5,4},{6,7},{7,6},{8,9},{9,8},{10,11... | collective-permute-start | bytes 1572872 | tf_op jit(solution)/shard_map/ppermute | solution.py:673
  117.8 12.9 %all_to_all.43.refs_1_ = bf16[8,256,128]{2,1,0:T(8,128)(2,1)S(1)} all-to-all(bf16[8,256,128]{2,1,0:T(8,128)(2,1)S(1)} %bitcast.53), channel_id=1, replica_groups=mesh['a'=8,'b'=2,'x'=4,'c'=2] {'b','x'}, dimensions={0} | all-to-all | bytes 1048576 | tf_op jit(solution)/shard_map/all_to_all | solution.py:677
  130.7 2.8 %finish.1 = (bf16[8,6,32,128]{3,2,1,0:T(8,128)(2,1)}, bf16[2,3072,128]{2,1,0:T(8,128)(2,1)S(1)}) custom-call(s32[4]{0:T(128)S(1)} %pad_add_fusion.refs_0_, bf16[8,256,128]{2,1,0:T(8,128)(2,1)S(1)} %all_to_all.43.refs_1_, bf16[320,1024]{1,0:T(8,128)(2,1)S(1)} %join.1.refs_2_, f32[256,320]{1,0:T(8,128)S(1)} %copy-done.1, f32[256,320]{1,0:T(8,128)S(1)} %copy-done.8, ...), custom_call_target="tpu_custom_call" | custom-call | tf_op jit(solution)/shard_map/finish/pallas_call | solution.py:134
  136.6 19.7 %all_to_all.44 = bf16[64,48,128]{2,1,0:T(8,128)(2,1)S(1)} all-to-all(bf16[64,48,128]{2,1,0:T(8,128)(2,1)S(1)} %bitcast.49), channel_id=1, replica_groups=mesh['a'=8,'b'=2,'x'=4,'c'=2] {'a','b','x'}, dimensions={0} | all-to-all | bytes 1572864 | tf_op jit(solution)/shard_map/all_to_all | solution.py:677
  156.4 11.5 %all_to_all.45.refs_0_ = bf16[8,240,128]{2,1,0:T(8,128)(2,1)S(1)} all-to-all(bf16[8,240,128]{2,1,0:T(8,128)(2,1)S(1)} %pad_maximum_fusion), channel_id=1, replica_groups=mesh['a'=8,'b'=2,'x'=4,'c'=2] {'a'}, dimensions={0} | all-to-all | bytes 983040 | tf_op jit(solution)/shard_map/all_to_all | solution.py:677
  168.1 12.4 %all_to_all.46 = bf16[8,384,128]{2,1,0:T(8,128)(2,1)S(1)} all-to-all(bf16[8,384,128]{2,1,0:T(8,128)(2,1)S(1)} %broadcast_in_dim.15), channel_id=1, replica_groups=mesh['a'=8,'b'=2,'x'=4,'c'=2] {'b','x'}, dimensions={0} | all-to-all | bytes 1572864 | tf_op jit(solution)/shard_map/all_to_all | solution.py:677
  180.5 4.0 %collective-permute-start.6 = (bf16[3072,128]{1,0:T(8,128)(2,1)S(1)}, bf16[3072,128]{1,0:T(8,128)(2,1)S(1)}, u32[]{:S(2)}, u32[]{:S(2)}) collective-permute-start(bf16[3072,128]{1,0:T(8,128)(2,1)S(1)} %bitcast.46), channel_id=1, source_target_pairs={{0,1},{1,0},{2,3},{3,2},{4,5},{5,4},{6,7},{7,6},{8,9},{9,8},{10,11... | collective-permute-start | bytes 2359304 | tf_op jit(solution)/shard_map/ppermute | solution.py:673
  186.4 5.6 %weights.1 = (f32[192,320]{1,0:T(8,128)}, f32[320]{0:T(512)}, f32[9,320,320]{2,1,0:T(8,128)}, f32[320]{0:T(512)}, f32[320,320]{1,0:T(8,128)}, /*index=5*/f32[320]{0:T(512)}) custom-call(s32[4]{0:T(128)S(1)} %pad_add_fusion.refs_0_, bf16[3072,128]{1,0:T(8,128)(2,1)S(1)} %bitcast.47, bf16[3072,128]{1,0:T(8,128)(2,1)S(1)} %collective-permute-done.6.refs_2_, ...), custom_call_target="tpu_custom_call" | custom-call | flops 6000000000 | bytes 20000000 | tf_op jit(solution)/shard_map/weights/pallas_call | solution.py:134
  (66 shorter events, 12.6 us)
Async XLA Ops:
  0.6 10.6 %copy-start = (bf16[8,77,768]{2,0,1:T(8,128)(2,1)S(1)}, bf16[8,77,768]{2,0,1:T(8,128)(2,1)}, u32[]{:S(2)}) copy-start(bf16[8,77,768]{2,0,1:T(8,128)(2,1)} %param.28) | copy-start | bytes 2838532
  2.7 19.2 %all-to-all-start = ((bf16[8,32,1024]{2,1,0:T(8,128)(2,1)}), bf16[8,32,1024]{2,1,0:T(8,128)(2,1)S(1)}, u32[]{:S(2)}, u32[]{:S(2)}) async-start(bf16[8,32,1024]{2,1,0:T(8,128)(2,1)} %fusion.6), calls=%async_computation | async-start | bytes 1048576 | tf_op jit(solution)/shard_map/all_to_all | solution.py:677
  22.0 3.2 %collective-permute-start = (bf16[8,2,8,256]{3,2,1,0:T(8,128)(2,1)S(1)}, bf16[8,2,8,256]{3,2,1,0:T(8,128)(2,1)S(1)}, u32[]{:S(2)}, u32[]{:S(2)}) collective-permute-start(bf16[8,2,8,256]{3,2,1,0:T(8,128)(2,1)S(1)} %pad_maximum_fusion.1), channel_id=1, source_target_pairs={{0,8},{8,0},{1,9},{9,1},{2,10},{10,2},{3,11},{11,3},{4,12},{12,4},... | collective-permute-start | bytes 196616 | tf_op jit(solution)/shard_map/ppermute | solution.py:714
  25.3 10.1 %collective-permute-start.1 = (bf16[48,256]{1,0:T(8,128)(2,1)S(1)}, bf16[48,256]{1,0:T(8,128)(2,1)S(1)}, u32[]{:S(2)}, u32[]{:S(2)}) collective-permute-start(bf16[48,256]{1,0:T(8,128)(2,1)S(1)} %reshape.80), channel_id=1, source_target_pairs={{0,1},{1,2},{2,3},{3,4},{4,5},{5,6},{6,7},{8,9},{9,10},{10,11},{11... | collective-permute-start | bytes 73736 | tf_op jit(solution)/shard_map/ppermute | solution.py:721
  31.3 5.1 %collective-permute-start.2 = (bf16[48,256]{1,0:T(8,128)(2,1)S(1)}, bf16[48,256]{1,0:T(8,128)(2,1)S(1)}, u32[]{:S(2)}, u32[]{:S(2)}) collective-permute-start(bf16[48,256]{1,0:T(8,128)(2,1)S(1)} %reshape.81), channel_id=1, source_target_pairs={{1,0},{2,1},{3,2},{4,3},{5,4},{6,5},{7,6},{9,8},{10,9},{11,10},{12... | collective-permute-start | bytes 73736 | tf_op jit(solution)/shard_map/ppermute | solution.py:722
  33.4 3.1 %copy-start.11 = (s32[8]{0:T(128)S(1)}, s32[8]{0:T(128)}, u32[]{:S(2)}) copy-start(s32[8]{0:T(128)} %refs_1_.7) | copy-start | bytes 100
  41.1 38.5 %copy-start.12 = (s32[8]{0:T(128)S(1)}, s32[8]{0:T(128)}, u32[]{:S(2)}) copy-start(s32[8]{0:T(128)} %refs_1_.9) | copy-start | bytes 100
  55.0 2.8 %collective-permute-start.3 = (bf16[2048,128]{1,0:T(8,128)(2,1)S(1)}, bf16[2048,128]{1,0:T(8,128)(2,1)S(1)}, u32[]{:S(2)}, u32[]{:S(2)}) collective-permute-start(bf16[2048,128]{1,0:T(8,128)(2,1)S(1)} %bitcast.43), channel_id=1, source_target_pairs={{0,1},{1,0},{2,3},{3,2},{4,5},{5,4},{6,7},{7,6},{8,9},{9,8},{10,11... | collective-permute-start | bytes 1572872 | tf_op jit(solution)/shard_map/ppermute | solution.py:673
  79.6 18.0 %copy-start.3 = (f32[2048,128]{1,0:T(8,128)S(1)}, f32[2048,128]{1,0:T(8,128)}, u32[]{:S(2)}) copy-start(f32[2048,128]{1,0:T(8,128)} %get-tuple-element.79.refs_2_) | copy-start | bytes 3145732
  79.6 18.0 %copy-start.4 = (bf16[128,4096]{1,0:T(8,128)(2,1)S(1)}, bf16[128,4096]{1,0:T(8,128)(2,1)}, u32[]{:S(2)}) copy-start(bf16[128,4096]{1,0:T(8,128)(2,1)} %get-tuple-element.77.refs_0_) | copy-start | bytes 3145732
  79.6 18.0 %copy-start.6 = (bf16[128,2048]{1,0:T(8,128)(2,1)S(1)}, bf16[128,2048]{1,0:T(8,128)(2,1)}, u32[]{:S(2)}) copy-start(bf16[128,2048]{1,0:T(8,128)(2,1)} %get-tuple-element.78.refs_1_) | copy-start | bytes 1572868
  113.6 4.0 %collective-permute-start.4 = (bf16[2048,128]{1,0:T(8,128)(2,1)S(1)}, bf16[2048,128]{1,0:T(8,128)(2,1)S(1)}, u32[]{:S(2)}, u32[]{:S(2)}) collective-permute-start(bf16[2048,128]{1,0:T(8,128)(2,1)S(1)} %get-tuple-element.90), channel_id=1, source_target_pairs={{0,1},{1,0},{2,3},{3,2},{4,5},{5,4},{6,7},{7,6},{8,9},{9,8},{10,11... | collective-permute-start | bytes 1572872 | tf_op jit(solution)/shard_map/ppermute | solution.py:673
  117.6 13.1 %copy-start.1 = (f32[256,320]{1,0:T(8,128)S(1)}, f32[256,320]{1,0:T(8,128)}, u32[]{:S(2)}) copy-start(f32[256,320]{1,0:T(8,128)} %get-tuple-element.81.refs_3_) | copy-start | bytes 983044
  117.6 13.1 %copy-start.2 = (bf16[9,256,256]{2,1,0:T(8,128)(2,1)S(1)}, bf16[9,256,256]{2,1,0:T(8,128)(2,1)}, u32[]{:S(2)}) copy-start(bf16[9,256,256]{2,1,0:T(8,128)(2,1)} %get-tuple-element.97.refs_7_) | copy-start | bytes 3538948
  117.6 13.1 %copy-start.5 = (bf16[320,320]{1,0:T(8,128)(2,1)S(1)}, bf16[320,320]{1,0:T(8,128)(2,1)}, u32[]{:S(2)}) copy-start(bf16[320,320]{1,0:T(8,128)(2,1)} %refs_8_.5) | copy-start | bytes 614404
  117.6 13.1 %copy-start.7 = (f32[256,320]{1,0:T(8,128)S(1)}, f32[256,320]{1,0:T(8,128)}, u32[]{:S(2)}) copy-start(f32[256,320]{1,0:T(8,128)} %get-tuple-element.95.refs_5_) | copy-start | bytes 983044
  117.6 13.1 %copy-start.8 = (f32[256,320]{1,0:T(8,128)S(1)}, f32[256,320]{1,0:T(8,128)}, u32[]{:S(2)}) copy-start(f32[256,320]{1,0:T(8,128)} %get-tuple-element.94.refs_4_) | copy-start | bytes 983044
  117.6 13.1 %copy-start.9 = (bf16[256,320]{1,0:T(8,128)(2,1)S(1)}, bf16[256,320]{1,0:T(8,128)(2,1)}, u32[]{:S(2)}) copy-start(bf16[256,320]{1,0:T(8,128)(2,1)} %get-tuple-element.96.refs_6_) | copy-start | bytes 491524
  117.6 13.1 %copy-start.10 = (bf16[256,320]{1,0:T(8,128)(2,1)S(1)}, bf16[256,320]{1,0:T(8,128)(2,1)}, u32[]{:S(2)}) copy-start(bf16[256,320]{1,0:T(8,128)(2,1)} %get-tuple-element.98.refs_9_) | copy-start | bytes 491524
  133.5 2.7 %collective-permute-start.5 = (bf16[3072,128]{1,0:T(8,128)(2,1)S(1)}, bf16[3072,128]{1,0:T(8,128)(2,1)S(1)}, u32[]{:S(2)}, u32[]{:S(2)}) collective-permute-start(bf16[3072,128]{1,0:T(8,128)(2,1)S(1)} %slice_bitcast_fusion), channel_id=1, source_target_pairs={{0,1},{1,0},{2,3},{3,2},{4,5},{5,4},{6,7},{7,6},{8,9},{9,8},{10,11... | collective-permute-start | bytes 2359304 | tf_op jit(solution)/shard_map/ppermute | solution.py:673
  136.5 19.8 %copy-start.13 = (bf16[8,6,32,128]{3,2,1,0:T(8,128)(2,1)S(1)}, bf16[8,6,32,128]{3,2,1,0:T(8,128)(2,1)}, u32[]{:S(2)}) copy-start(bf16[8,6,32,128]{3,2,1,0:T(8,128)(2,1)} %get-tuple-element.100) | copy-start | bytes 1179652
  180.5 5.9 %collective-permute-start.6 = (bf16[3072,128]{1,0:T(8,128)(2,1)S(1)}, bf16[3072,128]{1,0:T(8,128)(2,1)S(1)}, u32[]{:S(2)}, u32[]{:S(2)}) collective-permute-start(bf16[3072,128]{1,0:T(8,128)(2,1)S(1)} %bitcast.46), channel_id=1, source_target_pairs={{0,1},{1,0},{2,3},{3,2},{4,5},{5,4},{6,7},{7,6},{8,9},{9,8},{10,11... | collective-permute-start | bytes 2359304 | tf_op jit(solution)/shard_map/ppermute | solution.py:673

commit v5 on v4

--- a/solution.py
+++ b/solution.py
@@ -867,8 +867,9 @@
     sums = parcel[:, :SHARE].reshape(1, STRIPS * SHARE, LANES)
     sums = jnp.broadcast_to(sums, (HEADS,) + sums.shape[1:])
     mine = across(sums, GROUP_OF_ITEM).reshape(SUM_ROWS, LANES)
-    mine, parcel = after(mine, parcel)
+    mine, parcel, w_turned = after(mine, parcel, w_turned)
     theirs = swap(mine)
+    taps_here, w_turned_here = bring([w_conv.reshape(9, C, C), w_turned], "load_weights")
     result, latent_grad = call(
         unpack_kernel,
         (out(STRIPS, PART, C), out(STRIPS, PART, C, dtype=f32)),
@@ -886,7 +887,7 @@
             out(C, C, dtype=f32),
             out(C, dtype=f32),
         ),
-        (place, mine, theirs, w_turned, w_conv.reshape(9, C, C)),
+        (place, mine, theirs, w_turned_here, taps_here),
         "weights",
         scalars=1,
         scratch=[
@@ -894,9 +895,9 @@
             pltpu.SemaphoreType.DMA((9,)),
         ],
         vmem=24,
-        fetch=(3, 4),
         store=(0, 4),
         far=(7,),
+        held=(3, 4),
         cost=pl.CostEstimate(flops=6 * 10**9, bytes_accessed=2 * 10**7, transcendentals=0),
     )
     grid = (STRIPS, ROWS, COLS, C)

time: 193 us -> 192 us (level)
  transfers between devices with their start and end apart: 8 -> 8, of which waited for: 5 -> 4; matrix products, arithmetic and copies ran while one was open for 1% -> 1% of each run, Pallas kernels for 6% -> 7%
where the time goes in v5:
time: 192 us; the launch traced here: 191 us
  blocking collectives  89 us (46%)
  Pallas kernels  61.2 us (32%)
  starting transfers between devices  24.5 us (13%)
  waiting for transfers between devices  11 us (6%)
  other arithmetic  2.67 us (1%)
    all_to_all x7, blocking collectives, across(): return lax.all_to_all(blocks, axes, 0, 0, tiled=True)  89 us
    pallas_call x11, Pallas kernels, call(): pl.pallas_call(body, out_shape=tuple((made_as(i, made) for i, made in enu...  57.5 us
    all_to_all x1, starting transfers between devices, across(): return lax.all_to_all(blocks, axes, 0, 0, tiled=True)  8.49 us
    ppermute x4, starting transfers between devices, swap(): return lax.ppermute(array, 'c', [(0, 1), (1, 0)])  7.58 us
    ppermute x1, starting transfers between devices, per_device(): left = lax.ppermute(edge(COLS - 1), ('x', 'c'), right_way)  6.02 us
    all_to_all x1, waiting for transfers between devices, across(): return lax.all_to_all(blocks, axes, 0, 0, tiled=True)  5.35 us
  transfers between devices with their start and end apart: 8, of which 4 were waited for; matrix products, arithmetic and copies ran while one was open for 1% of the time, Pallas kernels for 7%

profile of v5, /device:TPU:1, one launch (start us, length us, event | category | flops | bytes accessed | tf_op | source)
XLA Modules:
  0.0 191.2 jit_solution(2396113133139432930)
XLA Ops:
  0.6 2.0 %fusion.6 = bf16[8,32,1024]{2,1,0:T(8,128)(2,1)} fusion(bf16[8,32,320]{2,1,0:T(8,128)(2,1)} %bitcast.58, bf16[8,32,320]{2,1,0:T(8,128)(2,1)} %bitcast.59, bf16[8,32,192]{2,1,0:T(8,128)(2,1)} %bitcast.60), kind=kLoop, calls=%fused_computation.13 | loop fusion | flops 3670016 | bytes 950272 | tf_op jit(solution)/shard_map/concatenate | solution.py:693
  2.7 8.5 %all-to-all-start = ((bf16[8,32,1024]{2,1,0:T(8,128)(2,1)}), bf16[8,32,1024]{2,1,0:T(8,128)(2,1)S(1)}, u32[]{:S(2)}, u32[]{:S(2)}) async-start(bf16[8,32,1024]{2,1,0:T(8,128)(2,1)} %fusion.6), calls=%async_computation | async-start | bytes 1048576 | tf_op jit(solution)/shard_map/all_to_all | solution.py:677
  13.9 2.6 %text.1 = (bf16[128,512]{1,0:T(8,128)(2,1)}, bf16[128,512]{1,0:T(8,128)(2,1)}) custom-call(bf16[128,768]{1,0:T(8,128)(2,1)} %pad.18.refs_0_, bf16[320,768]{1,0:T(8,128)(2,1)} %bitcast.61, bf16[320,768]{1,0:T(8,128)(2,1)} %bitcast.62), custom_call_target="tpu_custom_call" | custom-call | flops 4000000000 | bytes 2000000 | tf_op jit(solution)/shard_map/text/pallas_call | solution.py:134
  16.5 5.3 %all-to-all-done.refs_2_.refs_4_ = bf16[8,32,1024]{2,1,0:T(8,128)(2,1)S(1)} async-done(((bf16[8,32,1024]{2,1,0:T(8,128)(2,1)}), bf16[8,32,1024]{2,1,0:T(8,128)(2,1)S(1)}, u32[]{:S(2)}, u32[]{:S(2)}) %all-to-all-start) | async-done | bytes 524320 | tf_op jit(solution)/shard_map/all_to_all | solution.py:677
  22.5 2.7 %collective-permute-done.refs_3_ = bf16[8,2,8,256]{3,2,1,0:T(8,128)(2,1)S(1)} collective-permute-done((bf16[8,2,8,256]{3,2,1,0:T(8,128)(2,1)S(1)}, bf16[8,2,8,256]{3,2,1,0:T(8,128)(2,1)S(1)}, u32[]{:S(2)}, u32[]{:S(2)}) %collective-permute-start) | collective-permute-done | bytes 65568 | tf_op jit(solution)/shard_map/ppermute | solution.py:714
  25.3 6.0 %collective-permute-start.1 = (bf16[48,256]{1,0:T(8,128)(2,1)S(1)}, bf16[48,256]{1,0:T(8,128)(2,1)S(1)}, u32[]{:S(2)}, u32[]{:S(2)}) collective-permute-start(bf16[48,256]{1,0:T(8,128)(2,1)S(1)} %reshape.80), channel_id=1, source_target_pairs={{0,1},{1,2},{2,3},{3,4},{4,5},{5,6},{6,7},{8,9},{9,10},{10,11},{11... | collective-permute-start | bytes 73736 | tf_op jit(solution)/shard_map/ppermute | solution.py:721
  31.3 1.9 %collective-permute-start.2 = (bf16[48,256]{1,0:T(8,128)(2,1)S(1)}, bf16[48,256]{1,0:T(8,128)(2,1)S(1)}, u32[]{:S(2)}, u32[]{:S(2)}) collective-permute-start(bf16[48,256]{1,0:T(8,128)(2,1)S(1)} %reshape.81), channel_id=1, source_target_pairs={{1,0},{2,1},{3,2},{4,3},{5,4},{6,5},{7,6},{9,8},{10,9},{11,10},{12... | collective-permute-start | bytes 73736 | tf_op jit(solution)/shard_map/ppermute | solution.py:722
  33.4 2.0 %load_adapter.1 = (bf16[192,320]{1,0:T(8,128)(2,1)S(1)}, f32[320]{0:T(512)S(1)}, bf16[9,320,320]{2,1,0:T(8,128)(2,1)S(1)}, f32[320]{0:T(512)S(1)}, bf16[320,320]...) custom-call(bf16[192,320]{1,0:T(8,128)(2,1)} %refs_0_.4, ...), custom_call_target="tpu_custom_call" | custom-call | tf_op jit(solution)/shard_map/load_adapter/pallas_call | solution.py:170
  36.5 4.6 %adapter.1 = (bf16[8,256,128]{2,1,0:T(8,128)(2,1)S(1)}, f32[256,320]{1,0:T(8,128)}, bf16[256,320]{1,0:T(8,128)(2,1)}, f32[256,320]{1,0:T(8,128)}, bf16[9,256,256]{2,1,0:T(8,128)(2,1)}) custom-call(s32[4]{0:T(128)S(1)} %pad_add_fusion.refs_0_, s32[8]{0:T(128)S(1)} %copy-done.11, bf16[8,32,1024]{2,1,0:T(8,128)(2,1)S(1)} %all-to-all-done.refs_2_.refs_4_, ...), custom_call_target="tpu_custom_call" | custom-call | tf_op jit(solution)/shard_map/adapter/pallas_call | solution.py:134
  41.1 13.9 %all_to_all.40 = bf16[8,256,128]{2,1,0:T(8,128)(2,1)S(1)} all-to-all(bf16[8,256,128]{2,1,0:T(8,128)(2,1)S(1)} %get-tuple-element.76), channel_id=1, replica_groups=mesh['a'=8,'b'=2,'x'=4,'c'=2] {'b','x'}, dimensions={0} | all-to-all | bytes 1048576 | tf_op jit(solution)/shard_map/all_to_all | solution.py:677
  55.8 2.1 %form.1 = (bf16[320,512]{1,0:T(8,128)(2,1)}, bf16[512,320]{1,0:T(8,128)(2,1)}, bf16[1024,768]{1,0:T(8,128)(2,1)S(1)}) custom-call(bf16[320,320]{1,0:T(8,128)(2,1)} %refs_0_.5, bf16[320,320]{1,0:T(8,128)(2,1)} %refs_1_.8, bf16[320,320]{1,0:T(8,128)(2,1)} %refs_2_.1), custom_call_target="tpu_custom_call" | custom-call | tf_op jit(solution)/shard_map/form/pallas_call | solution.py:134
  57.9 11.8 %attend.1 = (bf16[64,16,128]{2,1,0:T(8,128)(2,1)S(1)}, f32[2048,128]{1,0:T(8,128)}, bf16[2048,4096]{1,0:T(8,128)(2,1)}, bf16[128,4096]{1,0:T(8,128)(2,1)}, bf16[128,2048]{1,0:T(8,128)(2,1)}) custom-call(bf16[2048,128]{1,0:T(8,128)(2,1)S(1)} %bitcast.44, bf16[2048,128]{1,0:T(8,128)(2,1)S(1)} %collective-permute-done.3.refs_1_), custom_call_target="tpu_custom_call" | custom-call | tf_op jit(solution)/shard_map/attend/pallas_call | solution.py:134
  69.7 9.9 %all_to_all.41.refs_2_ = bf16[8,128,128]{2,1,0:T(8,128)(2,1)S(1)} all-to-all(bf16[8,128,128]{2,1,0:T(8,128)(2,1)S(1)} %bitcast.48), channel_id=1, replica_groups=mesh['a'=8,'b'=2,'x'=4,'c'=2] {'b','x'}, dimensions={0} | all-to-all | bytes 524288 | tf_op jit(solution)/shard_map/all_to_all | solution.py:677
  79.6 9.3 %middle.1 = (bf16[256,320]{1,0:T(8,128)(2,1)}, f32[256,320]{1,0:T(8,128)}, bf16[8,128,128]{2,1,0:T(8,128)(2,1)S(1)}) custom-call(s32[4]{0:T(128)S(1)} %pad_add_fusion.refs_0_, s32[8]{0:T(128)S(1)} %copy-done.12, bf16[8,128,128]{2,1,0:T(8,128)(2,1)S(1)} %all_to_all.41.refs_2_, f32[256,320]{1,0:T(8,128)} %get-tuple-element.84.refs_3_, ...), custom_call_target="tpu_custom_call" | custom-call | tf_op jit(solution)/shard_map/middle/pallas_call | solution.py:134
  88.9 8.7 %all_to_all.42 = bf16[8,128,128]{2,1,0:T(8,128)(2,1)S(1)} all-to-all(bf16[8,128,128]{2,1,0:T(8,128)(2,1)S(1)} %get-tuple-element.90), channel_id=1, replica_groups=mesh['a'=8,'b'=2,'x'=4,'c'=2] {'b','x'}, dimensions={0} | all-to-all | bytes 524288 | tf_op jit(solution)/shard_map/all_to_all | solution.py:677
  97.7 16.0 %attend_back.1 = (f32[2048,128]{1,0:T(8,128)S(1)}, bf16[2048,128]{1,0:T(8,128)(2,1)S(1)}) custom-call(bf16[128,4096]{1,0:T(8,128)(2,1)S(1)} %copy-done.4, bf16[128,2048]{1,0:T(8,128)(2,1)S(1)} %copy-done.6, f32[2048,128]{1,0:T(8,128)S(1)} %copy-done.3, bf16[64,16,128]{2,1,0:T(8,128)(2,1)S(1)} %bitcast.45, bf16[2048,4096]{1,0:T(8,128)(2,1)} %get-tuple-element.91.refs_4_), custom_call_target="tpu_custom_call" | custom-call | tf_op jit(solution)/shard_map/attend_back/pallas_call | solution.py:134
  113.6 2.0 %collective-permute-start.4 = (bf16[2048,128]{1,0:T(8,128)(2,1)S(1)}, bf16[2048,128]{1,0:T(8,128)(2,1)S(1)}, u32[]{:S(2)}, u32[]{:S(2)}) collective-permute-start(bf16[2048,128]{1,0:T(8,128)(2,1)S(1)} %get-tuple-element.93), channel_id=1, source_target_pairs={{0,1},{1,0},{2,3},{3,2},{4,5},{5,4},{6,7},{7,6},{8,9},{9,8},{10,11... | collective-permute-start | bytes 1572872 | tf_op jit(solution)/shard_map/ppermute | solution.py:673
  117.8 12.9 %all_to_all.43.refs_1_ = bf16[8,256,128]{2,1,0:T(8,128)(2,1)S(1)} all-to-all(bf16[8,256,128]{2,1,0:T(8,128)(2,1)S(1)} %bitcast.53), channel_id=1, replica_groups=mesh['a'=8,'b'=2,'x'=4,'c'=2] {'b','x'}, dimensions={0} | all-to-all | bytes 1048576 | tf_op jit(solution)/shard_map/all_to_all | solution.py:677
  130.7 2.8 %finish.1 = (bf16[8,6,32,128]{3,2,1,0:T(8,128)(2,1)}, bf16[2,3072,128]{2,1,0:T(8,128)(2,1)S(1)}) custom-call(s32[4]{0:T(128)S(1)} %pad_add_fusion.refs_0_, bf16[8,256,128]{2,1,0:T(8,128)(2,1)S(1)} %all_to_all.43.refs_1_, bf16[320,1024]{1,0:T(8,128)(2,1)S(1)} %join.1.refs_2_, f32[256,320]{1,0:T(8,128)S(1)} %copy-done.1, f32[256,320]{1,0:T(8,128)S(1)} %copy-done.8, ...), custom_call_target="tpu_custom_call" | custom-call | tf_op jit(solution)/shard_map/finish/pallas_call | solution.py:134
  136.5 19.7 %all_to_all.44 = bf16[64,48,128]{2,1,0:T(8,128)(2,1)S(1)} all-to-all(bf16[64,48,128]{2,1,0:T(8,128)(2,1)S(1)} %bitcast.51), channel_id=1, replica_groups=mesh['a'=8,'b'=2,'x'=4,'c'=2] {'a','b','x'}, dimensions={0} | all-to-all | bytes 1572864 | tf_op jit(solution)/shard_map/all_to_all | solution.py:677
  156.5 11.5 %all_to_all.45.refs_0_ = bf16[8,240,128]{2,1,0:T(8,128)(2,1)S(1)} all-to-all(bf16[8,240,128]{2,1,0:T(8,128)(2,1)S(1)} %pad_maximum_fusion), channel_id=1, replica_groups=mesh['a'=8,'b'=2,'x'=4,'c'=2] {'a'}, dimensions={0} | all-to-all | bytes 983040 | tf_op jit(solution)/shard_map/all_to_all | solution.py:677
  168.1 12.4 %all_to_all.46 = bf16[8,384,128]{2,1,0:T(8,128)(2,1)S(1)} all-to-all(bf16[8,384,128]{2,1,0:T(8,128)(2,1)S(1)} %broadcast_in_dim.15), channel_id=1, replica_groups=mesh['a'=8,'b'=2,'x'=4,'c'=2] {'b','x'}, dimensions={0} | all-to-all | bytes 1572864 | tf_op jit(solution)/shard_map/all_to_all | solution.py:677
  180.5 4.0 %collective-permute-start.6 = (bf16[3072,128]{1,0:T(8,128)(2,1)S(1)}, bf16[3072,128]{1,0:T(8,128)(2,1)S(1)}, u32[]{:S(2)}, u32[]{:S(2)}) collective-permute-start(bf16[3072,128]{1,0:T(8,128)(2,1)S(1)} %bitcast.46), channel_id=1, source_target_pairs={{0,1},{1,0},{2,3},{3,2},{4,5},{5,4},{6,7},{7,6},{8,9},{9,8},{10,11... | collective-permute-start | bytes 2359304 | tf_op jit(solution)/shard_map/ppermute | solution.py:673
  187.0 3.9 %weights.1 = (f32[192,320]{1,0:T(8,128)}, f32[320]{0:T(512)}, f32[9,320,320]{2,1,0:T(8,128)}, f32[320]{0:T(512)}, f32[320,320]{1,0:T(8,128)}, /*index=5*/f32[320]{0:T(512)}) custom-call(s32[4]{0:T(128)S(1)} %pad_add_fusion.refs_0_, bf16[3072,128]{1,0:T(8,128)(2,1)S(1)} %bitcast.47, bf16[3072,128]{1,0:T(8,128)(2,1)S(1)} %collective-permute-done.6.refs_2_, ...), custom_call_target="tpu_custom_call" | custom-call | flops 6000000000 | bytes 20000000 | tf_op jit(solution)/shard_map/weights/pallas_call | solution.py:134
  (67 shorter events, 13.1 us)
Async XLA Ops:
  0.6 10.6 %copy-start = (bf16[8,77,768]{2,0,1:T(8,128)(2,1)S(1)}, bf16[8,77,768]{2,0,1:T(8,128)(2,1)}, u32[]{:S(2)}) copy-start(bf16[8,77,768]{2,0,1:T(8,128)(2,1)} %param.28) | copy-start | bytes 2838532
  2.7 19.2 %all-to-all-start = ((bf16[8,32,1024]{2,1,0:T(8,128)(2,1)}), bf16[8,32,1024]{2,1,0:T(8,128)(2,1)S(1)}, u32[]{:S(2)}, u32[]{:S(2)}) async-start(bf16[8,32,1024]{2,1,0:T(8,128)(2,1)} %fusion.6), calls=%async_computation | async-start | bytes 1048576 | tf_op jit(solution)/shard_map/all_to_all | solution.py:677
  22.0 3.2 %collective-permute-start = (bf16[8,2,8,256]{3,2,1,0:T(8,128)(2,1)S(1)}, bf16[8,2,8,256]{3,2,1,0:T(8,128)(2,1)S(1)}, u32[]{:S(2)}, u32[]{:S(2)}) collective-permute-start(bf16[8,2,8,256]{3,2,1,0:T(8,128)(2,1)S(1)} %pad_maximum_fusion.1), channel_id=1, source_target_pairs={{0,8},{8,0},{1,9},{9,1},{2,10},{10,2},{3,11},{11,3},{4,12},{12,4},... | collective-permute-start | bytes 196616 | tf_op jit(solution)/shard_map/ppermute | solution.py:714
  25.3 10.1 %collective-permute-start.1 = (bf16[48,256]{1,0:T(8,128)(2,1)S(1)}, bf16[48,256]{1,0:T(8,128)(2,1)S(1)}, u32[]{:S(2)}, u32[]{:S(2)}) collective-permute-start(bf16[48,256]{1,0:T(8,128)(2,1)S(1)} %reshape.80), channel_id=1, source_target_pairs={{0,1},{1,2},{2,3},{3,4},{4,5},{5,6},{6,7},{8,9},{9,10},{10,11},{11... | collective-permute-start | bytes 73736 | tf_op jit(solution)/shard_map/ppermute | solution.py:721
  31.3 5.1 %collective-permute-start.2 = (bf16[48,256]{1,0:T(8,128)(2,1)S(1)}, bf16[48,256]{1,0:T(8,128)(2,1)S(1)}, u32[]{:S(2)}, u32[]{:S(2)}) collective-permute-start(bf16[48,256]{1,0:T(8,128)(2,1)S(1)} %reshape.81), channel_id=1, source_target_pairs={{1,0},{2,1},{3,2},{4,3},{5,4},{6,5},{7,6},{9,8},{10,9},{11,10},{12... | collective-permute-start | bytes 73736 | tf_op jit(solution)/shard_map/ppermute | solution.py:722
  33.4 3.1 %copy-start.11 = (s32[8]{0:T(128)S(1)}, s32[8]{0:T(128)}, u32[]{:S(2)}) copy-start(s32[8]{0:T(128)} %refs_1_.7) | copy-start | bytes 100
  41.1 38.5 %copy-start.12 = (s32[8]{0:T(128)S(1)}, s32[8]{0:T(128)}, u32[]{:S(2)}) copy-start(s32[8]{0:T(128)} %refs_1_.9) | copy-start | bytes 100
  55.0 2.8 %collective-permute-start.3 = (bf16[2048,128]{1,0:T(8,128)(2,1)S(1)}, bf16[2048,128]{1,0:T(8,128)(2,1)S(1)}, u32[]{:S(2)}, u32[]{:S(2)}) collective-permute-start(bf16[2048,128]{1,0:T(8,128)(2,1)S(1)} %bitcast.43), channel_id=1, source_target_pairs={{0,1},{1,0},{2,3},{3,2},{4,5},{5,4},{6,7},{7,6},{8,9},{9,8},{10,11... | collective-permute-start | bytes 1572872 | tf_op jit(solution)/shard_map/ppermute | solution.py:673
  79.6 18.0 %copy-start.3 = (f32[2048,128]{1,0:T(8,128)S(1)}, f32[2048,128]{1,0:T(8,128)}, u32[]{:S(2)}) copy-start(f32[2048,128]{1,0:T(8,128)} %get-tuple-element.82.refs_2_) | copy-start | bytes 3145732
  79.6 18.0 %copy-start.4 = (bf16[128,4096]{1,0:T(8,128)(2,1)S(1)}, bf16[128,4096]{1,0:T(8,128)(2,1)}, u32[]{:S(2)}) copy-start(bf16[128,4096]{1,0:T(8,128)(2,1)} %get-tuple-element.80.refs_0_) | copy-start | bytes 3145732
  79.6 18.0 %copy-start.6 = (bf16[128,2048]{1,0:T(8,128)(2,1)S(1)}, bf16[128,2048]{1,0:T(8,128)(2,1)}, u32[]{:S(2)}) copy-start(bf16[128,2048]{1,0:T(8,128)(2,1)} %get-tuple-element.81.refs_1_) | copy-start | bytes 1572868
  113.6 4.0 %collective-permute-start.4 = (bf16[2048,128]{1,0:T(8,128)(2,1)S(1)}, bf16[2048,128]{1,0:T(8,128)(2,1)S(1)}, u32[]{:S(2)}, u32[]{:S(2)}) collective-permute-start(bf16[2048,128]{1,0:T(8,128)(2,1)S(1)} %get-tuple-element.93), channel_id=1, source_target_pairs={{0,1},{1,0},{2,3},{3,2},{4,5},{5,4},{6,7},{7,6},{8,9},{9,8},{10,11... | collective-permute-start | bytes 1572872 | tf_op jit(solution)/shard_map/ppermute | solution.py:673
  117.5 13.1 %copy-start.1 = (f32[256,320]{1,0:T(8,128)S(1)}, f32[256,320]{1,0:T(8,128)}, u32[]{:S(2)}) copy-start(f32[256,320]{1,0:T(8,128)} %get-tuple-element.84.refs_3_) | copy-start | bytes 983044
  117.6 13.1 %copy-start.2 = (bf16[9,256,256]{2,1,0:T(8,128)(2,1)S(1)}, bf16[9,256,256]{2,1,0:T(8,128)(2,1)}, u32[]{:S(2)}) copy-start(bf16[9,256,256]{2,1,0:T(8,128)(2,1)} %get-tuple-element.100.refs_7_) | copy-start | bytes 3538948
  117.6 13.1 %copy-start.5 = (bf16[320,320]{1,0:T(8,128)(2,1)S(1)}, bf16[320,320]{1,0:T(8,128)(2,1)}, u32[]{:S(2)}) copy-start(bf16[320,320]{1,0:T(8,128)(2,1)} %refs_8_.5) | copy-start | bytes 614404
  117.6 13.1 %copy-start.7 = (f32[256,320]{1,0:T(8,128)S(1)}, f32[256,320]{1,0:T(8,128)}, u32[]{:S(2)}) copy-start(f32[256,320]{1,0:T(8,128)} %get-tuple-element.98.refs_5_) | copy-start | bytes 983044
  117.6 13.1 %copy-start.8 = (f32[256,320]{1,0:T(8,128)S(1)}, f32[256,320]{1,0:T(8,128)}, u32[]{:S(2)}) copy-start(f32[256,320]{1,0:T(8,128)} %get-tuple-element.97.refs_4_) | copy-start | bytes 983044
  117.6 13.1 %copy-start.9 = (bf16[256,320]{1,0:T(8,128)(2,1)S(1)}, bf16[256,320]{1,0:T(8,128)(2,1)}, u32[]{:S(2)}) copy-start(bf16[256,320]{1,0:T(8,128)(2,1)} %get-tuple-element.99.refs_6_) | copy-start | bytes 491524
  117.6 13.1 %copy-start.10 = (bf16[256,320]{1,0:T(8,128)(2,1)S(1)}, bf16[256,320]{1,0:T(8,128)(2,1)}, u32[]{:S(2)}) copy-start(bf16[256,320]{1,0:T(8,128)(2,1)} %get-tuple-element.101.refs_9_) | copy-start | bytes 491524
  133.5 2.7 %collective-permute-start.5 = (bf16[3072,128]{1,0:T(8,128)(2,1)S(1)}, bf16[3072,128]{1,0:T(8,128)(2,1)S(1)}, u32[]{:S(2)}, u32[]{:S(2)}) collective-permute-start(bf16[3072,128]{1,0:T(8,128)(2,1)S(1)} %slice_bitcast_fusion), channel_id=1, source_target_pairs={{0,1},{1,0},{2,3},{3,2},{4,5},{5,4},{6,7},{7,6},{8,9},{9,8},{10,11... | collective-permute-start | bytes 2359304 | tf_op jit(solution)/shard_map/ppermute | solution.py:673
  136.5 19.9 %copy-start.13 = (bf16[8,6,32,128]{3,2,1,0:T(8,128)(2,1)S(1)}, bf16[8,6,32,128]{3,2,1,0:T(8,128)(2,1)}, u32[]{:S(2)}) copy-start(bf16[8,6,32,128]{3,2,1,0:T(8,128)(2,1)} %get-tuple-element.103) | copy-start | bytes 1179652
  180.5 6.5 %collective-permute-start.6 = (bf16[3072,128]{1,0:T(8,128)(2,1)S(1)}, bf16[3072,128]{1,0:T(8,128)(2,1)S(1)}, u32[]{:S(2)}, u32[]{:S(2)}) collective-permute-start(bf16[3072,128]{1,0:T(8,128)(2,1)S(1)} %bitcast.46), channel_id=1, source_target_pairs={{0,1},{1,0},{2,3},{3,2},{4,5},{5,4},{6,7},{7,6},{8,9},{9,8},{10,11... | collective-permute-start | bytes 2359304 | tf_op jit(solution)/shard_map/ppermute | solution.py:673

commit v6 on v5

--- a/solution.py
+++ b/solution.py
@@ -251,6 +251,7 @@
                 start_here = patch.astype(f32)
             inner += dot(patch, w_conv[3 * i + j])
             cond_out[3 * i + j] = moved[:, i : i + ROWS].reshape(CELLS, WIDE).astype(bf16)
+    cond_out.start()
     inner += b_conv[...]
     gate = jax.nn.sigmoid(inner)
     smooth = (inner * gate).astype(bf16)
@@ -594,6 +595,7 @@
     back = jnp.concatenate([result[...], blank, branch, blank], axis=1)
     for t in range(6):
         back_out[:, t] = back[:, t * LANES : (t + 1) * LANES].reshape(STRIPS, PART, LANES)
+    back_out.start()
     inner = (dot_nt(branch, w_out[...]) * slope[...]).astype(bf16)
     inner_turned = jnp.transpose(inner)
     branch_turned = jnp.transpose(branch)
@@ -648,6 +650,11 @@
         one = jnp.where(lane < 67, pltpu.roll(ones, LANES - 3 * n, 1) if n else ones, 0.0)
         return jnp.concatenate([first, jnp.where(low, middle, one)], axis=1).astype(bf16)
 
+    last = jnp.concatenate([tile(1, 6), tile(1, 7), ones], axis=1)
+    last = jnp.transpose(last)
+    wout_out[...] = last[:C]
+    bconv_out[...] = last[C + 12]
+    bout_out[...] = last[C + 27]
     grad_in = jnp.zeros((C, WIDE), f32)
     copies = []
     for n in range(9):
@@ -657,11 +664,6 @@
         copy.start()
         copies.append(copy)
         grad_in += dot(w_conv[n], moment)
-    last = jnp.concatenate([tile(1, 6), tile(1, 7), ones], axis=1)
-    last = jnp.transpose(last)
-    wout_out[...] = last[:C]
-    bconv_out[...] = last[C + 12]
-    bout_out[...] = last[C + 27]
     grad_in = jnp.transpose(grad_in + moment_of(9).astype(f32))
     win_out[...] = grad_in[:CIN]
     bin_out[...] = grad_in[CIN]

time: 192 us -> 192 us (level)
  no operation moved by 1% of the time
where the time goes in v6:
time: 192 us; the launch traced here: 191 us
  blocking collectives  89.1 us (46%)
  Pallas kernels  61.1 us (32%)
  starting transfers between devices  24.5 us (13%)
  waiting for transfers between devices  11 us (6%)
  other arithmetic  2.67 us (1%)
    all_to_all x7, blocking collectives, across(): return lax.all_to_all(blocks, axes, 0, 0, tiled=True)  89.1 us
    pallas_call x11, Pallas kernels, call(): pl.pallas_call(body, out_shape=tuple((made_as(i, made) for i, made in enu...  57.5 us
    all_to_all x1, starting transfers between devices, across(): return lax.all_to_all(blocks, axes, 0, 0, tiled=True)  8.49 us
    ppermute x4, starting transfers between devices, swap(): return lax.ppermute(array, 'c', [(0, 1), (1, 0)])  7.58 us
    ppermute x1, starting transfers between devices, per_device(): left = lax.ppermute(edge(COLS - 1), ('x', 'c'), right_way)  6.02 us
    all_to_all x1, waiting for transfers between devices, across(): return lax.all_to_all(blocks, axes, 0, 0, tiled=True)  5.35 us
  transfers between devices with their start and end apart: 8, of which 4 were waited for; matrix products, arithmetic and copies ran while one was open for 1% of the time, Pallas kernels for 7%

profile of v6, /device:TPU:1, one launch (start us, length us, event | category | flops | bytes accessed | tf_op | source)
XLA Modules:
  0.0 191.1 jit_solution(2512684077654640209)
XLA Ops:
  0.6 2.0 %fusion.6 = bf16[8,32,1024]{2,1,0:T(8,128)(2,1)} fusion(bf16[8,32,320]{2,1,0:T(8,128)(2,1)} %bitcast.58, bf16[8,32,320]{2,1,0:T(8,128)(2,1)} %bitcast.59, bf16[8,32,192]{2,1,0:T(8,128)(2,1)} %bitcast.60), kind=kLoop, calls=%fused_computation.13 | loop fusion | flops 3670016 | bytes 950272 | tf_op jit(solution)/shard_map/concatenate | solution.py:695
  2.7 8.5 %all-to-all-start = ((bf16[8,32,1024]{2,1,0:T(8,128)(2,1)}), bf16[8,32,1024]{2,1,0:T(8,128)(2,1)S(1)}, u32[]{:S(2)}, u32[]{:S(2)}) async-start(bf16[8,32,1024]{2,1,0:T(8,128)(2,1)} %fusion.6), calls=%async_computation | async-start | bytes 1048576 | tf_op jit(solution)/shard_map/all_to_all | solution.py:679
  13.9 2.6 %text.1 = (bf16[128,512]{1,0:T(8,128)(2,1)}, bf16[128,512]{1,0:T(8,128)(2,1)}) custom-call(bf16[128,768]{1,0:T(8,128)(2,1)} %pad.18.refs_0_, bf16[320,768]{1,0:T(8,128)(2,1)} %bitcast.61, bf16[320,768]{1,0:T(8,128)(2,1)} %bitcast.62), custom_call_target="tpu_custom_call" | custom-call | flops 4000000000 | bytes 2000000 | tf_op jit(solution)/shard_map/text/pallas_call | solution.py:134
  16.5 5.3 %all-to-all-done.refs_2_.refs_4_ = bf16[8,32,1024]{2,1,0:T(8,128)(2,1)S(1)} async-done(((bf16[8,32,1024]{2,1,0:T(8,128)(2,1)}), bf16[8,32,1024]{2,1,0:T(8,128)(2,1)S(1)}, u32[]{:S(2)}, u32[]{:S(2)}) %all-to-all-start) | async-done | bytes 524320 | tf_op jit(solution)/shard_map/all_to_all | solution.py:679
  22.5 2.7 %collective-permute-done.refs_3_ = bf16[8,2,8,256]{3,2,1,0:T(8,128)(2,1)S(1)} collective-permute-done((bf16[8,2,8,256]{3,2,1,0:T(8,128)(2,1)S(1)}, bf16[8,2,8,256]{3,2,1,0:T(8,128)(2,1)S(1)}, u32[]{:S(2)}, u32[]{:S(2)}) %collective-permute-start) | collective-permute-done | bytes 65568 | tf_op jit(solution)/shard_map/ppermute | solution.py:716
  25.3 6.0 %collective-permute-start.1 = (bf16[48,256]{1,0:T(8,128)(2,1)S(1)}, bf16[48,256]{1,0:T(8,128)(2,1)S(1)}, u32[]{:S(2)}, u32[]{:S(2)}) collective-permute-start(bf16[48,256]{1,0:T(8,128)(2,1)S(1)} %reshape.80), channel_id=1, source_target_pairs={{0,1},{1,2},{2,3},{3,4},{4,5},{5,6},{6,7},{8,9},{9,10},{10,11},{11... | collective-permute-start | bytes 73736 | tf_op jit(solution)/shard_map/ppermute | solution.py:723
  31.3 1.9 %collective-permute-start.2 = (bf16[48,256]{1,0:T(8,128)(2,1)S(1)}, bf16[48,256]{1,0:T(8,128)(2,1)S(1)}, u32[]{:S(2)}, u32[]{:S(2)}) collective-permute-start(bf16[48,256]{1,0:T(8,128)(2,1)S(1)} %reshape.81), channel_id=1, source_target_pairs={{1,0},{2,1},{3,2},{4,3},{5,4},{6,5},{7,6},{9,8},{10,9},{11,10},{12... | collective-permute-start | bytes 73736 | tf_op jit(solution)/shard_map/ppermute | solution.py:724
  33.4 2.0 %load_adapter.1 = (bf16[192,320]{1,0:T(8,128)(2,1)S(1)}, f32[320]{0:T(512)S(1)}, bf16[9,320,320]{2,1,0:T(8,128)(2,1)S(1)}, f32[320]{0:T(512)S(1)}, bf16[320,320]...) custom-call(bf16[192,320]{1,0:T(8,128)(2,1)} %refs_0_.4, ...), custom_call_target="tpu_custom_call" | custom-call | tf_op jit(solution)/shard_map/load_adapter/pallas_call | solution.py:170
  36.5 4.5 %adapter.1 = (bf16[8,256,128]{2,1,0:T(8,128)(2,1)S(1)}, f32[256,320]{1,0:T(8,128)}, bf16[256,320]{1,0:T(8,128)(2,1)}, f32[256,320]{1,0:T(8,128)}, bf16[9,256,256]{2,1,0:T(8,128)(2,1)}) custom-call(s32[4]{0:T(128)S(1)} %pad_add_fusion.refs_0_, s32[8]{0:T(128)S(1)} %copy-done.11, bf16[8,32,1024]{2,1,0:T(8,128)(2,1)S(1)} %all-to-all-done.refs_2_.refs_4_, ...), custom_call_target="tpu_custom_call" | custom-call | tf_op jit(solution)/shard_map/adapter/pallas_call | solution.py:134
  41.0 13.9 %all_to_all.40 = bf16[8,256,128]{2,1,0:T(8,128)(2,1)S(1)} all-to-all(bf16[8,256,128]{2,1,0:T(8,128)(2,1)S(1)} %get-tuple-element.76), channel_id=1, replica_groups=mesh['a'=8,'b'=2,'x'=4,'c'=2] {'b','x'}, dimensions={0} | all-to-all | bytes 1048576 | tf_op jit(solution)/shard_map/all_to_all | solution.py:679
  55.7 2.1 %form.1 = (bf16[320,512]{1,0:T(8,128)(2,1)}, bf16[512,320]{1,0:T(8,128)(2,1)}, bf16[1024,768]{1,0:T(8,128)(2,1)S(1)}) custom-call(bf16[320,320]{1,0:T(8,128)(2,1)} %refs_0_.5, bf16[320,320]{1,0:T(8,128)(2,1)} %refs_1_.8, bf16[320,320]{1,0:T(8,128)(2,1)} %refs_2_.1), custom_call_target="tpu_custom_call" | custom-call | tf_op jit(solution)/shard_map/form/pallas_call | solution.py:134
  57.8 11.8 %attend.1 = (bf16[64,16,128]{2,1,0:T(8,128)(2,1)S(1)}, f32[2048,128]{1,0:T(8,128)}, bf16[2048,4096]{1,0:T(8,128)(2,1)}, bf16[128,4096]{1,0:T(8,128)(2,1)}, bf16[128,2048]{1,0:T(8,128)(2,1)}) custom-call(bf16[2048,128]{1,0:T(8,128)(2,1)S(1)} %bitcast.44, bf16[2048,128]{1,0:T(8,128)(2,1)S(1)} %collective-permute-done.3.refs_1_), custom_call_target="tpu_custom_call" | custom-call | tf_op jit(solution)/shard_map/attend/pallas_call | solution.py:134
  69.6 9.9 %all_to_all.41.refs_2_ = bf16[8,128,128]{2,1,0:T(8,128)(2,1)S(1)} all-to-all(bf16[8,128,128]{2,1,0:T(8,128)(2,1)S(1)} %bitcast.48), channel_id=1, replica_groups=mesh['a'=8,'b'=2,'x'=4,'c'=2] {'b','x'}, dimensions={0} | all-to-all | bytes 524288 | tf_op jit(solution)/shard_map/all_to_all | solution.py:679
  79.5 9.3 %middle.1 = (bf16[256,320]{1,0:T(8,128)(2,1)}, f32[256,320]{1,0:T(8,128)}, bf16[8,128,128]{2,1,0:T(8,128)(2,1)S(1)}) custom-call(s32[4]{0:T(128)S(1)} %pad_add_fusion.refs_0_, s32[8]{0:T(128)S(1)} %copy-done.12, bf16[8,128,128]{2,1,0:T(8,128)(2,1)S(1)} %all_to_all.41.refs_2_, f32[256,320]{1,0:T(8,128)} %get-tuple-element.84.refs_3_, ...), custom_call_target="tpu_custom_call" | custom-call | tf_op jit(solution)/shard_map/middle/pallas_call | solution.py:134
  88.9 8.7 %all_to_all.42 = bf16[8,128,128]{2,1,0:T(8,128)(2,1)S(1)} all-to-all(bf16[8,128,128]{2,1,0:T(8,128)(2,1)S(1)} %get-tuple-element.90), channel_id=1, replica_groups=mesh['a'=8,'b'=2,'x'=4,'c'=2] {'b','x'}, dimensions={0} | all-to-all | bytes 524288 | tf_op jit(solution)/shard_map/all_to_all | solution.py:679
  97.6 16.0 %attend_back.1 = (f32[2048,128]{1,0:T(8,128)S(1)}, bf16[2048,128]{1,0:T(8,128)(2,1)S(1)}) custom-call(bf16[128,4096]{1,0:T(8,128)(2,1)S(1)} %copy-done.4, bf16[128,2048]{1,0:T(8,128)(2,1)S(1)} %copy-done.6, f32[2048,128]{1,0:T(8,128)S(1)} %copy-done.3, bf16[64,16,128]{2,1,0:T(8,128)(2,1)S(1)} %bitcast.45, bf16[2048,4096]{1,0:T(8,128)(2,1)} %get-tuple-element.91.refs_4_), custom_call_target="tpu_custom_call" | custom-call | tf_op jit(solution)/shard_map/attend_back/pallas_call | solution.py:134
  113.5 2.0 %collective-permute-start.4 = (bf16[2048,128]{1,0:T(8,128)(2,1)S(1)}, bf16[2048,128]{1,0:T(8,128)(2,1)S(1)}, u32[]{:S(2)}, u32[]{:S(2)}) collective-permute-start(bf16[2048,128]{1,0:T(8,128)(2,1)S(1)} %get-tuple-element.93), channel_id=1, source_target_pairs={{0,1},{1,0},{2,3},{3,2},{4,5},{5,4},{6,7},{7,6},{8,9},{9,8},{10,11... | collective-permute-start | bytes 1572872 | tf_op jit(solution)/shard_map/ppermute | solution.py:675
  117.7 12.9 %all_to_all.43.refs_1_ = bf16[8,256,128]{2,1,0:T(8,128)(2,1)S(1)} all-to-all(bf16[8,256,128]{2,1,0:T(8,128)(2,1)S(1)} %bitcast.53), channel_id=1, replica_groups=mesh['a'=8,'b'=2,'x'=4,'c'=2] {'b','x'}, dimensions={0} | all-to-all | bytes 1048576 | tf_op jit(solution)/shard_map/all_to_all | solution.py:679
  130.6 2.8 %finish.1 = (bf16[8,6,32,128]{3,2,1,0:T(8,128)(2,1)}, bf16[2,3072,128]{2,1,0:T(8,128)(2,1)S(1)}) custom-call(s32[4]{0:T(128)S(1)} %pad_add_fusion.refs_0_, bf16[8,256,128]{2,1,0:T(8,128)(2,1)S(1)} %all_to_all.43.refs_1_, bf16[320,1024]{1,0:T(8,128)(2,1)S(1)} %join.1.refs_2_, f32[256,320]{1,0:T(8,128)S(1)} %copy-done.1, f32[256,320]{1,0:T(8,128)S(1)} %copy-done.8, ...), custom_call_target="tpu_custom_call" | custom-call | tf_op jit(solution)/shard_map/finish/pallas_call | solution.py:134
  136.4 19.7 %all_to_all.44 = bf16[64,48,128]{2,1,0:T(8,128)(2,1)S(1)} all-to-all(bf16[64,48,128]{2,1,0:T(8,128)(2,1)S(1)} %bitcast.51), channel_id=1, replica_groups=mesh['a'=8,'b'=2,'x'=4,'c'=2] {'a','b','x'}, dimensions={0} | all-to-all | bytes 1572864 | tf_op jit(solution)/shard_map/all_to_all | solution.py:679
  156.4 11.5 %all_to_all.45.refs_0_ = bf16[8,240,128]{2,1,0:T(8,128)(2,1)S(1)} all-to-all(bf16[8,240,128]{2,1,0:T(8,128)(2,1)S(1)} %pad_maximum_fusion), channel_id=1, replica_groups=mesh['a'=8,'b'=2,'x'=4,'c'=2] {'a'}, dimensions={0} | all-to-all | bytes 983040 | tf_op jit(solution)/shard_map/all_to_all | solution.py:679
  168.0 12.4 %all_to_all.46 = bf16[8,384,128]{2,1,0:T(8,128)(2,1)S(1)} all-to-all(bf16[8,384,128]{2,1,0:T(8,128)(2,1)S(1)} %broadcast_in_dim.15), channel_id=1, replica_groups=mesh['a'=8,'b'=2,'x'=4,'c'=2] {'b','x'}, dimensions={0} | all-to-all | bytes 1572864 | tf_op jit(solution)/shard_map/all_to_all | solution.py:679
  180.4 4.0 %collective-permute-start.6 = (bf16[3072,128]{1,0:T(8,128)(2,1)S(1)}, bf16[3072,128]{1,0:T(8,128)(2,1)S(1)}, u32[]{:S(2)}, u32[]{:S(2)}) collective-permute-start(bf16[3072,128]{1,0:T(8,128)(2,1)S(1)} %bitcast.46), channel_id=1, source_target_pairs={{0,1},{1,0},{2,3},{3,2},{4,5},{5,4},{6,7},{7,6},{8,9},{9,8},{10,11... | collective-permute-start | bytes 2359304 | tf_op jit(solution)/shard_map/ppermute | solution.py:675
  187.0 3.9 %weights.1 = (f32[192,320]{1,0:T(8,128)}, f32[320]{0:T(512)}, f32[9,320,320]{2,1,0:T(8,128)}, f32[320]{0:T(512)}, f32[320,320]{1,0:T(8,128)}, /*index=5*/f32[320]{0:T(512)}) custom-call(s32[4]{0:T(128)S(1)} %pad_add_fusion.refs_0_, bf16[3072,128]{1,0:T(8,128)(2,1)S(1)} %bitcast.47, bf16[3072,128]{1,0:T(8,128)(2,1)S(1)} %collective-permute-done.6.refs_2_, ...), custom_call_target="tpu_custom_call" | custom-call | flops 6000000000 | bytes 20000000 | tf_op jit(solution)/shard_map/weights/pallas_call | solution.py:134
  (67 shorter events, 13.1 us)
Async XLA Ops:
  0.6 10.6 %copy-start = (bf16[8,77,768]{2,0,1:T(8,128)(2,1)S(1)}, bf16[8,77,768]{2,0,1:T(8,128)(2,1)}, u32[]{:S(2)}) copy-start(bf16[8,77,768]{2,0,1:T(8,128)(2,1)} %param.28) | copy-start | bytes 2838532
  2.7 19.2 %all-to-all-start = ((bf16[8,32,1024]{2,1,0:T(8,128)(2,1)}), bf16[8,32,1024]{2,1,0:T(8,128)(2,1)S(1)}, u32[]{:S(2)}, u32[]{:S(2)}) async-start(bf16[8,32,1024]{2,1,0:T(8,128)(2,1)} %fusion.6), calls=%async_computation | async-start | bytes 1048576 | tf_op jit(solution)/shard_map/all_to_all | solution.py:679
  22.0 3.2 %collective-permute-start = (bf16[8,2,8,256]{3,2,1,0:T(8,128)(2,1)S(1)}, bf16[8,2,8,256]{3,2,1,0:T(8,128)(2,1)S(1)}, u32[]{:S(2)}, u32[]{:S(2)}) collective-permute-start(bf16[8,2,8,256]{3,2,1,0:T(8,128)(2,1)S(1)} %pad_maximum_fusion.1), channel_id=1, source_target_pairs={{0,8},{8,0},{1,9},{9,1},{2,10},{10,2},{3,11},{11,3},{4,12},{12,4},... | collective-permute-start | bytes 196616 | tf_op jit(solution)/shard_map/ppermute | solution.py:716
  25.3 10.1 %collective-permute-start.1 = (bf16[48,256]{1,0:T(8,128)(2,1)S(1)}, bf16[48,256]{1,0:T(8,128)(2,1)S(1)}, u32[]{:S(2)}, u32[]{:S(2)}) collective-permute-start(bf16[48,256]{1,0:T(8,128)(2,1)S(1)} %reshape.80), channel_id=1, source_target_pairs={{0,1},{1,2},{2,3},{3,4},{4,5},{5,6},{6,7},{8,9},{9,10},{10,11},{11... | collective-permute-start | bytes 73736 | tf_op jit(solution)/shard_map/ppermute | solution.py:723
  31.3 5.1 %collective-permute-start.2 = (bf16[48,256]{1,0:T(8,128)(2,1)S(1)}, bf16[48,256]{1,0:T(8,128)(2,1)S(1)}, u32[]{:S(2)}, u32[]{:S(2)}) collective-permute-start(bf16[48,256]{1,0:T(8,128)(2,1)S(1)} %reshape.81), channel_id=1, source_target_pairs={{1,0},{2,1},{3,2},{4,3},{5,4},{6,5},{7,6},{9,8},{10,9},{11,10},{12... | collective-permute-start | bytes 73736 | tf_op jit(solution)/shard_map/ppermute | solution.py:724
  33.4 3.1 %copy-start.11 = (s32[8]{0:T(128)S(1)}, s32[8]{0:T(128)}, u32[]{:S(2)}) copy-start(s32[8]{0:T(128)} %refs_1_.7) | copy-start | bytes 100
  41.0 38.5 %copy-start.12 = (s32[8]{0:T(128)S(1)}, s32[8]{0:T(128)}, u32[]{:S(2)}) copy-start(s32[8]{0:T(128)} %refs_1_.9) | copy-start | bytes 100
  55.0 2.8 %collective-permute-start.3 = (bf16[2048,128]{1,0:T(8,128)(2,1)S(1)}, bf16[2048,128]{1,0:T(8,128)(2,1)S(1)}, u32[]{:S(2)}, u32[]{:S(2)}) collective-permute-start(bf16[2048,128]{1,0:T(8,128)(2,1)S(1)} %bitcast.43), channel_id=1, source_target_pairs={{0,1},{1,0},{2,3},{3,2},{4,5},{5,4},{6,7},{7,6},{8,9},{9,8},{10,11... | collective-permute-start | bytes 1572872 | tf_op jit(solution)/shard_map/ppermute | solution.py:675
  79.5 18.0 %copy-start.3 = (f32[2048,128]{1,0:T(8,128)S(1)}, f32[2048,128]{1,0:T(8,128)}, u32[]{:S(2)}) copy-start(f32[2048,128]{1,0:T(8,128)} %get-tuple-element.82.refs_2_) | copy-start | bytes 3145732
  79.5 18.0 %copy-start.4 = (bf16[128,4096]{1,0:T(8,128)(2,1)S(1)}, bf16[128,4096]{1,0:T(8,128)(2,1)}, u32[]{:S(2)}) copy-start(bf16[128,4096]{1,0:T(8,128)(2,1)} %get-tuple-element.80.refs_0_) | copy-start | bytes 3145732
  79.5 18.0 %copy-start.6 = (bf16[128,2048]{1,0:T(8,128)(2,1)S(1)}, bf16[128,2048]{1,0:T(8,128)(2,1)}, u32[]{:S(2)}) copy-start(bf16[128,2048]{1,0:T(8,128)(2,1)} %get-tuple-element.81.refs_1_) | copy-start | bytes 1572868
  113.5 4.0 %collective-permute-start.4 = (bf16[2048,128]{1,0:T(8,128)(2,1)S(1)}, bf16[2048,128]{1,0:T(8,128)(2,1)S(1)}, u32[]{:S(2)}, u32[]{:S(2)}) collective-permute-start(bf16[2048,128]{1,0:T(8,128)(2,1)S(1)} %get-tuple-element.93), channel_id=1, source_target_pairs={{0,1},{1,0},{2,3},{3,2},{4,5},{5,4},{6,7},{7,6},{8,9},{9,8},{10,11... | collective-permute-start | bytes 1572872 | tf_op jit(solution)/shard_map/ppermute | solution.py:675
  117.5 13.1 %copy-start.1 = (f32[256,320]{1,0:T(8,128)S(1)}, f32[256,320]{1,0:T(8,128)}, u32[]{:S(2)}) copy-start(f32[256,320]{1,0:T(8,128)} %get-tuple-element.84.refs_3_) | copy-start | bytes 983044
  117.5 13.1 %copy-start.2 = (bf16[9,256,256]{2,1,0:T(8,128)(2,1)S(1)}, bf16[9,256,256]{2,1,0:T(8,128)(2,1)}, u32[]{:S(2)}) copy-start(bf16[9,256,256]{2,1,0:T(8,128)(2,1)} %get-tuple-element.100.refs_7_) | copy-start | bytes 3538948
  117.5 13.1 %copy-start.5 = (bf16[320,320]{1,0:T(8,128)(2,1)S(1)}, bf16[320,320]{1,0:T(8,128)(2,1)}, u32[]{:S(2)}) copy-start(bf16[320,320]{1,0:T(8,128)(2,1)} %refs_8_.5) | copy-start | bytes 614404
  117.5 13.1 %copy-start.7 = (f32[256,320]{1,0:T(8,128)S(1)}, f32[256,320]{1,0:T(8,128)}, u32[]{:S(2)}) copy-start(f32[256,320]{1,0:T(8,128)} %get-tuple-element.98.refs_5_) | copy-start | bytes 983044
  117.5 13.1 %copy-start.8 = (f32[256,320]{1,0:T(8,128)S(1)}, f32[256,320]{1,0:T(8,128)}, u32[]{:S(2)}) copy-start(f32[256,320]{1,0:T(8,128)} %get-tuple-element.97.refs_4_) | copy-start | bytes 983044
  117.5 13.1 %copy-start.9 = (bf16[256,320]{1,0:T(8,128)(2,1)S(1)}, bf16[256,320]{1,0:T(8,128)(2,1)}, u32[]{:S(2)}) copy-start(bf16[256,320]{1,0:T(8,128)(2,1)} %get-tuple-element.99.refs_6_) | copy-start | bytes 491524
  117.5 13.1 %copy-start.10 = (bf16[256,320]{1,0:T(8,128)(2,1)S(1)}, bf16[256,320]{1,0:T(8,128)(2,1)}, u32[]{:S(2)}) copy-start(bf16[256,320]{1,0:T(8,128)(2,1)} %get-tuple-element.101.refs_9_) | copy-start | bytes 491524
  133.4 2.7 %collective-permute-start.5 = (bf16[3072,128]{1,0:T(8,128)(2,1)S(1)}, bf16[3072,128]{1,0:T(8,128)(2,1)S(1)}, u32[]{:S(2)}, u32[]{:S(2)}) collective-permute-start(bf16[3072,128]{1,0:T(8,128)(2,1)S(1)} %slice_bitcast_fusion), channel_id=1, source_target_pairs={{0,1},{1,0},{2,3},{3,2},{4,5},{5,4},{6,7},{7,6},{8,9},{9,8},{10,11... | collective-permute-start | bytes 2359304 | tf_op jit(solution)/shard_map/ppermute | solution.py:675
  136.4 19.9 %copy-start.13 = (bf16[8,6,32,128]{3,2,1,0:T(8,128)(2,1)S(1)}, bf16[8,6,32,128]{3,2,1,0:T(8,128)(2,1)}, u32[]{:S(2)}) copy-start(bf16[8,6,32,128]{3,2,1,0:T(8,128)(2,1)} %get-tuple-element.103) | copy-start | bytes 1179652
  180.4 6.5 %collective-permute-start.6 = (bf16[3072,128]{1,0:T(8,128)(2,1)S(1)}, bf16[3072,128]{1,0:T(8,128)(2,1)S(1)}, u32[]{:S(2)}, u32[]{:S(2)}) collective-permute-start(bf16[3072,128]{1,0:T(8,128)(2,1)S(1)} %bitcast.46), channel_id=1, source_target_pairs={{0,1},{1,0},{2,3},{3,2},{4,5},{5,4},{6,7},{7,6},{8,9},{9,8},{10,11... | collective-permute-start | bytes 2359304 | tf_op jit(solution)/shard_map/ppermute | solution.py:675
